TPU v7x, 512 devices: a whole 4x8x8 slice. The times are simulated.
512 devices in a mesh: blk: 16 (over z_lo, y), grp: 32 (over x, z_hi, core).
Axes of the slice: x: 4, y: 8, z: 8 (z_hi: 4, z_lo: 2; z = z_hi * 2 + z_lo), core: 2. Of those that a mesh axis runs over, the one named last changes fastest.
Arguments:
- image_cand: bfloat16 [131072, 1152], P(('blk', 'grp')), may hold values from -6 to 6
- text_cand: bfloat16 [131072, 1152], P(('blk', 'grp')), may hold values from -0.1796875 to 0.1796875
- selection: int32 [65536], P(('blk', 'grp')), may hold values from 0 to 255, as said below
- head_weight: bfloat16 [1152, 1152], P('grp'), may hold values from -0.1875 to 0.1875
- logit_temp: float32 [1], replicated, may hold values from 4 to 12
- logit_offset: float32 [1], replicated, may hold values from -5 to -2
- loss_scale: float32 [1], replicated, may hold values from 65536 to 262144
Outputs:
- head_grad: float32 [1152, 1152], P('grp')
- text_grad: float32 [131072, 1152], P(('blk', 'grp'))
Inputs may be any that keep to these rules, and one draw needn't show every extreme that they name: `selection`: within one device's 128 entries the indices are distinct.
All inputs are finite; a program needn't handle non-finite values.
Results may differ from a plain program's by a relative error of at most 0.022.
Values may be sent and summed in bfloat16 or wider, within the bound.
No kernel may reach another device: no remote copies, remote signals or barrier semaphores. Data moves between devices by JAX's collectives and lax.ppermute only.
A program may use at most 64 MiB of HBM per device.

v0:
```python
import jax
import jax.numpy as jnp
from jax import lax
from jax.sharding import PartitionSpec as P

EPS = 1e-06


def shifted(value, axis, steps):
    count = lax.axis_size(axis)
    pairs = [(source, (source + steps) % count) for source in range(count)]
    return lax.ppermute(value, axis, pairs)


def visit_one(own, work, accum, move, blocks):

    def turn(index, carry):
        held, total = carry
        held = move(held)
        return (held, total + work(held))

    return lax.fori_loop(0, blocks - 1, turn, (own, accum))[1]


def shards(image_cand, text_cand, selection, head_weight, logit_temp, logit_offset, loss_scale):
    pair_count = selection.shape[0]
    width = head_weight.shape[1]
    groups = lax.axis_size("grp")
    blocks = lax.axis_size("blk")
    picked = jnp.take(image_cand, selection, axis=0)
    texts = jnp.take(text_cand, selection, axis=0).astype(jnp.float32)
    columns = picked
    projected = jnp.dot(
        columns,
        lax.all_gather(head_weight, "grp", axis=0, tiled=True),
        preferred_element_type=jnp.float32,
    )
    img_norm = jnp.sqrt(jnp.sum(projected * projected, axis=1) + EPS)
    image_unit = (projected / img_norm[:, None]).astype(jnp.bfloat16)
    txt_norm = jnp.sqrt(jnp.sum(texts * texts, axis=1) + EPS)
    text_unit = (texts / txt_norm[:, None]).astype(jnp.bfloat16)
    temper = logit_temp[0]
    offset = logit_offset[0]
    factor = loss_scale[0] / (pair_count * blocks * groups)
    local_ids = jnp.arange(pair_count, dtype=jnp.int32)
    own_sign = jnp.where(local_ids[:, None] == local_ids[None, :], 1.0, -1.0).astype(jnp.float32)
    minus_sign = -jnp.ones((pair_count, pair_count), jnp.float32)

    def pair_tile(image_blk, text_blk, label_sign):
        inner = lax.dot_general(
            image_blk, text_blk, (((1,), (1,)), ((), ())), preferred_element_type=jnp.float32
        )
        logits = temper * inner + offset
        return (-factor * label_sign * jax.nn.sigmoid(-label_sign * logits)).astype(jnp.bfloat16)

    def image_work(text_blk):
        grad_tile = pair_tile(image_unit, text_blk, minus_sign)
        return temper * jnp.dot(grad_tile, text_blk, preferred_element_type=jnp.float32)

    def text_work(image_blk):
        grad_tile = pair_tile(image_blk, text_unit, minus_sign)
        return temper * lax.dot_general(
            grad_tile, image_blk, (((0,), (0,)), ((), ())), preferred_element_type=jnp.float32
        )

    own_tile = pair_tile(image_unit, text_unit, own_sign)
    image_start = temper * jnp.dot(own_tile, text_unit, preferred_element_type=jnp.float32)
    text_start = temper * lax.dot_general(
        own_tile, image_unit, (((0,), (0,)), ((), ())), preferred_element_type=jnp.float32
    )

    def text_next(held):
        return shifted(held, "blk", 1)

    def image_next(held):
        return shifted(held, "blk", 1)

    image_back = visit_one(text_unit, image_work, image_start, text_next, blocks)
    text_back = visit_one(image_unit, text_work, text_start, image_next, blocks)
    unit_float = image_unit.astype(jnp.float32)
    radial = jnp.sum(unit_float * image_back, axis=1, keepdims=True)
    proj_back = (image_back - unit_float * radial) / img_norm[:, None]
    picked_float = picked.astype(jnp.float32)
    columns = picked_float
    head_part = lax.psum_scatter(
        lax.dot_general(
            columns,
            proj_back,
            (((0,), (0,)), ((), ())),
            precision=lax.Precision.HIGHEST,
            preferred_element_type=jnp.float32,
        ).astype(jnp.bfloat16),
        "grp",
        scatter_dimension=0,
        tiled=True,
    ).astype(jnp.float32)
    head_grad = lax.psum(head_part, "blk")
    text_float = text_unit.astype(jnp.float32)
    text_radial = jnp.sum(text_float * text_back, axis=1, keepdims=True)
    text_rows = (text_back - text_float * text_radial) / txt_norm[:, None]
    text_grad = jnp.zeros((text_cand.shape[0], width), jnp.float32).at[selection].set(text_rows)
    return (head_grad, text_grad)


def solution(mesh):
    return jax.shard_map(
        shards,
        mesh=mesh,
        in_specs=(
            P(("blk", "grp"), None),
            P(("blk", "grp"), None),
            P(("blk", "grp")),
            P("grp", None),
            P(),
            P(),
            P(),
        ),
        out_specs=(P("grp", None), P(("blk", "grp"), None)),
        check_vma=False,
    )
```

profile of v0, /device:TPU:64, one launch (start us, length us, event | category | flops | bytes accessed | tf_op | source)
XLA Modules:
  0.0 633.8 jit_solution(16327539634278848707)
XLA Ops:
  13.3 62.8 %all-gather.3.cloned.1.call-done = bf16[32,36,1152]{2,1,0:T(8,128)(2,1)} async-done(((bf16[1,36,1152]{2,1,0:T(8,128)(2,1)}), bf16[32,36,1152]{2,1,0:T(8,128)(2,1)}) %all-gather.3.cloned.1.call-update) | async-done | bytes 2654224 | tf_op jit(solution)/shard_map/all_gather | solution.py:35
  76.1 3.6 reshape.50
  81.4 205.3 %while.28 = (s32[]{:T(128)}, bf16[128,1152]{1,0:T(8,128)(2,1)S(1)}, f32[128,1152]{1,0:T(8,128)S(1)}, f32[]{:T(128)}, f32[]{:T(128)}, /*index=5*/bf16[128,1152]{1,0:T(8,128)(2,1)S(1)}, f32[]{:T(128)}, s32[]{:T(128)}) while((s32[]{:T(128)}, bf16[128,1152]{1,0:T(8,128)(2,1)S(1)}, f32[128,1152]{1,0:T(8,128)S(1)}, f32[]{:T(128)}, f32[]{:T(128)}, ...), condition=%wide.region_3.5_spmd, body=%wide.region_2.4_spmd.sunk | while | flops 75907072 | bytes 3539081 | solution.py:22
  81.4 3.5 collective-permute-start
  84.9 10.2 %collective-permute-done = bf16[128,1152]{1,0:T(8,128)(2,1)S(1)} collective-permute-done((bf16[128,1152]{1,0:T(8,128)(2,1)S(1)}, bf16[128,1152]{1,0:T(8,128)(2,1)S(1)}, u32[]{:S(2)}, u32[]{:S(2)}) %collective-permute-start) | collective-permute-done | bytes 294944 | tf_op jit(solution)/shard_map/while/body/eval_jaxpr/ppermute | solution.py:12
  97.1 1.9 collective-permute-start
  99.0 10.8 %collective-permute-done = bf16[128,1152]{1,0:T(8,128)(2,1)S(1)} collective-permute-done((bf16[128,1152]{1,0:T(8,128)(2,1)S(1)}, bf16[128,1152]{1,0:T(8,128)(2,1)S(1)}, u32[]{:S(2)}, u32[]{:S(2)}) %collective-permute-start) | collective-permute-done | bytes 294944 | tf_op jit(solution)/shard_map/while/body/eval_jaxpr/ppermute | solution.py:12
  111.7 1.9 collective-permute-start
  113.6 9.9 %collective-permute-done = bf16[128,1152]{1,0:T(8,128)(2,1)S(1)} collective-permute-done((bf16[128,1152]{1,0:T(8,128)(2,1)S(1)}, bf16[128,1152]{1,0:T(8,128)(2,1)S(1)}, u32[]{:S(2)}, u32[]{:S(2)}) %collective-permute-start) | collective-permute-done | bytes 294944 | tf_op jit(solution)/shard_map/while/body/eval_jaxpr/ppermute | solution.py:12
  125.4 1.9 collective-permute-start
  127.3 9.0 %collective-permute-done = bf16[128,1152]{1,0:T(8,128)(2,1)S(1)} collective-permute-done((bf16[128,1152]{1,0:T(8,128)(2,1)S(1)}, bf16[128,1152]{1,0:T(8,128)(2,1)S(1)}, u32[]{:S(2)}, u32[]{:S(2)}) %collective-permute-start) | collective-permute-done | bytes 294944 | tf_op jit(solution)/shard_map/while/body/eval_jaxpr/ppermute | solution.py:12
  138.2 1.9 collective-permute-start
  140.1 8.8 %collective-permute-done = bf16[128,1152]{1,0:T(8,128)(2,1)S(1)} collective-permute-done((bf16[128,1152]{1,0:T(8,128)(2,1)S(1)}, bf16[128,1152]{1,0:T(8,128)(2,1)S(1)}, u32[]{:S(2)}, u32[]{:S(2)}) %collective-permute-start) | collective-permute-done | bytes 294944 | tf_op jit(solution)/shard_map/while/body/eval_jaxpr/ppermute | solution.py:12
  150.8 1.9 collective-permute-start
  152.7 8.8 %collective-permute-done = bf16[128,1152]{1,0:T(8,128)(2,1)S(1)} collective-permute-done((bf16[128,1152]{1,0:T(8,128)(2,1)S(1)}, bf16[128,1152]{1,0:T(8,128)(2,1)S(1)}, u32[]{:S(2)}, u32[]{:S(2)}) %collective-permute-start) | collective-permute-done | bytes 294944 | tf_op jit(solution)/shard_map/while/body/eval_jaxpr/ppermute | solution.py:12
  163.4 1.9 collective-permute-start
  165.4 8.8 %collective-permute-done = bf16[128,1152]{1,0:T(8,128)(2,1)S(1)} collective-permute-done((bf16[128,1152]{1,0:T(8,128)(2,1)S(1)}, bf16[128,1152]{1,0:T(8,128)(2,1)S(1)}, u32[]{:S(2)}, u32[]{:S(2)}) %collective-permute-start) | collective-permute-done | bytes 294944 | tf_op jit(solution)/shard_map/while/body/eval_jaxpr/ppermute | solution.py:12
  176.1 1.9 collective-permute-start
  178.0 8.8 %collective-permute-done = bf16[128,1152]{1,0:T(8,128)(2,1)S(1)} collective-permute-done((bf16[128,1152]{1,0:T(8,128)(2,1)S(1)}, bf16[128,1152]{1,0:T(8,128)(2,1)S(1)}, u32[]{:S(2)}, u32[]{:S(2)}) %collective-permute-start) | collective-permute-done | bytes 294944 | tf_op jit(solution)/shard_map/while/body/eval_jaxpr/ppermute | solution.py:12
  188.7 1.9 collective-permute-start
  190.6 8.9 %collective-permute-done = bf16[128,1152]{1,0:T(8,128)(2,1)S(1)} collective-permute-done((bf16[128,1152]{1,0:T(8,128)(2,1)S(1)}, bf16[128,1152]{1,0:T(8,128)(2,1)S(1)}, u32[]{:S(2)}, u32[]{:S(2)}) %collective-permute-start) | collective-permute-done | bytes 294944 | tf_op jit(solution)/shard_map/while/body/eval_jaxpr/ppermute | solution.py:12
  201.4 1.9 collective-permute-start
  203.4 10.0 %collective-permute-done = bf16[128,1152]{1,0:T(8,128)(2,1)S(1)} collective-permute-done((bf16[128,1152]{1,0:T(8,128)(2,1)S(1)}, bf16[128,1152]{1,0:T(8,128)(2,1)S(1)}, u32[]{:S(2)}, u32[]{:S(2)}) %collective-permute-start) | collective-permute-done | bytes 294944 | tf_op jit(solution)/shard_map/while/body/eval_jaxpr/ppermute | solution.py:12
  215.3 1.9 collective-permute-start
  217.2 11.2 %collective-permute-done = bf16[128,1152]{1,0:T(8,128)(2,1)S(1)} collective-permute-done((bf16[128,1152]{1,0:T(8,128)(2,1)S(1)}, bf16[128,1152]{1,0:T(8,128)(2,1)S(1)}, u32[]{:S(2)}, u32[]{:S(2)}) %collective-permute-start) | collective-permute-done | bytes 294944 | tf_op jit(solution)/shard_map/while/body/eval_jaxpr/ppermute | solution.py:12
  230.3 1.9 collective-permute-start
  232.2 11.6 %collective-permute-done = bf16[128,1152]{1,0:T(8,128)(2,1)S(1)} collective-permute-done((bf16[128,1152]{1,0:T(8,128)(2,1)S(1)}, bf16[128,1152]{1,0:T(8,128)(2,1)S(1)}, u32[]{:S(2)}, u32[]{:S(2)}) %collective-permute-start) | collective-permute-done | bytes 294944 | tf_op jit(solution)/shard_map/while/body/eval_jaxpr/ppermute | solution.py:12
  245.7 1.9 collective-permute-start
  247.6 10.8 %collective-permute-done = bf16[128,1152]{1,0:T(8,128)(2,1)S(1)} collective-permute-done((bf16[128,1152]{1,0:T(8,128)(2,1)S(1)}, bf16[128,1152]{1,0:T(8,128)(2,1)S(1)}, u32[]{:S(2)}, u32[]{:S(2)}) %collective-permute-start) | collective-permute-done | bytes 294944 | tf_op jit(solution)/shard_map/while/body/eval_jaxpr/ppermute | solution.py:12
  260.3 1.9 collective-permute-start
  262.2 9.9 %collective-permute-done = bf16[128,1152]{1,0:T(8,128)(2,1)S(1)} collective-permute-done((bf16[128,1152]{1,0:T(8,128)(2,1)S(1)}, bf16[128,1152]{1,0:T(8,128)(2,1)S(1)}, u32[]{:S(2)}, u32[]{:S(2)}) %collective-permute-start) | collective-permute-done | bytes 294944 | tf_op jit(solution)/shard_map/while/body/eval_jaxpr/ppermute | solution.py:12
  274.1 1.9 collective-permute-start
  276.0 8.8 %collective-permute-done = bf16[128,1152]{1,0:T(8,128)(2,1)S(1)} collective-permute-done((bf16[128,1152]{1,0:T(8,128)(2,1)S(1)}, bf16[128,1152]{1,0:T(8,128)(2,1)S(1)}, u32[]{:S(2)}, u32[]{:S(2)}) %collective-permute-start) | collective-permute-done | bytes 294944 | tf_op jit(solution)/shard_map/while/body/eval_jaxpr/ppermute | solution.py:12
  286.8 3.9 convolution_convert_fusion
  290.8 87.5 %fusion = bf16[48,1152]{1,0:T(8,128)(2,1)S(1)} fusion(bf16[1152,1152]{1,0:T(8,128)(2,1)} %convolution_convert_fusion), kind=kCustom, calls=%all-reduce-scatter | all-reduce-scatter fusion | flops 1769473 | bytes 2766848
  380.9 1.9 collective-permute-start.9
  386.1 6.5 %collective-permute-start.5 = (bf16[48,1152]{1,0:T(8,128)(2,1)S(1)}, bf16[48,1152]{1,0:T(8,128)(2,1)S(1)}, u32[]{:S(2)}, u32[]{:S(2)}) collective-permute-start(bf16[48,1152]{1,0:T(8,128)(2,1)S(1)} %fusion), channel_id=1, source_target_pairs={{0,4},{1,5},{2,6},{3,7},{4,8},{5,9},{6,10},{7,11},{8,12},{9,13},{1... | collective-permute-start | bytes 331784
  393.9 6.7 %collective-permute-start.3 = (bf16[48,1152]{1,0:T(8,128)(2,1)S(1)}, bf16[48,1152]{1,0:T(8,128)(2,1)S(1)}, u32[]{:S(2)}, u32[]{:S(2)}) collective-permute-start(bf16[48,1152]{1,0:T(8,128)(2,1)S(1)} %fusion), channel_id=1, source_target_pairs={{0,2},{1,3},{2,4},{3,5},{4,6},{5,7},{6,8},{7,9},{8,10},{9,11},{10,... | collective-permute-start | bytes 331784
  400.6 4.5 collective-permute-start.2
  405.4 5.1 collective-permute-done.3
  410.5 3.8 concatenate
  415.1 207.8 %while.29 = (s32[]{:T(128)}, bf16[128,1152]{1,0:T(8,128)(2,1)S(1)}, f32[128,1152]{1,0:T(8,128)S(1)}, f32[]{:T(128)}, f32[]{:T(128)}, /*index=5*/bf16[128,1152]{1,0:T(8,128)(2,1)S(1)}, f32[]{:T(128)}, s32[]{:T(128)}) while((s32[]{:T(128)}, bf16[128,1152]{1,0:T(8,128)(2,1)S(1)}, f32[128,1152]{1,0:T(8,128)S(1)}, f32[]{:T(128)}, f32[]{:T(128)}, ...), condition=%wide.region_8.10_spmd, body=%wide.region_7.9_spmd.sunk | while | flops 75907072 | bytes 3539081 | solution.py:22
  415.1 1.9 collective-permute-start.1
  417.1 11.5 %collective-permute-done.1 = bf16[128,1152]{1,0:T(8,128)(2,1)S(1)} collective-permute-done((bf16[128,1152]{1,0:T(8,128)(2,1)S(1)}, bf16[128,1152]{1,0:T(8,128)(2,1)S(1)}, u32[]{:S(2)}, u32[]{:S(2)}) %collective-permute-start.1) | collective-permute-done | bytes 294944 | tf_op jit(solution)/shard_map/while/body/eval_jaxpr/ppermute | solution.py:12
  430.5 1.9 collective-permute-start.1
  432.5 11.6 %collective-permute-done.1 = bf16[128,1152]{1,0:T(8,128)(2,1)S(1)} collective-permute-done((bf16[128,1152]{1,0:T(8,128)(2,1)S(1)}, bf16[128,1152]{1,0:T(8,128)(2,1)S(1)}, u32[]{:S(2)}, u32[]{:S(2)}) %collective-permute-start.1) | collective-permute-done | bytes 294944 | tf_op jit(solution)/shard_map/while/body/eval_jaxpr/ppermute | solution.py:12
  446.0 1.9 collective-permute-start.1
  447.9 10.9 %collective-permute-done.1 = bf16[128,1152]{1,0:T(8,128)(2,1)S(1)} collective-permute-done((bf16[128,1152]{1,0:T(8,128)(2,1)S(1)}, bf16[128,1152]{1,0:T(8,128)(2,1)S(1)}, u32[]{:S(2)}, u32[]{:S(2)}) %collective-permute-start.1) | collective-permute-done | bytes 294944 | tf_op jit(solution)/shard_map/while/body/eval_jaxpr/ppermute | solution.py:12
  460.8 1.9 collective-permute-start.1
  462.7 10.0 %collective-permute-done.1 = bf16[128,1152]{1,0:T(8,128)(2,1)S(1)} collective-permute-done((bf16[128,1152]{1,0:T(8,128)(2,1)S(1)}, bf16[128,1152]{1,0:T(8,128)(2,1)S(1)}, u32[]{:S(2)}, u32[]{:S(2)}) %collective-permute-start.1) | collective-permute-done | bytes 294944 | tf_op jit(solution)/shard_map/while/body/eval_jaxpr/ppermute | solution.py:12
  476.6 8.9 %collective-permute-done.1 = bf16[128,1152]{1,0:T(8,128)(2,1)S(1)} collective-permute-done((bf16[128,1152]{1,0:T(8,128)(2,1)S(1)}, bf16[128,1152]{1,0:T(8,128)(2,1)S(1)}, u32[]{:S(2)}, u32[]{:S(2)}) %collective-permute-start.1) | collective-permute-done | bytes 294944 | tf_op jit(solution)/shard_map/while/body/eval_jaxpr/ppermute | solution.py:12
  487.5 1.9 collective-permute-start.1
  489.4 8.8 %collective-permute-done.1 = bf16[128,1152]{1,0:T(8,128)(2,1)S(1)} collective-permute-done((bf16[128,1152]{1,0:T(8,128)(2,1)S(1)}, bf16[128,1152]{1,0:T(8,128)(2,1)S(1)}, u32[]{:S(2)}, u32[]{:S(2)}) %collective-permute-start.1) | collective-permute-done | bytes 294944 | tf_op jit(solution)/shard_map/while/body/eval_jaxpr/ppermute | solution.py:12
  502.1 9.0 %collective-permute-done.1 = bf16[128,1152]{1,0:T(8,128)(2,1)S(1)} collective-permute-done((bf16[128,1152]{1,0:T(8,128)(2,1)S(1)}, bf16[128,1152]{1,0:T(8,128)(2,1)S(1)}, u32[]{:S(2)}, u32[]{:S(2)}) %collective-permute-start.1) | collective-permute-done | bytes 294944 | tf_op jit(solution)/shard_map/while/body/eval_jaxpr/ppermute | solution.py:12
  515.0 8.9 %collective-permute-done.1 = bf16[128,1152]{1,0:T(8,128)(2,1)S(1)} collective-permute-done((bf16[128,1152]{1,0:T(8,128)(2,1)S(1)}, bf16[128,1152]{1,0:T(8,128)(2,1)S(1)}, u32[]{:S(2)}, u32[]{:S(2)}) %collective-permute-start.1) | collective-permute-done | bytes 294944 | tf_op jit(solution)/shard_map/while/body/eval_jaxpr/ppermute | solution.py:12
  527.8 8.9 %collective-permute-done.1 = bf16[128,1152]{1,0:T(8,128)(2,1)S(1)} collective-permute-done((bf16[128,1152]{1,0:T(8,128)(2,1)S(1)}, bf16[128,1152]{1,0:T(8,128)(2,1)S(1)}, u32[]{:S(2)}, u32[]{:S(2)}) %collective-permute-start.1) | collective-permute-done | bytes 294944 | tf_op jit(solution)/shard_map/while/body/eval_jaxpr/ppermute | solution.py:12
  540.6 8.8 %collective-permute-done.1 = bf16[128,1152]{1,0:T(8,128)(2,1)S(1)} collective-permute-done((bf16[128,1152]{1,0:T(8,128)(2,1)S(1)}, bf16[128,1152]{1,0:T(8,128)(2,1)S(1)}, u32[]{:S(2)}, u32[]{:S(2)}) %collective-permute-start.1) | collective-permute-done | bytes 294944 | tf_op jit(solution)/shard_map/while/body/eval_jaxpr/ppermute | solution.py:12
  553.3 9.6 %collective-permute-done.1 = bf16[128,1152]{1,0:T(8,128)(2,1)S(1)} collective-permute-done((bf16[128,1152]{1,0:T(8,128)(2,1)S(1)}, bf16[128,1152]{1,0:T(8,128)(2,1)S(1)}, u32[]{:S(2)}, u32[]{:S(2)}) %collective-permute-start.1) | collective-permute-done | bytes 294944 | tf_op jit(solution)/shard_map/while/body/eval_jaxpr/ppermute | solution.py:12
  566.8 10.8 %collective-permute-done.1 = bf16[128,1152]{1,0:T(8,128)(2,1)S(1)} collective-permute-done((bf16[128,1152]{1,0:T(8,128)(2,1)S(1)}, bf16[128,1152]{1,0:T(8,128)(2,1)S(1)}, u32[]{:S(2)}, u32[]{:S(2)}) %collective-permute-start.1) | collective-permute-done | bytes 294944 | tf_op jit(solution)/shard_map/while/body/eval_jaxpr/ppermute | solution.py:12
  581.4 11.9 %collective-permute-done.1 = bf16[128,1152]{1,0:T(8,128)(2,1)S(1)} collective-permute-done((bf16[128,1152]{1,0:T(8,128)(2,1)S(1)}, bf16[128,1152]{1,0:T(8,128)(2,1)S(1)}, u32[]{:S(2)}, u32[]{:S(2)}) %collective-permute-start.1) | collective-permute-done | bytes 294944 | tf_op jit(solution)/shard_map/while/body/eval_jaxpr/ppermute | solution.py:12
  595.3 1.9 collective-permute-start.1
  597.2 11.1 %collective-permute-done.1 = bf16[128,1152]{1,0:T(8,128)(2,1)S(1)} collective-permute-done((bf16[128,1152]{1,0:T(8,128)(2,1)S(1)}, bf16[128,1152]{1,0:T(8,128)(2,1)S(1)}, u32[]{:S(2)}, u32[]{:S(2)}) %collective-permute-start.1) | collective-permute-done | bytes 294944 | tf_op jit(solution)/shard_map/while/body/eval_jaxpr/ppermute | solution.py:12
  612.2 8.8 %collective-permute-done.1 = bf16[128,1152]{1,0:T(8,128)(2,1)S(1)} collective-permute-done((bf16[128,1152]{1,0:T(8,128)(2,1)S(1)}, bf16[128,1152]{1,0:T(8,128)(2,1)S(1)}, u32[]{:S(2)}, u32[]{:S(2)}) %collective-permute-start.1) | collective-permute-done | bytes 294944 | tf_op jit(solution)/shard_map/while/body/eval_jaxpr/ppermute | solution.py:12
  623.1 2.3 scatter_custom_fusion
  (121 shorter events, 89.3 us)
Async XLA Ops:
  7.2 4.0 copy-start
  7.2 4.9 copy-start.1
  7.2 68.9 %all-gather.3.cloned.1.call-start = ((), (), s32[]{:S(2)}) async-start(), calls=%async_computation.1 | async-start | bytes 3041280 | tf_op jit(solution)/shard_map/all_gather | solution.py:35
  7.9 617.5 %all-reduce.4.cloned.1.call-start = ((), (), s32[]{:S(2)}) async-start(), calls=%async_computation | async-start | bytes 368640 | tf_op jit(solution)/shard_map/psum | solution.py:97
  10.6 0.6 copy-start.6
  11.2 1.8 copy-start.7
  12.1 1.2 copy-start.2
  13.3 67.2 %copy-start.4 = (f32[128]{0:T(128)}, f32[128]{0:T(128)S(1)}, u32[]{:S(2)}) copy-start(f32[128]{0:T(128)S(1)} %add_sqrt_fusion.1) | copy-start | bytes 1540
  79.7 1.0 copy-start.3
  81.4 13.8 %collective-permute-start = (bf16[128,1152]{1,0:T(8,128)(2,1)S(1)}, bf16[128,1152]{1,0:T(8,128)(2,1)S(1)}, u32[]{:S(2)}, u32[]{:S(2)}) collective-permute-start(bf16[128,1152]{1,0:T(8,128)(2,1)S(1)} %get-tuple-element.300), channel_id=1, source_target_pairs={{0,32},{32,64},{64,96},{96,128},{128,160},{160,192},{192,224},{224... | collective-permute-start | bytes 884744 | tf_op jit(solution)/shard_map/while/body/eval_jaxpr/ppermute | solution.py:12
  97.1 12.7 %collective-permute-start = (bf16[128,1152]{1,0:T(8,128)(2,1)S(1)}, bf16[128,1152]{1,0:T(8,128)(2,1)S(1)}, u32[]{:S(2)}, u32[]{:S(2)}) collective-permute-start(bf16[128,1152]{1,0:T(8,128)(2,1)S(1)} %get-tuple-element.300), channel_id=1, source_target_pairs={{0,32},{32,64},{64,96},{96,128},{128,160},{160,192},{192,224},{224... | collective-permute-start | bytes 884744 | tf_op jit(solution)/shard_map/while/body/eval_jaxpr/ppermute | solution.py:12
  111.7 11.8 %collective-permute-start = (bf16[128,1152]{1,0:T(8,128)(2,1)S(1)}, bf16[128,1152]{1,0:T(8,128)(2,1)S(1)}, u32[]{:S(2)}, u32[]{:S(2)}) collective-permute-start(bf16[128,1152]{1,0:T(8,128)(2,1)S(1)} %get-tuple-element.300), channel_id=1, source_target_pairs={{0,32},{32,64},{64,96},{96,128},{128,160},{160,192},{192,224},{224... | collective-permute-start | bytes 884744 | tf_op jit(solution)/shard_map/while/body/eval_jaxpr/ppermute | solution.py:12
  125.4 10.9 %collective-permute-start = (bf16[128,1152]{1,0:T(8,128)(2,1)S(1)}, bf16[128,1152]{1,0:T(8,128)(2,1)S(1)}, u32[]{:S(2)}, u32[]{:S(2)}) collective-permute-start(bf16[128,1152]{1,0:T(8,128)(2,1)S(1)} %get-tuple-element.300), channel_id=1, source_target_pairs={{0,32},{32,64},{64,96},{96,128},{128,160},{160,192},{192,224},{224... | collective-permute-start | bytes 884744 | tf_op jit(solution)/shard_map/while/body/eval_jaxpr/ppermute | solution.py:12
  138.2 10.7 %collective-permute-start = (bf16[128,1152]{1,0:T(8,128)(2,1)S(1)}, bf16[128,1152]{1,0:T(8,128)(2,1)S(1)}, u32[]{:S(2)}, u32[]{:S(2)}) collective-permute-start(bf16[128,1152]{1,0:T(8,128)(2,1)S(1)} %get-tuple-element.300), channel_id=1, source_target_pairs={{0,32},{32,64},{64,96},{96,128},{128,160},{160,192},{192,224},{224... | collective-permute-start | bytes 884744 | tf_op jit(solution)/shard_map/while/body/eval_jaxpr/ppermute | solution.py:12
  150.8 10.7 %collective-permute-start = (bf16[128,1152]{1,0:T(8,128)(2,1)S(1)}, bf16[128,1152]{1,0:T(8,128)(2,1)S(1)}, u32[]{:S(2)}, u32[]{:S(2)}) collective-permute-start(bf16[128,1152]{1,0:T(8,128)(2,1)S(1)} %get-tuple-element.300), channel_id=1, source_target_pairs={{0,32},{32,64},{64,96},{96,128},{128,160},{160,192},{192,224},{224... | collective-permute-start | bytes 884744 | tf_op jit(solution)/shard_map/while/body/eval_jaxpr/ppermute | solution.py:12
  163.4 10.7 %collective-permute-start = (bf16[128,1152]{1,0:T(8,128)(2,1)S(1)}, bf16[128,1152]{1,0:T(8,128)(2,1)S(1)}, u32[]{:S(2)}, u32[]{:S(2)}) collective-permute-start(bf16[128,1152]{1,0:T(8,128)(2,1)S(1)} %get-tuple-element.300), channel_id=1, source_target_pairs={{0,32},{32,64},{64,96},{96,128},{128,160},{160,192},{192,224},{224... | collective-permute-start | bytes 884744 | tf_op jit(solution)/shard_map/while/body/eval_jaxpr/ppermute | solution.py:12
  176.1 10.7 %collective-permute-start = (bf16[128,1152]{1,0:T(8,128)(2,1)S(1)}, bf16[128,1152]{1,0:T(8,128)(2,1)S(1)}, u32[]{:S(2)}, u32[]{:S(2)}) collective-permute-start(bf16[128,1152]{1,0:T(8,128)(2,1)S(1)} %get-tuple-element.300), channel_id=1, source_target_pairs={{0,32},{32,64},{64,96},{96,128},{128,160},{160,192},{192,224},{224... | collective-permute-start | bytes 884744 | tf_op jit(solution)/shard_map/while/body/eval_jaxpr/ppermute | solution.py:12
  188.7 10.9 %collective-permute-start = (bf16[128,1152]{1,0:T(8,128)(2,1)S(1)}, bf16[128,1152]{1,0:T(8,128)(2,1)S(1)}, u32[]{:S(2)}, u32[]{:S(2)}) collective-permute-start(bf16[128,1152]{1,0:T(8,128)(2,1)S(1)} %get-tuple-element.300), channel_id=1, source_target_pairs={{0,32},{32,64},{64,96},{96,128},{128,160},{160,192},{192,224},{224... | collective-permute-start | bytes 884744 | tf_op jit(solution)/shard_map/while/body/eval_jaxpr/ppermute | solution.py:12
  201.4 11.9 %collective-permute-start = (bf16[128,1152]{1,0:T(8,128)(2,1)S(1)}, bf16[128,1152]{1,0:T(8,128)(2,1)S(1)}, u32[]{:S(2)}, u32[]{:S(2)}) collective-permute-start(bf16[128,1152]{1,0:T(8,128)(2,1)S(1)} %get-tuple-element.300), channel_id=1, source_target_pairs={{0,32},{32,64},{64,96},{96,128},{128,160},{160,192},{192,224},{224... | collective-permute-start | bytes 884744 | tf_op jit(solution)/shard_map/while/body/eval_jaxpr/ppermute | solution.py:12
  215.3 13.1 %collective-permute-start = (bf16[128,1152]{1,0:T(8,128)(2,1)S(1)}, bf16[128,1152]{1,0:T(8,128)(2,1)S(1)}, u32[]{:S(2)}, u32[]{:S(2)}) collective-permute-start(bf16[128,1152]{1,0:T(8,128)(2,1)S(1)} %get-tuple-element.300), channel_id=1, source_target_pairs={{0,32},{32,64},{64,96},{96,128},{128,160},{160,192},{192,224},{224... | collective-permute-start | bytes 884744 | tf_op jit(solution)/shard_map/while/body/eval_jaxpr/ppermute | solution.py:12
  230.3 13.5 %collective-permute-start = (bf16[128,1152]{1,0:T(8,128)(2,1)S(1)}, bf16[128,1152]{1,0:T(8,128)(2,1)S(1)}, u32[]{:S(2)}, u32[]{:S(2)}) collective-permute-start(bf16[128,1152]{1,0:T(8,128)(2,1)S(1)} %get-tuple-element.300), channel_id=1, source_target_pairs={{0,32},{32,64},{64,96},{96,128},{128,160},{160,192},{192,224},{224... | collective-permute-start | bytes 884744 | tf_op jit(solution)/shard_map/while/body/eval_jaxpr/ppermute | solution.py:12
  245.7 12.8 %collective-permute-start = (bf16[128,1152]{1,0:T(8,128)(2,1)S(1)}, bf16[128,1152]{1,0:T(8,128)(2,1)S(1)}, u32[]{:S(2)}, u32[]{:S(2)}) collective-permute-start(bf16[128,1152]{1,0:T(8,128)(2,1)S(1)} %get-tuple-element.300), channel_id=1, source_target_pairs={{0,32},{32,64},{64,96},{96,128},{128,160},{160,192},{192,224},{224... | collective-permute-start | bytes 884744 | tf_op jit(solution)/shard_map/while/body/eval_jaxpr/ppermute | solution.py:12
  260.3 11.9 %collective-permute-start = (bf16[128,1152]{1,0:T(8,128)(2,1)S(1)}, bf16[128,1152]{1,0:T(8,128)(2,1)S(1)}, u32[]{:S(2)}, u32[]{:S(2)}) collective-permute-start(bf16[128,1152]{1,0:T(8,128)(2,1)S(1)} %get-tuple-element.300), channel_id=1, source_target_pairs={{0,32},{32,64},{64,96},{96,128},{128,160},{160,192},{192,224},{224... | collective-permute-start | bytes 884744 | tf_op jit(solution)/shard_map/while/body/eval_jaxpr/ppermute | solution.py:12
  274.1 10.7 %collective-permute-start = (bf16[128,1152]{1,0:T(8,128)(2,1)S(1)}, bf16[128,1152]{1,0:T(8,128)(2,1)S(1)}, u32[]{:S(2)}, u32[]{:S(2)}) collective-permute-start(bf16[128,1152]{1,0:T(8,128)(2,1)S(1)} %get-tuple-element.300), channel_id=1, source_target_pairs={{0,32},{32,64},{64,96},{96,128},{128,160},{160,192},{192,224},{224... | collective-permute-start | bytes 884744 | tf_op jit(solution)/shard_map/while/body/eval_jaxpr/ppermute | solution.py:12
  378.3 15.6 %collective-permute-start.8 = (bf16[48,1152]{1,0:T(8,128)(2,1)S(1)}, bf16[48,1152]{1,0:T(8,128)(2,1)S(1)}, u32[]{:S(2)}, u32[]{:S(2)}) collective-permute-start(bf16[48,1152]{1,0:T(8,128)(2,1)S(1)} %fusion), channel_id=1, source_target_pairs={{0,7},{1,8},{2,9},{3,10},{4,11},{5,12},{6,13},{7,14},{8,15},{9,16}... | collective-permute-start | bytes 331784
  379.6 21.1 %collective-permute-start.7 = (bf16[48,1152]{1,0:T(8,128)(2,1)S(1)}, bf16[48,1152]{1,0:T(8,128)(2,1)S(1)}, u32[]{:S(2)}, u32[]{:S(2)}) collective-permute-start(bf16[48,1152]{1,0:T(8,128)(2,1)S(1)} %fusion), channel_id=1, source_target_pairs={{0,6},{1,7},{2,8},{3,9},{4,10},{5,11},{6,12},{7,13},{8,14},{9,15},... | collective-permute-start | bytes 331784
  380.9 11.7 %collective-permute-start.9 = (bf16[36,1152]{1,0:T(8,128)(2,1)S(1)}, bf16[36,1152]{1,0:T(8,128)(2,1)}, u32[]{:S(2)}, u32[]{:S(2)}) collective-permute-start(bf16[36,1152]{1,0:T(8,128)(2,1)S(1)} %slice.4), channel_id=1, source_target_pairs={{0,8},{1,9},{2,10},{3,11},{4,12},{5,13},{6,14},{7,15},{8,16},{9,17... | collective-permute-start | bytes 248840
  384.7 20.6 %collective-permute-start.6 = (bf16[48,1152]{1,0:T(8,128)(2,1)S(1)}, bf16[48,1152]{1,0:T(8,128)(2,1)S(1)}, u32[]{:S(2)}, u32[]{:S(2)}) collective-permute-start(bf16[48,1152]{1,0:T(8,128)(2,1)S(1)} %fusion), channel_id=1, source_target_pairs={{0,5},{1,6},{2,7},{3,8},{4,9},{5,10},{6,11},{7,12},{8,13},{9,14},{... | collective-permute-start | bytes 331784
  386.1 19.3 %collective-permute-start.5 = (bf16[48,1152]{1,0:T(8,128)(2,1)S(1)}, bf16[48,1152]{1,0:T(8,128)(2,1)S(1)}, u32[]{:S(2)}, u32[]{:S(2)}) collective-permute-start(bf16[48,1152]{1,0:T(8,128)(2,1)S(1)} %fusion), channel_id=1, source_target_pairs={{0,4},{1,5},{2,6},{3,7},{4,8},{5,9},{6,10},{7,11},{8,12},{9,13},{1... | collective-permute-start | bytes 331784
  392.6 12.8 %collective-permute-start.4 = (bf16[48,1152]{1,0:T(8,128)(2,1)S(1)}, bf16[48,1152]{1,0:T(8,128)(2,1)S(1)}, u32[]{:S(2)}, u32[]{:S(2)}) collective-permute-start(bf16[48,1152]{1,0:T(8,128)(2,1)S(1)} %fusion), channel_id=1, source_target_pairs={{0,3},{1,4},{2,5},{3,6},{4,7},{5,8},{6,9},{7,10},{8,11},{9,12},{10... | collective-permute-start | bytes 331784
  393.9 16.7 %collective-permute-start.3 = (bf16[48,1152]{1,0:T(8,128)(2,1)S(1)}, bf16[48,1152]{1,0:T(8,128)(2,1)S(1)}, u32[]{:S(2)}, u32[]{:S(2)}) collective-permute-start(bf16[48,1152]{1,0:T(8,128)(2,1)S(1)} %fusion), channel_id=1, source_target_pairs={{0,2},{1,3},{2,4},{3,5},{4,6},{5,7},{6,8},{7,9},{8,10},{9,11},{10,... | collective-permute-start | bytes 331784
  400.6 9.9 %collective-permute-start.2 = (bf16[48,1152]{1,0:T(8,128)(2,1)S(1)}, bf16[48,1152]{1,0:T(8,128)(2,1)}, u32[]{:S(2)}, u32[]{:S(2)}) collective-permute-start(bf16[48,1152]{1,0:T(8,128)(2,1)S(1)} %fusion), channel_id=1, source_target_pairs={{0,1},{1,2},{2,3},{3,4},{4,5},{5,6},{6,7},{7,8},{8,9},{9,10},{10,1... | collective-permute-start | bytes 331784
  415.1 208.0 %copy-start.5 = (f32[128]{0:T(128)S(1)}, f32[128]{0:T(128)}, u32[]{:S(2)}) copy-start(f32[128]{0:T(128)} %copy-done.4) | copy-start | bytes 1540
  415.1 13.4 %collective-permute-start.1 = (bf16[128,1152]{1,0:T(8,128)(2,1)S(1)}, bf16[128,1152]{1,0:T(8,128)(2,1)S(1)}, u32[]{:S(2)}, u32[]{:S(2)}) collective-permute-start(bf16[128,1152]{1,0:T(8,128)(2,1)S(1)} %get-tuple-element.324), channel_id=1, source_target_pairs={{0,32},{32,64},{64,96},{96,128},{128,160},{160,192},{192,224},{224... | collective-permute-start | bytes 884744 | tf_op jit(solution)/shard_map/while/body/eval_jaxpr/ppermute | solution.py:12
  430.5 13.5 %collective-permute-start.1 = (bf16[128,1152]{1,0:T(8,128)(2,1)S(1)}, bf16[128,1152]{1,0:T(8,128)(2,1)S(1)}, u32[]{:S(2)}, u32[]{:S(2)}) collective-permute-start(bf16[128,1152]{1,0:T(8,128)(2,1)S(1)} %get-tuple-element.324), channel_id=1, source_target_pairs={{0,32},{32,64},{64,96},{96,128},{128,160},{160,192},{192,224},{224... | collective-permute-start | bytes 884744 | tf_op jit(solution)/shard_map/while/body/eval_jaxpr/ppermute | solution.py:12
  446.0 12.8 %collective-permute-start.1 = (bf16[128,1152]{1,0:T(8,128)(2,1)S(1)}, bf16[128,1152]{1,0:T(8,128)(2,1)S(1)}, u32[]{:S(2)}, u32[]{:S(2)}) collective-permute-start(bf16[128,1152]{1,0:T(8,128)(2,1)S(1)} %get-tuple-element.324), channel_id=1, source_target_pairs={{0,32},{32,64},{64,96},{96,128},{128,160},{160,192},{192,224},{224... | collective-permute-start | bytes 884744 | tf_op jit(solution)/shard_map/while/body/eval_jaxpr/ppermute | solution.py:12
  460.8 12.0 %collective-permute-start.1 = (bf16[128,1152]{1,0:T(8,128)(2,1)S(1)}, bf16[128,1152]{1,0:T(8,128)(2,1)S(1)}, u32[]{:S(2)}, u32[]{:S(2)}) collective-permute-start(bf16[128,1152]{1,0:T(8,128)(2,1)S(1)} %get-tuple-element.324), channel_id=1, source_target_pairs={{0,32},{32,64},{64,96},{96,128},{128,160},{160,192},{192,224},{224... | collective-permute-start | bytes 884744 | tf_op jit(solution)/shard_map/while/body/eval_jaxpr/ppermute | solution.py:12
  474.7 10.8 %collective-permute-start.1 = (bf16[128,1152]{1,0:T(8,128)(2,1)S(1)}, bf16[128,1152]{1,0:T(8,128)(2,1)S(1)}, u32[]{:S(2)}, u32[]{:S(2)}) collective-permute-start(bf16[128,1152]{1,0:T(8,128)(2,1)S(1)} %get-tuple-element.324), channel_id=1, source_target_pairs={{0,32},{32,64},{64,96},{96,128},{128,160},{160,192},{192,224},{224... | collective-permute-start | bytes 884744 | tf_op jit(solution)/shard_map/while/body/eval_jaxpr/ppermute | solution.py:12
  487.5 10.7 %collective-permute-start.1 = (bf16[128,1152]{1,0:T(8,128)(2,1)S(1)}, bf16[128,1152]{1,0:T(8,128)(2,1)S(1)}, u32[]{:S(2)}, u32[]{:S(2)}) collective-permute-start(bf16[128,1152]{1,0:T(8,128)(2,1)S(1)} %get-tuple-element.324), channel_id=1, source_target_pairs={{0,32},{32,64},{64,96},{96,128},{128,160},{160,192},{192,224},{224... | collective-permute-start | bytes 884744 | tf_op jit(solution)/shard_map/while/body/eval_jaxpr/ppermute | solution.py:12
  500.1 11.0 %collective-permute-start.1 = (bf16[128,1152]{1,0:T(8,128)(2,1)S(1)}, bf16[128,1152]{1,0:T(8,128)(2,1)S(1)}, u32[]{:S(2)}, u32[]{:S(2)}) collective-permute-start(bf16[128,1152]{1,0:T(8,128)(2,1)S(1)} %get-tuple-element.324), channel_id=1, source_target_pairs={{0,32},{32,64},{64,96},{96,128},{128,160},{160,192},{192,224},{224... | collective-permute-start | bytes 884744 | tf_op jit(solution)/shard_map/while/body/eval_jaxpr/ppermute | solution.py:12
  513.1 10.8 %collective-permute-start.1 = (bf16[128,1152]{1,0:T(8,128)(2,1)S(1)}, bf16[128,1152]{1,0:T(8,128)(2,1)S(1)}, u32[]{:S(2)}, u32[]{:S(2)}) collective-permute-start(bf16[128,1152]{1,0:T(8,128)(2,1)S(1)} %get-tuple-element.324), channel_id=1, source_target_pairs={{0,32},{32,64},{64,96},{96,128},{128,160},{160,192},{192,224},{224... | collective-permute-start | bytes 884744 | tf_op jit(solution)/shard_map/while/body/eval_jaxpr/ppermute | solution.py:12
  525.9 10.8 %collective-permute-start.1 = (bf16[128,1152]{1,0:T(8,128)(2,1)S(1)}, bf16[128,1152]{1,0:T(8,128)(2,1)S(1)}, u32[]{:S(2)}, u32[]{:S(2)}) collective-permute-start(bf16[128,1152]{1,0:T(8,128)(2,1)S(1)} %get-tuple-element.324), channel_id=1, source_target_pairs={{0,32},{32,64},{64,96},{96,128},{128,160},{160,192},{192,224},{224... | collective-permute-start | bytes 884744 | tf_op jit(solution)/shard_map/while/body/eval_jaxpr/ppermute | solution.py:12
  538.6 10.7 %collective-permute-start.1 = (bf16[128,1152]{1,0:T(8,128)(2,1)S(1)}, bf16[128,1152]{1,0:T(8,128)(2,1)S(1)}, u32[]{:S(2)}, u32[]{:S(2)}) collective-permute-start(bf16[128,1152]{1,0:T(8,128)(2,1)S(1)} %get-tuple-element.324), channel_id=1, source_target_pairs={{0,32},{32,64},{64,96},{96,128},{128,160},{160,192},{192,224},{224... | collective-permute-start | bytes 884744 | tf_op jit(solution)/shard_map/while/body/eval_jaxpr/ppermute | solution.py:12
  551.3 11.6 %collective-permute-start.1 = (bf16[128,1152]{1,0:T(8,128)(2,1)S(1)}, bf16[128,1152]{1,0:T(8,128)(2,1)S(1)}, u32[]{:S(2)}, u32[]{:S(2)}) collective-permute-start(bf16[128,1152]{1,0:T(8,128)(2,1)S(1)} %get-tuple-element.324), channel_id=1, source_target_pairs={{0,32},{32,64},{64,96},{96,128},{128,160},{160,192},{192,224},{224... | collective-permute-start | bytes 884744 | tf_op jit(solution)/shard_map/while/body/eval_jaxpr/ppermute | solution.py:12
  564.8 12.7 %collective-permute-start.1 = (bf16[128,1152]{1,0:T(8,128)(2,1)S(1)}, bf16[128,1152]{1,0:T(8,128)(2,1)S(1)}, u32[]{:S(2)}, u32[]{:S(2)}) collective-permute-start(bf16[128,1152]{1,0:T(8,128)(2,1)S(1)} %get-tuple-element.324), channel_id=1, source_target_pairs={{0,32},{32,64},{64,96},{96,128},{128,160},{160,192},{192,224},{224... | collective-permute-start | bytes 884744 | tf_op jit(solution)/shard_map/while/body/eval_jaxpr/ppermute | solution.py:12
  579.5 13.8 %collective-permute-start.1 = (bf16[128,1152]{1,0:T(8,128)(2,1)S(1)}, bf16[128,1152]{1,0:T(8,128)(2,1)S(1)}, u32[]{:S(2)}, u32[]{:S(2)}) collective-permute-start(bf16[128,1152]{1,0:T(8,128)(2,1)S(1)} %get-tuple-element.324), channel_id=1, source_target_pairs={{0,32},{32,64},{64,96},{96,128},{128,160},{160,192},{192,224},{224... | collective-permute-start | bytes 884744 | tf_op jit(solution)/shard_map/while/body/eval_jaxpr/ppermute | solution.py:12
  595.3 13.0 %collective-permute-start.1 = (bf16[128,1152]{1,0:T(8,128)(2,1)S(1)}, bf16[128,1152]{1,0:T(8,128)(2,1)S(1)}, u32[]{:S(2)}, u32[]{:S(2)}) collective-permute-start(bf16[128,1152]{1,0:T(8,128)(2,1)S(1)} %get-tuple-element.324), channel_id=1, source_target_pairs={{0,32},{32,64},{64,96},{96,128},{128,160},{160,192},{192,224},{224... | collective-permute-start | bytes 884744 | tf_op jit(solution)/shard_map/while/body/eval_jaxpr/ppermute | solution.py:12
  610.2 10.7 %collective-permute-start.1 = (bf16[128,1152]{1,0:T(8,128)(2,1)S(1)}, bf16[128,1152]{1,0:T(8,128)(2,1)S(1)}, u32[]{:S(2)}, u32[]{:S(2)}) collective-permute-start(bf16[128,1152]{1,0:T(8,128)(2,1)S(1)} %get-tuple-element.324), channel_id=1, source_target_pairs={{0,32},{32,64},{64,96},{96,128},{128,160},{160,192},{192,224},{224... | collective-permute-start | bytes 884744 | tf_op jit(solution)/shard_map/while/body/eval_jaxpr/ppermute | solution.py:12
Sparse Core Ops, SparseCore 0:
  11.2 64.8 all-gather.2
  415.2 131.0 all-reduce.3
where the time goes:
time: 637 us; the launch traced here: 634 us
  waiting for transfers between devices  365 us (57%)
  blocking collectives  87.5 us (14%)
  starting transfers between devices  84.1 us (13%)
  matrix products  61.7 us (10%)
  between operations  16.9 us (3%)
  local copies, waits for them, and re-layouts  13.6 us (2%)
    ppermute x30, waiting for transfers between devices, shifted(): return lax.ppermute(value, axis, pairs)  296 us
    unnamed x1, blocking collectives  87.5 us
    all_gather x1, waiting for transfers between devices, shards(): lax.all_gather(head_weight, 'grp', axis=0, tiled=True)  62.8 us
    ppermute x30, starting transfers between devices, shifted(): return lax.ppermute(value, axis, pairs)  59.2 us
    dot_general x15, matrix products, text_work(): lax.dot_general(grad_tile, image_blk, (((0,), (0,)), ((), ())), preferred...  28.6 us
    dot_general x15, matrix products, image_work(): jnp.dot(grad_tile, text_blk, preferred_element_type=jnp.float32)  27.7 us
    unnamed x8, starting transfers between devices  24.8 us
  transfers between devices with their start and end apart: 40, of which 32 were waited for; matrix products, arithmetic and copies ran while one was open for 6% of the time, Pallas kernels for 0%

commit v1 on v0

v1 whole, which is shorter than its diff:
```python
import jax
import jax.numpy as jnp
from jax import lax
from jax.sharding import Mesh, PartitionSpec as P

EPS = 1e-06
ALL = ("zl", "y", "x", "zh", "c")
WIDE = 640


def ring(axis, steps):
    count = lax.axis_size(axis)
    return [(source, (source + steps) % count) for source in range(count)]


def hop(value, axis, steps):
    return lax.ppermute(value, axis, ring(axis, steps))


def gather_weight(head_weight):
    core = lax.axis_index("c")
    place = lax.axis_index("x")
    rows = lax.all_gather(head_weight, "c", axis=0, tiled=True)
    width = rows.shape[1]
    part = lax.dynamic_slice(rows, (0, core * (width - WIDE)), (rows.shape[0], WIDE))
    slab = lax.all_gather(part, "zh", axis=0, tiled=True)
    before = hop(slab, "x", 1)
    after = hop(slab, "x", -1)
    half = slab.shape[0] // 2
    far_low = hop(after[:half], "x", -1)
    far_high = hop(before[half:], "x", 1)
    far = jnp.concatenate([far_low, far_high], axis=0)
    count = lax.axis_size("x")
    held = jnp.zeros((count,) + slab.shape, slab.dtype)
    for steps, block in ((0, slab), (-1, before), (1, after), (2, far)):
        spot = lax.rem(place + steps + count, count)
        held = lax.dynamic_update_slice(held, block[None], (spot, 0, 0))
    mine = held.reshape(count * slab.shape[0], WIDE)
    other = hop(mine, "c", 1)
    low = jnp.where(core == 0, mine, other)
    high = jnp.where(core == 0, other, mine)
    return low, high


def shards(image_cand, text_cand, selection, head_weight, logit_temp, logit_offset, loss_scale):
    pairs = selection.shape[0]
    depth = image_cand.shape[1]
    width = head_weight.shape[1]
    n_y, n_x, n_zh = lax.axis_size("y"), lax.axis_size("x"), lax.axis_size("zh")
    my_zl, my_y, core = lax.axis_index("zl"), lax.axis_index("y"), lax.axis_index("c")
    total = pairs * lax.axis_size(ALL)

    picked = image_cand.at[selection].get(mode="promise_in_bounds")
    images = lax.all_gather(picked, "y", axis=0, tiled=True)
    texts = text_cand.at[selection].get(mode="promise_in_bounds").astype(jnp.float32)
    txt_norm = jnp.sqrt(jnp.sum(texts * texts, axis=1, keepdims=True) + EPS)
    text_unit = (texts / txt_norm).astype(jnp.bfloat16)
    text_pair = lax.all_gather(text_unit, "zl", axis=0, tiled=True)

    low, high = gather_weight(head_weight)
    proj_low = jnp.dot(images, low, preferred_element_type=jnp.float32)
    proj_high = jnp.dot(images, high[:, 2 * WIDE - width:], preferred_element_type=jnp.float32)
    projected = jnp.concatenate([proj_low, proj_high], axis=1)
    img_norm = jnp.sqrt(jnp.sum(projected * projected, axis=1, keepdims=True) + EPS)
    image_unit = (projected / img_norm).astype(jnp.bfloat16)

    temper, offset = logit_temp[0], logit_offset[0]
    factor = loss_scale[0] / total
    row_id = jnp.arange(n_y * pairs, dtype=jnp.int32)[:, None]
    col_id = jnp.arange(2 * pairs, dtype=jnp.int32)[None, :]
    same = (row_id - my_y * pairs == col_id - my_zl * pairs) & (row_id // pairs == my_y)
    label_sign = jnp.where(same, 1.0, -1.0).astype(jnp.float32)
    inner = lax.dot_general(image_unit, text_pair, (((1,), (1,)), ((), ())), preferred_element_type=jnp.float32)
    logits = temper * inner + offset
    grad_tile = (-factor * label_sign * jax.nn.sigmoid(-label_sign * logits)).astype(jnp.bfloat16)

    image_back = temper * jnp.dot(grad_tile, text_pair, preferred_element_type=jnp.float32)
    unit_float = image_unit.astype(jnp.float32)
    radial = jnp.sum(unit_float * image_back, axis=1, keepdims=True)
    proj_back = ((image_back - unit_float * radial) / img_norm).astype(jnp.bfloat16)

    def head_half(values):
        return lax.dot_general(images, values, (((0,), (0,)), ((), ())), preferred_element_type=jnp.float32)

    mid = width // 2
    halves = [proj_back[:, :mid], proj_back[:, mid:]]
    mine_cols = jnp.where(core == 0, halves[0], halves[1])
    other_cols = jnp.where(core == 0, halves[1], halves[0])
    send = head_half(other_cols).astype(jnp.bfloat16)
    got = hop(send, "c", 1)
    head = head_half(mine_cols) + got.astype(jnp.float32)

    tile_t = lax.dot_general(grad_tile, image_unit, (((0,), (0,)), ((), ())), preferred_element_type=jnp.float32)
    text_mine = lax.dynamic_slice(tile_t, (my_zl * pairs, 0), (pairs, width))
    text_other = lax.dynamic_slice(tile_t, ((1 - my_zl) * pairs, 0), (pairs, width)).astype(jnp.bfloat16)
    text_got = hop(text_other, "zl", 1)

    def spread(values, axis):
        count = lax.axis_size(axis)
        parts = values.astype(jnp.bfloat16).reshape(count, values.shape[0] // count, values.shape[1])
        came = lax.all_to_all(parts, axis, 0, 0)
        return jnp.sum(came.astype(jnp.float32), axis=0)

    head = spread(head, "x")
    head = spread(head, "zh")
    both = lax.all_gather(head.astype(jnp.bfloat16), "c", axis=0)
    half_rows = head.shape[0] // 2
    both = lax.dynamic_slice(both, (0, core * half_rows, 0), (2, half_rows, mid))
    head = jnp.concatenate([both[0], both[1]], axis=1)
    head = jnp.sum(lax.all_gather(head, "zl", axis=0).astype(jnp.float32), axis=0)
    head_grad = jnp.sum(lax.all_gather(head.astype(jnp.bfloat16), "y", axis=0).astype(jnp.float32), axis=0)

    text_back = temper * (text_mine + text_got.astype(jnp.float32))
    text_float = text_unit.astype(jnp.float32)
    text_radial = jnp.sum(text_float * text_back, axis=1, keepdims=True)
    text_rows = (text_back - text_float * text_radial) / txt_norm
    text_grad = jnp.zeros((text_cand.shape[0], width), jnp.float32).at[selection].set(
        text_rows, mode="promise_in_bounds", unique_indices=True)
    return head_grad, text_grad


def solution(mesh):
    devices = mesh.devices
    fine = Mesh(devices.reshape(2, devices.shape[0] // 2, 4, devices.shape[1] // 8, 2), ALL)
    return jax.shard_map(
        shards,
        mesh=fine,
        in_specs=(P(ALL, None), P(ALL, None), P(ALL), P(("x", "zh", "c"), None), P(), P(), P()),
        out_specs=(P(("x", "zh", "c"), None), P(ALL, None)),
        check_vma=False,
    )
```

time: 637 us -> 191 us (0.30)
  the two profiles are of different devices: /device:TPU:64 before, /device:TPU:2 now
where the time goes in v1:
time: 191 us; the launch traced here: 190 us
  blocking collectives  68 us (36%)
  waiting for transfers between devices  41.1 us (22%)
  starting transfers between devices  30.3 us (16%)
  matrix products  16.6 us (9%)
  between operations  16.3 us (9%)
  other arithmetic  9.14 us (5%)
  local copies, waits for them, and re-layouts  8.12 us (4%)
    all_gather x1, blocking collectives, shards(): lax.all_gather(head.astype(jnp.bfloat16), 'y', axis=0).astype(jnp.float32)  27.8 us
    ppermute x7, waiting for transfers between devices, hop(): return lax.ppermute(value, axis, ring(axis, steps))  25 us
    all_gather x1, blocking collectives, gather_weight(): slab = lax.all_gather(part, 'zh', axis=0, tiled=True)  20.5 us
    ppermute x7, starting transfers between devices, hop(): return lax.ppermute(value, axis, ring(axis, steps))  19 us
    all_to_all x2, waiting for transfers between devices, spread(): came = lax.all_to_all(parts, axis, 0, 0)  16.1 us
    all_to_all x2, starting transfers between devices, spread(): came = lax.all_to_all(parts, axis, 0, 0)  11.3 us
    all_gather x1, blocking collectives, shards(): text_pair = lax.all_gather(text_unit, 'zl', axis=0, tiled=True)  10.4 us
    all_gather x1, blocking collectives, shards(): lax.all_gather(head, 'zl', axis=0).astype(jnp.float32)  5.4 us
  transfers between devices with their start and end apart: 10, of which 6 were waited for; matrix products, arithmetic and copies ran while one was open for 5% of the time, Pallas kernels for 0%

profile of v1, /device:TPU:2, one launch (start us, length us, event | category | flops | bytes accessed | tf_op | source)
XLA Modules:
  0.0 189.7 jit_solution(3277579449682003990)
XLA Ops:
  7.2 0.0 copy-start
  7.2 0.0 copy-start.5
  7.2 0.0 all-gather.9.cloned.1.call-start
  7.2 0.7 compare_select_fusion
  8.0 0.3 copy-done
  8.3 1.6 gather_fusion
  9.9 0.0 all-gather.9.cloned.1.call-update
  9.9 0.0 copy-done.5
  9.9 1.9 %all-gather.4 = bf16[2,36,1152]{2,1,0:T(8,128)(2,1)S(1)} all-gather(bf16[1,36,1152]{2,1,0:T(8,128)(2,1)S(1)} %bitcast.46), channel_id=1, replica_groups=mesh['zl'=2,'y'=8,'x'=4,'zh'=4,'c'=2] {'c'}, dimensions={0}, use_global_device_ids=true | all-gather | bytes 248832 | tf_op jit(solution)/shard_map/all_gather | solution.py:23
  11.9 20.5 %all_gather.32 = bf16[288,640]{1,0:T(8,128)(2,1)S(1)} all-gather(bf16[72,640]{1,0:T(8,128)(2,1)S(1)} %constant_dynamic-slice_fusion), channel_id=1, replica_groups=mesh['zl'=2,'y'=8,'x'=4,'zh'=4,'c'=2] {'zh'}, dimensions={0}, use_global_device_ids=true | all-gather | bytes 460800 | tf_op jit(solution)/shard_map/all_gather | solution.py:26
  32.4 2.4 %collective-permute-start.1 = (bf16[288,640]{1,0:T(8,128)(2,1)S(1)}, bf16[288,640]{1,0:T(8,128)(2,1)S(1)}, u32[]{:S(2)}, u32[]{:S(2)}) collective-permute-start(bf16[288,640]{1,0:T(8,128)(2,1)S(1)} %all_gather.32), channel_id=1, source_target_pairs={{0,24},{8,0},{16,8},{24,16},{1,25},{9,1},{17,9},{25,17},{2,26},{10... | collective-permute-start | bytes 1105928 | tf_op jit(solution)/shard_map/ppermute | solution.py:17
  34.8 3.4 %collective-permute-start = (bf16[288,640]{1,0:T(8,128)(2,1)S(1)}, bf16[288,640]{1,0:T(8,128)(2,1)}, u32[]{:S(2)}, u32[]{:S(2)}) collective-permute-start(bf16[288,640]{1,0:T(8,128)(2,1)S(1)} %all_gather.32), channel_id=1, source_target_pairs={{0,8},{8,16},{16,24},{24,0},{1,9},{9,17},{17,25},{25,1},{2,10},{10... | collective-permute-start | bytes 1105928 | tf_op jit(solution)/shard_map/ppermute | solution.py:17
  38.3 0.1 broadcast_in_dim.40
  38.4 0.0 copy-start.1
  38.4 0.1 bitcast_dynamic-update-slice_fusion.2
  38.5 4.7 %collective-permute-done.1 = bf16[288,640]{1,0:T(8,128)(2,1)S(1)} collective-permute-done((bf16[288,640]{1,0:T(8,128)(2,1)S(1)}, bf16[288,640]{1,0:T(8,128)(2,1)S(1)}, u32[]{:S(2)}, u32[]{:S(2)}) %collective-permute-start.1) | collective-permute-done | bytes 368672 | tf_op jit(solution)/shard_map/ppermute | solution.py:17
  43.2 2.7 %collective-permute-start.2 = (bf16[144,640]{1,0:T(8,128)(2,1)S(1)}, bf16[144,640]{1,0:T(8,128)(2,1)S(1)}, u32[]{:S(2)}, u32[]{:S(2)}) collective-permute-start(bf16[144,640]{1,0:T(8,128)(2,1)S(1)} %slice.32), channel_id=1, source_target_pairs={{0,24},{8,0},{16,8},{24,16},{1,25},{9,1},{17,9},{25,17},{2,26},{10... | collective-permute-start | bytes 552968 | tf_op jit(solution)/shard_map/ppermute | solution.py:17
  45.9 0.6 collective-permute-done
  46.5 0.9 slice.33
  47.4 2.6 %collective-permute-start.3 = (bf16[144,640]{1,0:T(8,128)(2,1)S(1)}, bf16[144,640]{1,0:T(8,128)(2,1)S(1)}, u32[]{:S(2)}, u32[]{:S(2)}) collective-permute-start(bf16[144,640]{1,0:T(8,128)(2,1)S(1)} %slice.33), channel_id=1, source_target_pairs={{0,8},{8,16},{16,24},{24,0},{1,9},{9,17},{17,25},{25,1},{2,10},{10... | collective-permute-start | bytes 552968 | tf_op jit(solution)/shard_map/ppermute | solution.py:17
  50.0 1.0 bitcast_dynamic-update-slice_fusion.1
  51.1 0.1 bitcast_dynamic-update-slice_fusion
  51.1 0.0 collective-permute-done.2
  51.1 4.9 %collective-permute-done.3 = bf16[144,640]{1,0:T(8,128)(2,1)S(1)} collective-permute-done((bf16[144,640]{1,0:T(8,128)(2,1)S(1)}, bf16[144,640]{1,0:T(8,128)(2,1)S(1)}, u32[]{:S(2)}, u32[]{:S(2)}) %collective-permute-start.3) | collective-permute-done | bytes 184352 | tf_op jit(solution)/shard_map/ppermute | solution.py:17
  56.0 1.9 %collective-permute-start.4 = (bf16[1152,640]{1,0:T(8,128)(2,1)S(1)}, bf16[1152,640]{1,0:T(8,128)(2,1)}, u32[]{:S(2)}, u32[]{:S(2)}) collective-permute-start(bf16[1152,640]{1,0:T(8,128)(2,1)S(1)} %bitcast.41), channel_id=1, source_target_pairs={{0,1},{1,0},{2,3},{3,2},{4,5},{5,4},{6,7},{7,6},{8,9},{9,8},{10,11... | collective-permute-start | bytes 4423688 | tf_op jit(solution)/shard_map/ppermute | solution.py:17
  58.0 0.0 copy-done.1
  58.0 0.9 gather_fusion.1
  60.9 0.1 fusion.29
  61.0 0.1 fusion.30
  61.2 10.4 %all_gather.33 = bf16[256,1152]{1,0:T(8,128)(2,1)} all-gather(bf16[128,1152]{1,0:T(8,128)(2,1)S(1)} %fusion.30), channel_id=1, replica_groups=mesh['zl'=2,'y'=8,'x'=4,'zh'=4,'c'=2] {'zl'}, dimensions={0}, use_global_device_ids=true | all-gather | bytes 884736 | tf_op jit(solution)/shard_map/all_gather | solution.py:58
  71.6 0.0 collective-permute-done.4
  71.6 3.8 %fusion.4 = f32[1024,640]{0,1:T(8,128)S(1)} fusion(bf16[1024,1152]{1,0:T(8,128)(2,1)} %all-gather.9.cloned.1.call-done, bf16[1152,640]{1,0:T(8,128)(2,1)S(1)} %bitcast.42, bf16[1152,640]{1,0:T(8,128)(2,1)} %collective-permute-done.4, pred[]{:T(512)S(6)} %eq.30), kind=kOutput, calls=%fused_computation.16 | convolution fusion | flops 1510686720 | bytes 7929857 | tf_op jit(solution)/shard_map/dot_general | solution.py:61
  75.4 0.0 copy-done.6
  75.4 2.9 %fusion.15 = f32[1024,512]{0,1:T(8,128)S(1)} fusion(bf16[1024,1152]{1,0:T(8,128)(2,1)S(1)} %copy-done.6, bf16[1152,640]{1,0:T(8,128)(2,1)S(1)} %bitcast.43, bf16[1152,640]{1,0:T(8,128)(2,1)} %collective-permute-done.4, pred[]{:T(512)S(6)} %eq.30), kind=kOutput, calls=%fused_computation.31 | convolution fusion | flops 1208549376 | bytes 6815745 | tf_op jit(solution)/shard_map/dot_general | solution.py:62
  78.3 0.4 multiply_reduce_fusion
  78.7 0.7 divide_convert_fusion
  79.4 0.4 copy-done.4
  79.7 1.6 fusion.14
  81.4 0.0 copy-start.3
  81.4 0.9 fusion
  82.3 0.0 copy-done.3
  82.3 1.0 fusion.3
  83.3 1.7 convolution_convert_fusion
  85.1 2.4 %collective-permute-start.5 = (bf16[1152,576]{0,1:T(8,128)(2,1)S(1)}, bf16[1152,576]{0,1:T(8,128)(2,1)S(1)}, u32[]{:S(2)}, u32[]{:S(2)}) collective-permute-start(bf16[1152,576]{0,1:T(8,128)(2,1)S(1)} %convolution_convert_fusion), channel_id=1, source_target_pairs={{0,1},{1,0},{2,3},{3,2},{4,5},{5,4},{6,7},{7,6},{8,9},{9,8},{10,11... | collective-permute-start | bytes 3981320 | tf_op jit(solution)/shard_map/ppermute | solution.py:17
  87.4 2.6 %collective-permute-done.5 = bf16[1152,576]{0,1:T(8,128)(2,1)S(1)} collective-permute-done((bf16[1152,576]{0,1:T(8,128)(2,1)S(1)}, bf16[1152,576]{0,1:T(8,128)(2,1)S(1)}, u32[]{:S(2)}, u32[]{:S(2)}) %collective-permute-start.5) | collective-permute-done | bytes 1327136 | tf_op jit(solution)/shard_map/ppermute | solution.py:17
  90.0 2.8 %add_convert_fusion = bf16[1152,576]{0,1:T(8,128)(2,1)} fusion(bf16[1152,576]{0,1:T(8,128)(2,1)S(1)} %collective-permute-done.5, bf16[1024,1152]{1,0:T(8,128)(2,1)S(1)} %copy-done.6, pred[]{:T(512)S(6)} %eq.30, bf16[1024,1152]{0,1:T(8,128)(2,1)S(1)} %fusion.3), kind=kOutput, calls=%fused_computation.14 | convolution fusion | flops 1361534976 | bytes 7372801 | tf_op jit(solution)/shard_map/dot_general | solution.py:83
  92.8 2.6 %copy.15 = bf16[1152,576]{1,0:T(8,128)(2,1)} copy(bf16[1152,576]{0,1:T(8,128)(2,1)} %add_convert_fusion) | data formatting | bytes 2654208 | tf_op jit(solution)/shard_map/convert_element_type | solution.py:100
  95.4 7.5 %all-to-all-start = ((bf16[4,288,576]{2,1,0:T(8,128)(2,1)}), bf16[4,288,576]{2,1,0:T(8,128)(2,1)}, u32[]{:S(2)}, u32[]{:S(2)}) async-start(bf16[4,288,576]{2,1,0:T(8,128)(2,1)} %bitcast.40), calls=%async_computation | async-start | bytes 2949120 | tf_op jit(solution)/shard_map/all_to_all | solution.py:101
  102.9 3.0 %fusion.45 = f32[256,1152]{1,0:T(8,128)} fusion(bf16[1024,256]{1,0:T(8,128)(2,1)} %copy-done.3, bf16[1024,1152]{0,1:T(8,128)(2,1)S(1)} %divide_convert_fusion), kind=kOutput, calls=%fused_computation.82 | convolution fusion | flops 603979776 | bytes 4063232 | tf_op jit(solution)/shard_map/dot_general | solution.py:93
  105.8 16.1 %all-to-all-done = bf16[4,288,576]{2,1,0:T(8,128)(2,1)} async-done(((bf16[4,288,576]{2,1,0:T(8,128)(2,1)}), bf16[4,288,576]{2,1,0:T(8,128)(2,1)}, u32[]{:S(2)}, u32[]{:S(2)}) %all-to-all-start) | async-done | bytes 1327136 | tf_op jit(solution)/shard_map/all_to_all | solution.py:101
  121.9 2.5 %reduce_sum.84 = bf16[288,576]{1,0:T(8,128)(2,1)} reduce(bf16[4,288,576]{2,1,0:T(8,128)(2,1)} %all-to-all-done, bf16[]{:T(256)} %constant.77.clone.1), dimensions={0}, to_apply=%region_3.4 | reduce | flops 497664 | bytes 1658882 | tf_op jit(solution)/shard_map/reduce_sum | solution.py:102
  124.4 3.8 %all-to-all-start.1 = ((bf16[4,72,576]{2,1,0:T(8,128)(2,1)}), bf16[4,72,576]{2,1,0:T(8,128)(2,1)S(1)}, u32[]{:S(2)}, u32[]{:S(2)}) async-start(bf16[4,72,576]{2,1,0:T(8,128)(2,1)} %bitcast.10), calls=%async_computation.1 | async-start | bytes 737280 | tf_op jit(solution)/shard_map/all_to_all | solution.py:101
  128.2 0.0 copy-done.2
  128.3 3.6 %collective-permute-start.6 = (bf16[128,1152]{1,0:T(8,128)(2,1)S(1)}, bf16[128,1152]{1,0:T(8,128)(2,1)S(1)}, u32[]{:S(2)}, u32[]{:S(2)}) collective-permute-start(bf16[128,1152]{1,0:T(8,128)(2,1)S(1)} %dynamic-slice_convert_fusion), channel_id=1, source_target_pairs={{0,256},{256,0},{1,257},{257,1},{2,258},{258,2},{3,259},{259,3},{4... | collective-permute-start | bytes 884744 | tf_op jit(solution)/shard_map/ppermute | solution.py:17
  131.8 12.3 %collective-permute-done.6 = bf16[128,1152]{1,0:T(8,128)(2,1)S(1)} collective-permute-done((bf16[128,1152]{1,0:T(8,128)(2,1)S(1)}, bf16[128,1152]{1,0:T(8,128)(2,1)S(1)}, u32[]{:S(2)}, u32[]{:S(2)}) %collective-permute-start.6) | collective-permute-done | bytes 294944 | tf_op jit(solution)/shard_map/ppermute | solution.py:17
  144.2 0.2 fusion.31
  144.4 2.3 %scatter_custom_fusion = f32[256,1152]{1,0:T(8,128)} fusion(s32[128]{0:T(128)S(1)} %compare_select_fusion, f32[]{:T(128)} %constant.85.clone.1, bf16[128,1152]{1,0:T(8,128)(2,1)S(1)} %collective-permute-done.6, f32[256,1152]{1,0:T(8,128)S(1)} %copy-done.2, s32[]{:T(128)S(6)} %select_n.82, s32[]{:T(128)} %constant.63.clone.1, f32[128]{0:T(128)S(1)} %fusion.31, ...), kind=kCustom, calls=%fused_computation.52 | custom fusion | flops 1474560 | bytes 2360848 | tf_op jit(solution)/shard_map/scatter | solution.py:117
  146.7 0.0 all-to-all-done.1
  146.7 0.1 reduce_sum.85
  146.8 1.9 %all-gather.1 = bf16[144,576]{1,0:T(8,128)(2,1)S(1)} all-gather(bf16[72,576]{1,0:T(8,128)(2,1)S(1)} %reduce_sum.85), channel_id=3, replica_groups=mesh['zl'=2,'y'=8,'x'=4,'zh'=4,'c'=2] {'c'}, dimensions={0}, use_global_device_ids=true | all-gather | bytes 248832 | tf_op jit(solution)/shard_map/all_gather | solution.py:106
  148.8 0.1 maximum_bitcast_fusion.1
  148.8 5.4 %all-gather.5 = bf16[2,36,1152]{2,1,0:T(8,128)(2,1)S(1)} all-gather(bf16[1,36,1152]{2,1,0:T(8,128)(2,1)S(1)} %maximum_bitcast_fusion.1), channel_id=4, replica_groups=mesh['zl'=2,'y'=8,'x'=4,'zh'=4,'c'=2] {'zl'}, dimensions={0}, use_global_device_ids=true | all-gather | bytes 248832 | tf_op jit(solution)/shard_map/all_gather | solution.py:110
  154.3 27.8 %all-gather.6 = bf16[8,36,1152]{2,1,0:T(8,128)(2,1)S(1)} all-gather(bf16[1,36,1152]{2,1,0:T(8,128)(2,1)S(1)} %bitcast.45), channel_id=5, replica_groups=mesh['zl'=2,'y'=8,'x'=4,'zh'=4,'c'=2] {'y'}, dimensions={0}, use_global_device_ids=true | all-gather | bytes 746496 | tf_op jit(solution)/shard_map/all_gather | solution.py:111
  182.1 0.8 convert_reduce_fusion
  (17 shorter events, 0.3 us)
Async XLA Ops:
  7.2 1.1 copy-start
  7.2 2.7 %copy-start.5 = (bf16[36,1152]{1,0:T(8,128)(2,1)S(1)}, bf16[36,1152]{1,0:T(8,128)(2,1)}, u32[]{:S(2)}) copy-start(bf16[36,1152]{1,0:T(8,128)(2,1)} %param.10) | copy-start | bytes 248836
  7.2 64.4 %all-gather.9.cloned.1.call-start = ((), (), s32[]{:S(2)}) async-start(), calls=%async_computation.2 | async-start | bytes 2654208 | tf_op jit(solution)/shard_map/all_gather | solution.py:54
  32.4 10.8 %collective-permute-start.1 = (bf16[288,640]{1,0:T(8,128)(2,1)S(1)}, bf16[288,640]{1,0:T(8,128)(2,1)S(1)}, u32[]{:S(2)}, u32[]{:S(2)}) collective-permute-start(bf16[288,640]{1,0:T(8,128)(2,1)S(1)} %all_gather.32), channel_id=1, source_target_pairs={{0,24},{8,0},{16,8},{24,16},{1,25},{9,1},{17,9},{25,17},{2,26},{10... | collective-permute-start | bytes 1105928 | tf_op jit(solution)/shard_map/ppermute | solution.py:17
  34.8 11.6 %collective-permute-start = (bf16[288,640]{1,0:T(8,128)(2,1)S(1)}, bf16[288,640]{1,0:T(8,128)(2,1)}, u32[]{:S(2)}, u32[]{:S(2)}) collective-permute-start(bf16[288,640]{1,0:T(8,128)(2,1)S(1)} %all_gather.32), channel_id=1, source_target_pairs={{0,8},{8,16},{16,24},{24,0},{1,9},{9,17},{17,25},{25,1},{2,10},{10... | collective-permute-start | bytes 1105928 | tf_op jit(solution)/shard_map/ppermute | solution.py:17
  38.4 19.6 %copy-start.1 = (bf16[256,1152]{1,0:T(8,128)(2,1)S(1)}, bf16[256,1152]{1,0:T(8,128)(2,1)}, u32[]{:S(2)}) copy-start(bf16[256,1152]{1,0:T(8,128)(2,1)} %param.8) | copy-start | bytes 1769476
  43.2 7.9 %collective-permute-start.2 = (bf16[144,640]{1,0:T(8,128)(2,1)S(1)}, bf16[144,640]{1,0:T(8,128)(2,1)S(1)}, u32[]{:S(2)}, u32[]{:S(2)}) collective-permute-start(bf16[144,640]{1,0:T(8,128)(2,1)S(1)} %slice.32), channel_id=1, source_target_pairs={{0,24},{8,0},{16,8},{24,16},{1,25},{9,1},{17,9},{25,17},{2,26},{10... | collective-permute-start | bytes 552968 | tf_op jit(solution)/shard_map/ppermute | solution.py:17
  47.4 8.6 %collective-permute-start.3 = (bf16[144,640]{1,0:T(8,128)(2,1)S(1)}, bf16[144,640]{1,0:T(8,128)(2,1)S(1)}, u32[]{:S(2)}, u32[]{:S(2)}) collective-permute-start(bf16[144,640]{1,0:T(8,128)(2,1)S(1)} %slice.33), channel_id=1, source_target_pairs={{0,8},{8,16},{16,24},{24,0},{1,9},{9,17},{17,25},{25,1},{2,10},{10... | collective-permute-start | bytes 552968 | tf_op jit(solution)/shard_map/ppermute | solution.py:17
  56.0 15.6 %collective-permute-start.4 = (bf16[1152,640]{1,0:T(8,128)(2,1)S(1)}, bf16[1152,640]{1,0:T(8,128)(2,1)}, u32[]{:S(2)}, u32[]{:S(2)}) collective-permute-start(bf16[1152,640]{1,0:T(8,128)(2,1)S(1)} %bitcast.41), channel_id=1, source_target_pairs={{0,1},{1,0},{2,3},{3,2},{4,5},{5,4},{6,7},{7,6},{8,9},{9,8},{10,11... | collective-permute-start | bytes 4423688 | tf_op jit(solution)/shard_map/ppermute | solution.py:17
  71.6 3.8 %copy-start.6 = (bf16[1024,1152]{1,0:T(8,128)(2,1)S(1)}, bf16[1024,1152]{1,0:T(8,128)(2,1)}, u32[]{:S(2)}) copy-start(bf16[1024,1152]{1,0:T(8,128)(2,1)} %all-gather.9.cloned.1.call-done) | copy-start | bytes 7077892
  78.7 1.1 copy-start.4
  81.4 0.9 copy-start.3
  85.1 5.0 %collective-permute-start.5 = (bf16[1152,576]{0,1:T(8,128)(2,1)S(1)}, bf16[1152,576]{0,1:T(8,128)(2,1)S(1)}, u32[]{:S(2)}, u32[]{:S(2)}) collective-permute-start(bf16[1152,576]{0,1:T(8,128)(2,1)S(1)} %convolution_convert_fusion), channel_id=1, source_target_pairs={{0,1},{1,0},{2,3},{3,2},{4,5},{5,4},{6,7},{7,6},{8,9},{9,8},{10,11... | collective-permute-start | bytes 3981320 | tf_op jit(solution)/shard_map/ppermute | solution.py:17
  95.4 26.5 %all-to-all-start = ((bf16[4,288,576]{2,1,0:T(8,128)(2,1)}), bf16[4,288,576]{2,1,0:T(8,128)(2,1)}, u32[]{:S(2)}, u32[]{:S(2)}) async-start(bf16[4,288,576]{2,1,0:T(8,128)(2,1)} %bitcast.40), calls=%async_computation | async-start | bytes 2949120 | tf_op jit(solution)/shard_map/all_to_all | solution.py:101
  105.8 22.4 %copy-start.2 = (f32[256,1152]{1,0:T(8,128)S(1)}, f32[256,1152]{1,0:T(8,128)}, u32[]{:S(2)}) copy-start(f32[256,1152]{1,0:T(8,128)} %fusion.45) | copy-start | bytes 3538948
  124.4 22.3 %all-to-all-start.1 = ((bf16[4,72,576]{2,1,0:T(8,128)(2,1)}), bf16[4,72,576]{2,1,0:T(8,128)(2,1)S(1)}, u32[]{:S(2)}, u32[]{:S(2)}) async-start(bf16[4,72,576]{2,1,0:T(8,128)(2,1)} %bitcast.10), calls=%async_computation.1 | async-start | bytes 737280 | tf_op jit(solution)/shard_map/all_to_all | solution.py:101
  128.3 15.9 %collective-permute-start.6 = (bf16[128,1152]{1,0:T(8,128)(2,1)S(1)}, bf16[128,1152]{1,0:T(8,128)(2,1)S(1)}, u32[]{:S(2)}, u32[]{:S(2)}) collective-permute-start(bf16[128,1152]{1,0:T(8,128)(2,1)S(1)} %dynamic-slice_convert_fusion), channel_id=1, source_target_pairs={{0,256},{256,0},{1,257},{257,1},{2,258},{258,2},{3,259},{259,3},{4... | collective-permute-start | bytes 884744 | tf_op jit(solution)/shard_map/ppermute | solution.py:17
Sparse Core Ops, SparseCore 0:
  10.7 48.9 all-gather.8

commit v2 on v1

v2 whole, which is shorter than its diff:
```python
import functools

import jax
import jax.numpy as jnp
from jax import lax
from jax.experimental import pallas as pl
from jax.experimental.pallas import tpu as pltpu
from jax.sharding import Mesh, PartitionSpec as P

EPS = 1e-06
ALL = ("zl", "y", "x", "zh", "c")
WIDE = 640
CHUNK = 256
VMEM = pl.BlockSpec(memory_space=pltpu.VMEM)
SMEM = pl.BlockSpec(memory_space=pltpu.SMEM)
PARAMS = pltpu.CompilerParams(vmem_limit_bytes=48 * 1024 * 1024)


def hop(value, axis, steps):
    count = lax.axis_size(axis)
    return lax.ppermute(value, axis, [(s, (s + steps) % count) for s in range(count)])


def nn(a, b):
    return jnp.dot(a, b, preferred_element_type=jnp.float32)


def nt(a, b):
    return lax.dot_general(a, b, (((1,), (1,)), ((), ())), preferred_element_type=jnp.float32)


def project_kernel(core_ref, x_ref, *refs):
    pieces, (unit_ref, norm_ref, proj_ref) = refs[:10], refs[10:]
    width = unit_ref.shape[1]
    half = pieces[3].shape[0]
    sums = []
    for own, before, after, far_low, far_high in (pieces[:5], pieces[5:]):
        total = nn(x_ref[0], own[...]) + nn(x_ref[1], before[...]) + nn(x_ref[2], after[...])
        total += nn(x_ref[3, :, :half], far_low[...]) + nn(x_ref[3, :, half:], far_high[...])
        sums.append(total)
    mine, other = sums
    first = core_ref[0] == 0
    proj_ref[:, :WIDE] = jnp.where(first, mine, other)
    proj_ref[:, WIDE:] = jnp.where(first, other, mine)[:, 2 * WIDE - width:]
    proj = proj_ref[...]
    norm = jnp.sqrt(jnp.sum(proj * proj, axis=1, keepdims=True) + EPS)
    unit_ref[...] = (proj / norm).astype(jnp.bfloat16)
    norm_ref[...] = norm


def tile_kernel(scal_ref, spot_ref, unit_ref, norm_ref, text_ref, cols_ref, send_ref, back_ref, grad_ref, total_ref):
    temper, offset, factor = scal_ref[0], scal_ref[1], scal_ref[2]
    rows = unit_ref.shape[0]
    unit = unit_ref[...]
    pair = rows // 2
    row_id = lax.broadcasted_iota(jnp.int32, (rows, CHUNK), 0) - spot_ref[0]
    col_id = lax.broadcasted_iota(jnp.int32, (rows, CHUNK), 1) - spot_ref[1]
    inside = (row_id >= 0) & (row_id < pair)
    for k in range(text_ref.shape[0] // CHUNK):
        text = text_ref[k * CHUNK:(k + 1) * CHUNK, :]
        logits = temper * nt(unit, text) + offset
        same = inside & (col_id + k * CHUNK == row_id)
        sign = jnp.where(same, 1.0, -1.0)
        grad = (-factor * sign / (1.0 + jnp.exp(sign * logits))).astype(jnp.bfloat16)
        grad_ref[:, k * CHUNK:(k + 1) * CHUNK] = grad
        part = nn(grad, text)
        if k == 0:
            total_ref[...] = part
        else:
            total_ref[...] += part
    image_back = temper * total_ref[...]
    unit_float = unit.astype(jnp.float32)
    radial = jnp.sum(unit_float * image_back, axis=1, keepdims=True)
    back = ((image_back - unit_float * radial) / norm_ref[...]).astype(jnp.bfloat16)
    back_ref[...] = back
    send_ref[...] = nn(cols_ref[...], back).astype(jnp.bfloat16)


def gather_weight(head_weight, after_this):
    core = lax.axis_index("c")
    rows = lax.all_gather(head_weight, "c", axis=0, tiled=True)
    width = rows.shape[1]
    part = lax.dynamic_slice(rows, (0, core * (width - WIDE)), (rows.shape[0], WIDE))
    slab = lax.all_gather(part, "zh", axis=0, tiled=True)
    slab, after_this = lax.optimization_barrier((slab, after_this))
    before = hop(slab, "x", 1)
    after = hop(slab, "x", -1)
    half = slab.shape[0] // 2
    far_low = hop(after[:half], "x", -1)
    far_high = hop(before[half:], "x", 1)
    mine = (slab, before, after, far_low, far_high)
    other = tuple(hop(piece, "c", 1) for piece in mine)
    return mine + other, after_this


def shards(image_cand, text_cand, selection, head_weight, logit_temp, logit_offset, loss_scale):
    pairs = selection.shape[0]
    depth = image_cand.shape[1]
    width = head_weight.shape[1]
    n_y, n_x, n_z = lax.axis_size("y"), lax.axis_size("x"), lax.axis_size(("zh", "zl"))
    my_zl, my_y, my_x, core = (lax.axis_index(a) for a in ("zl", "y", "x", "c"))
    total = pairs * lax.axis_size(ALL)
    own_rows = head_weight.shape[0]

    texts = text_cand.at[selection].get(mode="promise_in_bounds").astype(jnp.float32)
    txt_norm = jnp.sqrt(jnp.sum(texts * texts, axis=1, keepdims=True) + EPS)
    text_unit = (texts / txt_norm).astype(jnp.bfloat16)
    text_all = lax.all_gather(text_unit, "y", axis=0, tiled=True)

    picked = image_cand.at[selection].get(mode="promise_in_bounds")
    pieces, picked = gather_weight(head_weight, picked)
    there = hop(picked, "zl", 1)
    images = jnp.concatenate([jnp.where(my_zl == 0, picked, there), jnp.where(my_zl == 0, there, picked)], axis=0)

    rows = images.shape[0]
    by_x = images.reshape(rows, n_x, depth // n_x).transpose(1, 0, 2)
    by_x = jnp.stack([by_x[lax.rem(my_x + s + n_x, n_x)] for s in (0, -1, 1, 2)])
    by_core = images.T.reshape(depth // (2 * own_rows), 2, own_rows, rows).transpose(1, 0, 2, 3)
    by_core = by_core.reshape(2, depth // 2, rows)
    cols_mine, cols_other = by_core[core], by_core[1 - core]

    image_unit, img_norm = pl.pallas_call(
        project_kernel,
        out_shape=(jax.ShapeDtypeStruct((rows, width), jnp.bfloat16), jax.ShapeDtypeStruct((rows, 1), jnp.float32)),
        in_specs=[SMEM] + [VMEM] * 11,
        out_specs=(VMEM, VMEM),
        scratch_shapes=[pltpu.VMEM((rows, width), jnp.float32)],
        compiler_params=PARAMS,
        cost_estimate=pl.CostEstimate(flops=2 * rows * depth * width, bytes_accessed=4_000_000, transcendentals=0),
    )(core[None], by_x, *pieces)

    temper = logit_temp[0]
    factor = loss_scale[0] / total
    scalars = jnp.stack([temper, logit_offset[0], factor])
    spot = jnp.stack([my_zl * pairs, my_y * pairs])
    send, proj_back, grad_tile = pl.pallas_call(
        tile_kernel,
        out_shape=(
            jax.ShapeDtypeStruct((depth // 2, width), jnp.bfloat16),
            jax.ShapeDtypeStruct((rows, width), jnp.bfloat16),
            jax.ShapeDtypeStruct((rows, n_y * pairs), jnp.bfloat16),
        ),
        in_specs=[SMEM, SMEM] + [VMEM] * 4,
        out_specs=(VMEM, VMEM, VMEM),
        scratch_shapes=[pltpu.VMEM((rows, width), jnp.float32)],
        compiler_params=PARAMS,
        cost_estimate=pl.CostEstimate(flops=5 * rows * n_y * pairs * width, bytes_accessed=4_000_000, transcendentals=0),
    )(scalars, spot, image_unit, img_norm, text_all, cols_other)

    got = hop(send, "c", 1)
    head = nn(cols_mine, proj_back) + got.astype(jnp.float32)

    text_part = lax.dot_general(grad_tile, image_unit, (((0,), (0,)), ((), ())), preferred_element_type=jnp.float32)
    text_part = (temper * text_part).astype(jnp.bfloat16).reshape(n_y, pairs, width)
    text_back = lax.psum_scatter(text_part, "y", scatter_dimension=0).astype(jnp.float32)

    def spread(values, axis):
        count = lax.axis_size(axis)
        parts = values.astype(jnp.bfloat16).reshape(count, values.shape[0] // count, values.shape[1])
        return jnp.sum(lax.all_to_all(parts, axis, 0, 0).astype(jnp.float32), axis=0)

    head = spread(head, "x")
    head = spread(head, ("zh", "zl"))
    copies = jnp.broadcast_to(head.astype(jnp.bfloat16)[None], (n_y,) + head.shape)
    head = jnp.sum(lax.all_to_all(copies, "y", 0, 0).astype(jnp.float32), axis=0)
    head_grad = lax.all_gather(head, "zl", axis=0, tiled=True)

    text_float = text_unit.astype(jnp.float32)
    text_radial = jnp.sum(text_float * text_back, axis=1, keepdims=True)
    text_rows = (text_back - text_float * text_radial) / txt_norm
    text_grad = jnp.zeros((text_cand.shape[0], width), jnp.float32).at[selection].set(
        text_rows, mode="promise_in_bounds", unique_indices=True)
    return head_grad, text_grad


def solution(mesh):
    devices = mesh.devices
    fine = Mesh(devices.reshape(2, devices.shape[0] // 2, 4, devices.shape[1] // 8, 2), ALL)
    return jax.shard_map(
        shards,
        mesh=fine,
        in_specs=(P(ALL, None), P(ALL, None), P(ALL), P(("x", "zh", "c"), None), P(), P(), P()),
        out_specs=(P(("x", "zh", "c"), None), P(ALL, None)),
        check_vma=False,
    )
```

time: 191 us -> 182 us (0.953)
  waiting for transfers between devices: 41.1 us -> 3.75 us
  blocking collectives: 68 us -> 91 us
  local copies, waits for them, and re-layouts: 8.12 us -> 23.5 us
  matrix products: 16.6 us -> 2.89 us
  Pallas kernels: 0 us -> 6.86 us
  starting transfers between devices: 30.3 us -> 28.1 us
    all_to_all x0 -> x3, blocking collectives: none -> 63.2 us  [the longest x2 42.6 us: spread(): lax.all_to_all(parts, axis, 0, 0).astype(jnp.float32)]
    all_gather x4 -> x1, blocking collectives: 45.6 us -> 5.43 us  [shards(): head_grad = lax.all_gather(head, 'zl', axis=0, tiled=True)]
    ppermute x7 -> x11, waiting for transfers between devices: 25 us -> 3.71 us  [hop(): lax.ppermute(value, axis, [(s, (s + steps) % count) for s in range(count)])]
    all_to_all x2 -> x0, waiting for transfers between devices: 16.1 us -> none  [spread(): came = lax.all_to_all(parts, axis, 0, 0)]
    dot_general x6 -> x1, matrix products: 13.7 us -> 0.56 us  [nn(): return jnp.dot(a, b, preferred_element_type=jnp.float32)]
    all_to_all x2 -> x0, starting transfers between devices: 11.3 us -> none  [spread(): came = lax.all_to_all(parts, axis, 0, 0)]
    ppermute x7 -> x11, starting transfers between devices: 19 us -> 28.1 us  [hop(): lax.ppermute(value, axis, [(s, (s + steps) % count) for s in range(count)])]
    pallas_call x0 -> x2, Pallas kernels: none -> 6.86 us  [the longest x1 4 us: shards(): pl.pallas_call(tile_kernel, out_shape=(jax.ShapeDtypeStruct((depth // 2,...]
  transfers between devices with their start and end apart: 10 -> 13, of which waited for: 6 -> 2; matrix products, arithmetic and copies ran while one was open for 5% -> 11% of each run, Pallas kernels for 0% -> 2%
where the time goes in v2:
time: 182 us; the launch traced here: 181 us
  blocking collectives  91 us (50%)
  starting transfers between devices  28.1 us (15%)
  local copies, waits for them, and re-layouts  23.5 us (13%)
  between operations  16.3 us (9%)
  other arithmetic  8.64 us (5%)
  Pallas kernels  6.86 us (4%)
  waiting for transfers between devices  3.75 us (2%)
  matrix products  2.89 us (2%)
    all_to_all x2, blocking collectives, spread(): lax.all_to_all(parts, axis, 0, 0).astype(jnp.float32)  42.6 us
    ppermute x11, starting transfers between devices, hop(): lax.ppermute(value, axis, [(s, (s + steps) % count) for s in range(count)])  28.1 us
    all_to_all x1, blocking collectives, shards(): lax.all_to_all(copies, 'y', 0, 0).astype(jnp.float32)  20.5 us
    all_gather x1, blocking collectives, gather_weight(): slab = lax.all_gather(part, 'zh', axis=0, tiled=True)  20.5 us
    unnamed x27, local copies, waits for them, and re-layouts  7.27 us
    another operation x5, local copies, waits for them, and re-layouts  5.83 us
    all_gather x1, blocking collectives, shards(): head_grad = lax.all_gather(head, 'zl', axis=0, tiled=True)  5.43 us
    pallas_call x1, Pallas kernels, shards(): pl.pallas_call(tile_kernel, out_shape=(jax.ShapeDtypeStruct((depth // 2,...  4 us
  transfers between devices with their start and end apart: 13, of which 2 were waited for; matrix products, arithmetic and copies ran while one was open for 11% of the time, Pallas kernels for 2%

profile of v2, /device:TPU:2, one launch (start us, length us, event | category | flops | bytes accessed | tf_op | source)
XLA Modules:
  0.0 181.2 jit_solution(16771011022017040610)
XLA Ops:
  7.2 0.0 copy-start
  7.2 0.0 all-gather.4.cloned.1.call-start
  7.2 0.7 compare_select_fusion
  7.9 0.3 copy-done
  8.3 0.9 gather_fusion.1
  9.2 0.1 fusion.2
  9.3 0.8 fusion.3
  10.2 0.0 all-gather.4.cloned.1.call-update
  10.2 0.0 reduce-scatter.2.cloned.1.call-start
  10.2 1.9 %all-gather = bf16[2,36,1152]{2,1,0:T(8,128)(2,1)S(1)} all-gather(bf16[1,36,1152]{2,1,0:T(8,128)(2,1)S(1)} %bitcast.45), channel_id=1, replica_groups=mesh['zl'=2,'y'=8,'x'=4,'zh'=4,'c'=2] {'c'}, dimensions={0}, use_global_device_ids=true | all-gather | bytes 248832 | tf_op jit(solution)/shard_map/all_gather | solution.py:81
  12.2 0.9 gather_fusion
  13.2 20.5 %all_gather.13.refs_0_ = bf16[288,640]{1,0:T(8,128)(2,1)S(1)} all-gather(bf16[72,640]{1,0:T(8,128)(2,1)S(1)} %constant_dynamic-slice_fusion.6), channel_id=1, replica_groups=mesh['zl'=2,'y'=8,'x'=4,'zh'=4,'c'=2] {'zh'}, dimensions={0}, use_global_device_ids=true | all-gather | bytes 460800 | tf_op jit(solution)/shard_map/all_gather | solution.py:84
  33.7 3.6 %collective-permute-start = (bf16[128,1152]{1,0:T(8,128)(2,1)S(1)}, bf16[128,1152]{1,0:T(8,128)(2,1)S(1)}, u32[]{:S(2)}, u32[]{:S(2)}) collective-permute-start(bf16[128,1152]{1,0:T(8,128)(2,1)S(1)} %gather_fusion), channel_id=1, source_target_pairs={{0,256},{256,0},{1,257},{257,1},{2,258},{258,2},{3,259},{259,3},{4... | collective-permute-start | bytes 884744 | tf_op jit(solution)/shard_map/ppermute | solution.py:21
  37.3 2.4 %collective-permute-start.2 = (bf16[288,640]{1,0:T(8,128)(2,1)S(1)}, bf16[288,640]{1,0:T(8,128)(2,1)S(1)}, u32[]{:S(2)}, u32[]{:S(2)}) collective-permute-start(bf16[288,640]{1,0:T(8,128)(2,1)S(1)} %all_gather.13.refs_0_), channel_id=1, source_target_pairs={{0,24},{8,0},{16,8},{24,16},{1,25},{9,1},{17,9},{25,17},{2,26},{10... | collective-permute-start | bytes 1105928 | tf_op jit(solution)/shard_map/ppermute | solution.py:21
  39.8 3.4 %collective-permute-start.1 = (bf16[288,640]{1,0:T(8,128)(2,1)S(1)}, bf16[288,640]{1,0:T(8,128)(2,1)S(1)}, u32[]{:S(2)}, u32[]{:S(2)}) collective-permute-start(bf16[288,640]{1,0:T(8,128)(2,1)S(1)} %all_gather.13.refs_0_), channel_id=1, source_target_pairs={{0,8},{8,16},{16,24},{24,0},{1,9},{9,17},{17,25},{25,1},{2,10},{10... | collective-permute-start | bytes 1105928 | tf_op jit(solution)/shard_map/ppermute | solution.py:21
  43.2 1.9 %collective-permute-start.5 = (bf16[288,640]{1,0:T(8,128)(2,1)S(1)}, bf16[288,640]{1,0:T(8,128)(2,1)S(1)}, u32[]{:S(2)}, u32[]{:S(2)}) collective-permute-start(bf16[288,640]{1,0:T(8,128)(2,1)S(1)} %all_gather.13.refs_0_), channel_id=1, source_target_pairs={{0,1},{1,0},{2,3},{3,2},{4,5},{5,4},{6,7},{7,6},{8,9},{9,8},{10,11... | collective-permute-start | bytes 1105928 | tf_op jit(solution)/shard_map/ppermute | solution.py:21
  47.1 0.1 pad_add_fusion.spot_ref
  47.2 0.1 pad_maximum_fusion.2.scal_ref
  47.2 0.1 broadcast_select_fusion.1
  47.3 0.7 collective-permute-done.2.refs_2_
  48.0 0.7 slice.12
  48.7 2.7 %collective-permute-start.3 = (bf16[144,640]{1,0:T(8,128)(2,1)}, bf16[144,640]{1,0:T(8,128)(2,1)S(1)}, u32[]{:S(2)}, u32[]{:S(2)}) collective-permute-start(bf16[144,640]{1,0:T(8,128)(2,1)} %slice.12), channel_id=1, source_target_pairs={{0,24},{8,0},{16,8},{24,16},{1,25},{9,1},{17,9},{25,17},{2,26},{10... | collective-permute-start | bytes 552968 | tf_op jit(solution)/shard_map/ppermute | solution.py:21
  51.4 0.7 slice.13
  52.1 3.1 %collective-permute-start.4 = (bf16[144,640]{1,0:T(8,128)(2,1)}, bf16[144,640]{1,0:T(8,128)(2,1)S(1)}, u32[]{:S(2)}, u32[]{:S(2)}) collective-permute-start(bf16[144,640]{1,0:T(8,128)(2,1)} %slice.13), channel_id=1, source_target_pairs={{0,8},{8,16},{16,24},{24,0},{1,9},{9,17},{17,25},{25,1},{2,10},{10... | collective-permute-start | bytes 552968 | tf_op jit(solution)/shard_map/ppermute | solution.py:21
  55.2 0.9 fusion.14
  56.1 2.1 %copy.52 = bf16[256,1152]{0,1:T(8,128)(2,1)} copy(bf16[256,1152]{1,0:T(8,128)(2,1)} %get-tuple-element.19) | data formatting | bytes 1179648 | tf_op jit(solution)/shard_map/concatenate | solution.py:113
  58.2 1.1 copy.50
  59.3 1.2 reshape.39
  60.5 0.5 copy.51
  61.0 2.1 %collective-permute-start.6 = (bf16[288,640]{1,0:T(8,128)(2,1)S(1)}, bf16[288,640]{1,0:T(8,128)(2,1)S(1)}, u32[]{:S(2)}, u32[]{:S(2)}) collective-permute-start(bf16[288,640]{1,0:T(8,128)(2,1)S(1)} %collective-permute-done.1.refs_1_), channel_id=1, source_target_pairs={{0,1},{1,0},{2,3},{3,2},{4,5},{5,4},{6,7},{7,6},{8,9},{9,8},{10,11... | collective-permute-start | bytes 1105928 | tf_op jit(solution)/shard_map/ppermute | solution.py:21
  63.0 2.4 %collective-permute-start.7 = (bf16[288,640]{1,0:T(8,128)(2,1)S(1)}, bf16[288,640]{1,0:T(8,128)(2,1)S(1)}, u32[]{:S(2)}, u32[]{:S(2)}) collective-permute-start(bf16[288,640]{1,0:T(8,128)(2,1)S(1)} %collective-permute-done.2.refs_2_), channel_id=1, source_target_pairs={{0,1},{1,0},{2,3},{3,2},{4,5},{5,4},{6,7},{7,6},{8,9},{9,8},{10,11... | collective-permute-start | bytes 1105928 | tf_op jit(solution)/shard_map/ppermute | solution.py:21
  65.4 2.2 %constant_dynamic-slice_fusion.5 = (bf16[1,576,256]{2,0,1:T(2,128)(2,1)}, bf16[1,576,256]{2,0,1:T(2,128)(2,1)}) fusion(bf16[2,576,256]{2,0,1:T(2,128)(2,1)S(1)} %bitcast.36, s32[]{:T(128)S(6)} %select_n.43, s32[]{:T(128)S(6)} %select_n.48), kind=kLoop, calls=%fused_computation.36 | loop fusion | bytes 1179656 | tf_op jit(solution)/shard_map/dynamic_slice | solution.py:120
  67.7 1.9 %collective-permute-start.8 = (bf16[144,640]{1,0:T(8,128)(2,1)S(1)}, bf16[144,640]{1,0:T(8,128)(2,1)}, u32[]{:S(2)}, u32[]{:S(2)}) collective-permute-start(bf16[144,640]{1,0:T(8,128)(2,1)S(1)} %collective-permute-done.3.refs_3_), channel_id=1, source_target_pairs={{0,1},{1,0},{2,3},{3,2},{4,5},{5,4},{6,7},{7,6},{8,9},{9,8},{10,11... | collective-permute-start | bytes 552968 | tf_op jit(solution)/shard_map/ppermute | solution.py:21
  69.6 2.4 %collective-permute-start.9 = (bf16[144,640]{1,0:T(8,128)(2,1)S(1)}, bf16[144,640]{1,0:T(8,128)(2,1)}, u32[]{:S(2)}, u32[]{:S(2)}) collective-permute-start(bf16[144,640]{1,0:T(8,128)(2,1)S(1)} %collective-permute-done.4.refs_4_), channel_id=1, source_target_pairs={{0,1},{1,0},{2,3},{3,2},{4,5},{5,4},{6,7},{7,6},{8,9},{9,8},{10,11... | collective-permute-start | bytes 552968 | tf_op jit(solution)/shard_map/ppermute | solution.py:21
  72.0 0.8 constant_dynamic-slice_fusion.4
  72.8 1.7 copy.55
  74.5 1.7 copy.56
  76.2 0.8 copy.53
  77.1 0.8 copy.54
  77.9 1.1 copy.66
  79.0 1.4 pad_maximum_fusion.x_ref
  80.4 2.9 %shard_map.86 = (bf16[256,1152]{1,0:T(8,128)(2,1)S(1)}, f32[256,1]{1,0:T(8,128)S(1)}) custom-call(s32[1]{0:T(128)} %bitcast.6.core_ref, bf16[4,256,288]{2,1,0:T(8,128)(2,1)S(1)} %pad_maximum_fusion.x_ref, bf16[288,640]{1,0:T(8,128)(2,1)S(1)} %all_gather.13.refs_0_, bf16[288,640]{1,0:T(8,128)(2,1)S(1)} %collective-permute-done.1.refs_1_, ...), custom_call_target="tpu_custom_call" | custom-call | flops 679477248 | bytes 4000000 | tf_op jit(solution)/shard_map/pallas_call | solution.py:122
  83.3 0.8 copy-done.2
  84.1 0.7 copy-done.4
  84.8 1.7 copy-done.1
  86.4 1.1 copy-done.3
  87.5 0.9 copy-done.5
  88.4 4.0 %shard_map.87 = (bf16[576,1152]{1,0:T(8,128)(2,1)S(1)}, bf16[256,1152]{1,0:T(8,128)(2,1)S(1)}, bf16[256,1024]{1,0:T(8,128)(2,1)S(1)}) custom-call(f32[3]{0:T(128)S(1)} %pad_maximum_fusion.2.scal_ref, s32[2]{0:T(128)S(1)} %pad_add_fusion.spot_ref, bf16[256,1152]{1,0:T(8,128)(2,1)S(1)} %copy-done.3, f32[256,1]{1,0:T(8,128)S(1)} %copy-done.5, ...), custom_call_target="tpu_custom_call" | custom-call | flops 1509949440 | bytes 4000000 | tf_op jit(solution)/shard_map/pallas_call | solution.py:136
  92.4 2.3 %fusion = bf16[1024,1152]{1,0:T(8,128)(2,1)} fusion(bf16[256,1024]{1,0:T(8,128)(2,1)S(1)} %get-tuple-element.15, bf16[256,1152]{1,0:T(8,128)(2,1)S(1)} %copy-done.3, f32[]{:T(128)} %bitcast.33), kind=kOutput, calls=%fused_computation.4 | convolution fusion | flops 606339072 | bytes 3473412 | tf_op jit(solution)/shard_map/dot_general | solution.py:153
  94.7 0.0 reduce-scatter.2.cloned.1.call-update
  94.8 2.1 %collective-permute-start.10 = (bf16[576,1152]{1,0:T(8,128)(2,1)S(1)}, bf16[576,1152]{1,0:T(8,128)(2,1)S(1)}, u32[]{:S(2)}, u32[]{:S(2)}) collective-permute-start(bf16[576,1152]{1,0:T(8,128)(2,1)S(1)} %get-tuple-element.14), channel_id=1, source_target_pairs={{0,1},{1,0},{2,3},{3,2},{4,5},{5,4},{6,7},{7,6},{8,9},{9,8},{10,11... | collective-permute-start | bytes 3981320 | tf_op jit(solution)/shard_map/ppermute | solution.py:21
  96.8 3.0 %collective-permute-done.10 = bf16[576,1152]{1,0:T(8,128)(2,1)S(1)} collective-permute-done((bf16[576,1152]{1,0:T(8,128)(2,1)S(1)}, bf16[576,1152]{1,0:T(8,128)(2,1)S(1)}, u32[]{:S(2)}, u32[]{:S(2)}) %collective-permute-start.10) | collective-permute-done | bytes 1327136 | tf_op jit(solution)/shard_map/ppermute | solution.py:21
  99.9 0.6 fusion.1
  100.4 23.7 %all_to_all.15 = bf16[4,144,1152]{2,1,0:T(8,128)(2,1)S(1)} all-to-all(bf16[4,144,1152]{2,1,0:T(8,128)(2,1)S(1)} %bitcast.35), channel_id=1, replica_groups=mesh['zl'=2,'y'=8,'x'=4,'zh'=4,'c'=2] {'x'}, dimensions={0} | all-to-all | bytes 2654208 | tf_op jit(solution)/shard_map/all_to_all | solution.py:160
  124.1 0.2 reduce_sum.52
  124.4 0.1 reshape.43
  124.5 18.9 %all_to_all.16 = bf16[8,18,1152]{2,1,0:T(8,128)(2,1)S(1)} all-to-all(bf16[8,18,1152]{2,1,0:T(8,128)(2,1)S(1)} %reshape.43), channel_id=1, replica_groups=mesh['zl'=2,'y'=8,'x'=4,'zh'=4,'c'=2] {'zh','zl'}, dimensions={0} | all-to-all | bytes 663552 | tf_op jit(solution)/shard_map/all_to_all | solution.py:160
  143.4 0.1 reduce_sum.53
  143.5 20.5 %all_to_all.17 = bf16[8,18,1152]{2,1,0:T(8,128)(2,1)S(1)} all-to-all(bf16[8,18,1152]{2,1,0:T(8,128)(2,1)S(1)} %broadcast_in_dim.10), channel_id=1, replica_groups=mesh['zl'=2,'y'=8,'x'=4,'zh'=4,'c'=2] {'y'}, dimensions={0} | all-to-all | bytes 663552 | tf_op jit(solution)/shard_map/all_to_all | solution.py:165
  164.1 0.2 convert_reduce_fusion
  164.3 5.4 %all-gather.1 = f32[2,18,1152]{2,1,0:T(8,128)S(1)} all-gather(f32[1,18,1152]{2,1,0:T(8,128)S(1)} %bitcast.44), channel_id=1, replica_groups=mesh['zl'=2,'y'=8,'x'=4,'zh'=4,'c'=2] {'zl'}, dimensions={0}, use_global_device_ids=true | all-gather | bytes 248832 | tf_op jit(solution)/shard_map/all_gather | solution.py:166
  169.7 0.7 reshape.76
  170.4 1.2 fusion.4
  171.6 2.7 %scatter_custom_fusion = f32[256,1152]{1,0:T(8,128)} fusion(s32[128]{0:T(128)S(1)} %compare_select_fusion, f32[]{:T(128)} %constant.59.clone.1, bf16[1,128,1152]{2,1,0:T(8,128)(2,1)} %reduce-scatter.2.cloned.1.call-done, f32[128]{0:T(128)S(1)} %fusion.4, f32[128]{0:T(128)S(1)} %add_sqrt_fusion, bf16[128,1152]{1,0:T(8,128)(2,1)S(1)} %copy-done.8), kind=kCustom, calls=%fused_computation.18 | custom fusion | flops 1179648 | bytes 1771012 | tf_op jit(solution)/shard_map/scatter | solution.py:171
  (33 shorter events, 0.2 us)
Async XLA Ops:
  7.2 1.1 copy-start
  7.2 77.6 %all-gather.4.cloned.1.call-start = ((), (), s32[]{:S(2)}) async-start(), calls=%async_computation.4 | async-start | bytes 2654208 | tf_op jit(solution)/shard_map/all_gather | solution.py:108
  8.3 2.0 %copy-start.11 = (bf16[36,1152]{1,0:T(8,128)(2,1)S(1)}, bf16[36,1152]{1,0:T(8,128)(2,1)}, u32[]{:S(2)}) copy-start(bf16[36,1152]{1,0:T(8,128)(2,1)} %param.10) | copy-start | bytes 248836
  9.2 4.0 %copy-start.7 = (bf16[128,1152]{1,0:T(8,128)(2,1)}, bf16[128,1152]{1,0:T(8,128)(2,1)S(1)}, u32[]{:S(2)}) copy-start(bf16[128,1152]{1,0:T(8,128)(2,1)S(1)} %gather_fusion.1) | copy-start | bytes 884740
  9.2 3.1 %copy-start.6 = (bf16[256,1152]{1,0:T(8,128)(2,1)S(1)}, bf16[256,1152]{1,0:T(8,128)(2,1)}, u32[]{:S(2)}) copy-start(bf16[256,1152]{1,0:T(8,128)(2,1)} %param.7) | copy-start | bytes 1769476
  10.2 160.2 %reduce-scatter.2.cloned.1.call-start = ((), (), s32[]{:S(2)}) async-start(), calls=%async_computation.5 | async-start | bytes 2654208 | tf_op jit(solution)/shard_map/reduce_scatter | solution.py:155
  33.7 13.6 %collective-permute-start = (bf16[128,1152]{1,0:T(8,128)(2,1)S(1)}, bf16[128,1152]{1,0:T(8,128)(2,1)S(1)}, u32[]{:S(2)}, u32[]{:S(2)}) collective-permute-start(bf16[128,1152]{1,0:T(8,128)(2,1)S(1)} %gather_fusion), channel_id=1, source_target_pairs={{0,256},{256,0},{1,257},{257,1},{2,258},{258,2},{3,259},{259,3},{4... | collective-permute-start | bytes 884744 | tf_op jit(solution)/shard_map/ppermute | solution.py:21
  37.3 10.7 %collective-permute-start.2 = (bf16[288,640]{1,0:T(8,128)(2,1)S(1)}, bf16[288,640]{1,0:T(8,128)(2,1)S(1)}, u32[]{:S(2)}, u32[]{:S(2)}) collective-permute-start(bf16[288,640]{1,0:T(8,128)(2,1)S(1)} %all_gather.13.refs_0_), channel_id=1, source_target_pairs={{0,24},{8,0},{16,8},{24,16},{1,25},{9,1},{17,9},{25,17},{2,26},{10... | collective-permute-start | bytes 1105928 | tf_op jit(solution)/shard_map/ppermute | solution.py:21
  39.8 11.6 %collective-permute-start.1 = (bf16[288,640]{1,0:T(8,128)(2,1)S(1)}, bf16[288,640]{1,0:T(8,128)(2,1)S(1)}, u32[]{:S(2)}, u32[]{:S(2)}) collective-permute-start(bf16[288,640]{1,0:T(8,128)(2,1)S(1)} %all_gather.13.refs_0_), channel_id=1, source_target_pairs={{0,8},{8,16},{16,24},{24,0},{1,9},{9,17},{17,25},{25,1},{2,10},{10... | collective-permute-start | bytes 1105928 | tf_op jit(solution)/shard_map/ppermute | solution.py:21
  43.2 37.2 %collective-permute-start.5 = (bf16[288,640]{1,0:T(8,128)(2,1)S(1)}, bf16[288,640]{1,0:T(8,128)(2,1)S(1)}, u32[]{:S(2)}, u32[]{:S(2)}) collective-permute-start(bf16[288,640]{1,0:T(8,128)(2,1)S(1)} %all_gather.13.refs_0_), channel_id=1, source_target_pairs={{0,1},{1,0},{2,3},{3,2},{4,5},{5,4},{6,7},{7,6},{8,9},{9,8},{10,11... | collective-permute-start | bytes 1105928 | tf_op jit(solution)/shard_map/ppermute | solution.py:21
  48.7 19.0 %collective-permute-start.3 = (bf16[144,640]{1,0:T(8,128)(2,1)}, bf16[144,640]{1,0:T(8,128)(2,1)S(1)}, u32[]{:S(2)}, u32[]{:S(2)}) collective-permute-start(bf16[144,640]{1,0:T(8,128)(2,1)} %slice.12), channel_id=1, source_target_pairs={{0,24},{8,0},{16,8},{24,16},{1,25},{9,1},{17,9},{25,17},{2,26},{10... | collective-permute-start | bytes 552968 | tf_op jit(solution)/shard_map/ppermute | solution.py:21
  52.1 17.5 %collective-permute-start.4 = (bf16[144,640]{1,0:T(8,128)(2,1)}, bf16[144,640]{1,0:T(8,128)(2,1)S(1)}, u32[]{:S(2)}, u32[]{:S(2)}) collective-permute-start(bf16[144,640]{1,0:T(8,128)(2,1)} %slice.13), channel_id=1, source_target_pairs={{0,8},{8,16},{16,24},{24,0},{1,9},{9,17},{17,25},{25,1},{2,10},{10... | collective-permute-start | bytes 552968 | tf_op jit(solution)/shard_map/ppermute | solution.py:21
  60.9 11.1 %copy-start.9 = (bf16[256,1152]{0,1:T(8,128)(2,1)S(1)}, bf16[256,1152]{0,1:T(8,128)(2,1)}, u32[]{:S(2)}) copy-start(bf16[256,1152]{0,1:T(8,128)(2,1)} %copy.52) | copy-start | bytes 1769476
  61.0 19.5 %collective-permute-start.6 = (bf16[288,640]{1,0:T(8,128)(2,1)S(1)}, bf16[288,640]{1,0:T(8,128)(2,1)S(1)}, u32[]{:S(2)}, u32[]{:S(2)}) collective-permute-start(bf16[288,640]{1,0:T(8,128)(2,1)S(1)} %collective-permute-done.1.refs_1_), channel_id=1, source_target_pairs={{0,1},{1,0},{2,3},{3,2},{4,5},{5,4},{6,7},{7,6},{8,9},{9,8},{10,11... | collective-permute-start | bytes 1105928 | tf_op jit(solution)/shard_map/ppermute | solution.py:21
  63.0 17.4 %collective-permute-start.7 = (bf16[288,640]{1,0:T(8,128)(2,1)S(1)}, bf16[288,640]{1,0:T(8,128)(2,1)S(1)}, u32[]{:S(2)}, u32[]{:S(2)}) collective-permute-start(bf16[288,640]{1,0:T(8,128)(2,1)S(1)} %collective-permute-done.2.refs_2_), channel_id=1, source_target_pairs={{0,1},{1,0},{2,3},{3,2},{4,5},{5,4},{6,7},{7,6},{8,9},{9,8},{10,11... | collective-permute-start | bytes 1105928 | tf_op jit(solution)/shard_map/ppermute | solution.py:21
  67.7 12.7 %collective-permute-start.8 = (bf16[144,640]{1,0:T(8,128)(2,1)S(1)}, bf16[144,640]{1,0:T(8,128)(2,1)}, u32[]{:S(2)}, u32[]{:S(2)}) collective-permute-start(bf16[144,640]{1,0:T(8,128)(2,1)S(1)} %collective-permute-done.3.refs_3_), channel_id=1, source_target_pairs={{0,1},{1,0},{2,3},{3,2},{4,5},{5,4},{6,7},{7,6},{8,9},{9,8},{10,11... | collective-permute-start | bytes 552968 | tf_op jit(solution)/shard_map/ppermute | solution.py:21
  69.6 10.8 %collective-permute-start.9 = (bf16[144,640]{1,0:T(8,128)(2,1)S(1)}, bf16[144,640]{1,0:T(8,128)(2,1)}, u32[]{:S(2)}, u32[]{:S(2)}) collective-permute-start(bf16[144,640]{1,0:T(8,128)(2,1)S(1)} %collective-permute-done.4.refs_4_), channel_id=1, source_target_pairs={{0,1},{1,0},{2,3},{3,2},{4,5},{5,4},{6,7},{7,6},{8,9},{9,8},{10,11... | collective-permute-start | bytes 552968 | tf_op jit(solution)/shard_map/ppermute | solution.py:21
  83.3 0.8 copy-start.2
  84.1 0.7 copy-start.4
  84.8 1.7 copy-start.1
  86.4 1.1 copy-start.3
  87.5 0.9 copy-start.5
  94.7 5.1 %copy-start.10 = (bf16[1,576,256]{2,0,1:T(2,128)(2,1)S(1)}, bf16[1,576,256]{2,0,1:T(2,128)(2,1)}, u32[]{:S(2)}) copy-start(bf16[1,576,256]{2,0,1:T(2,128)(2,1)} %get-tuple-element.16) | copy-start | bytes 884740
  94.8 5.1 %collective-permute-start.10 = (bf16[576,1152]{1,0:T(8,128)(2,1)S(1)}, bf16[576,1152]{1,0:T(8,128)(2,1)S(1)}, u32[]{:S(2)}, u32[]{:S(2)}) collective-permute-start(bf16[576,1152]{1,0:T(8,128)(2,1)S(1)} %get-tuple-element.14), channel_id=1, source_target_pairs={{0,1},{1,0},{2,3},{3,2},{4,5},{5,4},{6,7},{7,6},{8,9},{9,8},{10,11... | collective-permute-start | bytes 3981320 | tf_op jit(solution)/shard_map/ppermute | solution.py:21
  143.5 26.9 %copy-start.8 = (bf16[128,1152]{1,0:T(8,128)(2,1)S(1)}, bf16[128,1152]{1,0:T(8,128)(2,1)}, u32[]{:S(2)}) copy-start(bf16[128,1152]{1,0:T(8,128)(2,1)} %copy-done.7) | copy-start | bytes 884740
Sparse Core Ops, SparseCore 0:
  10.3 48.9 all-gather.3
  94.9 46.0 reduce-scatter.1

commit v3 on v2

v3 whole, which is shorter than its diff:
```python
import jax
import jax.numpy as jnp
from jax import lax
from jax.experimental import pallas as pl
from jax.experimental.pallas import tpu as pltpu
from jax.sharding import Mesh, PartitionSpec as P

EPS = 1e-06
ALL = ("zl", "y", "x", "zh", "c")
WIDE = 640
CHUNK = 256
VMEM = pl.BlockSpec(memory_space=pltpu.VMEM)
SMEM = pl.BlockSpec(memory_space=pltpu.SMEM)
ANY = pl.BlockSpec(memory_space=pl.ANY)
PARAMS = pltpu.CompilerParams(vmem_limit_bytes=40 * 1024 * 1024)
F32, BF16 = jnp.float32, jnp.bfloat16


def hop(value, axis, steps):
    count = lax.axis_size(axis)
    return lax.ppermute(value, axis, [(s, (s + steps) % count) for s in range(count)])


def nn(a, b):
    return jnp.dot(a, b, preferred_element_type=F32)


def nt(a, b):
    return lax.dot_general(a, b, (((1,), (1,)), ((), ())), preferred_element_type=F32)


def tn(a, b):
    return lax.dot_general(a, b, (((0,), (0,)), ((), ())), preferred_element_type=F32)


def pick_rows(chosen_ref, cand_ref):
    pairs, cands = chosen_ref.shape[0], cand_ref.shape[0]
    spots = lax.broadcasted_iota(jnp.int32, (pairs, cands), 1)
    return nn((spots == chosen_ref[...]).astype(BF16), cand_ref[...])


def text_kernel(chosen_ref, cand_ref, unit_ref, norm_ref):
    texts = pick_rows(chosen_ref, cand_ref)
    norm = jnp.sqrt(jnp.sum(texts * texts, axis=1, keepdims=True) + EPS)
    unit_ref[...] = (texts / norm).astype(BF16)
    norm_ref[...] = norm


def image_kernel(chosen_ref, cand_ref, out_ref):
    out_ref[...] = pick_rows(chosen_ref, cand_ref).astype(BF16)


def pair_kernel(blocks, spot_ref, mine_ref, there_ref, images_ref, cols_mine_ref, cols_other_ref, flat_ref, group_ref):
    pairs, depth = mine_ref.shape
    first = spot_ref[0] == 0
    images_ref[:pairs, :] = jnp.where(first, mine_ref[...], there_ref[...])
    images_ref[pairs:, :] = jnp.where(first, there_ref[...], mine_ref[...])
    flat_ref[...] = images_ref[...].astype(F32).T
    size = depth // blocks
    for block in range(blocks):
        place = block // 2 * size
        group_ref[block % 2, place:place + size, :] = flat_ref[block * size:(block + 1) * size, :]
    core = spot_ref[2]
    cols_mine_ref[...] = group_ref[core].astype(BF16)
    cols_other_ref[...] = group_ref[1 - core].astype(BF16)


def main_kernel(scal_ref, spot_ref, images_ref, mine_ref, other_ref, cols_ref, text_hbm, send_ref, back_ref, part_hbm,
                text_ref, part_ref, proj_ref, total_ref, in_sem, out_sem):
    load = pltpu.make_async_copy(text_hbm, text_ref, in_sem)
    load.start()
    temper, offset, factor = scal_ref[0], scal_ref[1], scal_ref[2]
    rows, width = proj_ref.shape
    first = spot_ref[2] == 0
    proj_mine, proj_other = nn(images_ref[...], mine_ref[...]), nn(images_ref[...], other_ref[...])
    proj_ref[:, :WIDE] = jnp.where(first, proj_mine, proj_other)
    proj_ref[:, WIDE:] = jnp.where(first, proj_other, proj_mine)[:, 2 * WIDE - width:]
    proj = proj_ref[...]
    norm = jnp.sqrt(jnp.sum(proj * proj, axis=1, keepdims=True) + EPS)
    unit = (proj / norm).astype(BF16)
    pair = rows // 2
    row_id = lax.broadcasted_iota(jnp.int32, (rows, CHUNK), 0) - spot_ref[0]
    col_id = lax.broadcasted_iota(jnp.int32, (rows, CHUNK), 1) - spot_ref[1]
    inside = (row_id >= 0) & (row_id < pair)
    load.wait()
    stores = []
    for k in range(text_ref.shape[0] // CHUNK):
        block = pl.ds(k * CHUNK, CHUNK)
        text = text_ref[block, :]
        logits = temper * nt(unit, text) + offset
        sign = jnp.where(inside & (col_id + k * CHUNK == row_id), 1.0, -1.0)
        grad = (-factor * sign / (1.0 + jnp.exp(sign * logits))).astype(BF16)
        if k == 0:
            total_ref[...] = nn(grad, text)
        else:
            total_ref[...] += nn(grad, text)
        part_ref[block, :] = (temper * tn(grad, unit)).astype(BF16)
        store = pltpu.make_async_copy(part_ref.at[block], part_hbm.at[block], out_sem.at[k])
        store.start()
        stores.append(store)
    image_back = temper * total_ref[...]
    unit_float = unit.astype(F32)
    radial = jnp.sum(unit_float * image_back, axis=1, keepdims=True)
    back = ((image_back - unit_float * radial) / norm).astype(BF16)
    back_ref[...] = back
    send_ref[...] = nn(cols_ref[...], back).astype(BF16)
    for store in stores:
        store.wait()


def place_kernel(chosen_ref, back_ref, unit_ref, norm_ref, out_ref):
    back = back_ref[...].astype(F32)
    unit = unit_ref[...].astype(F32)
    radial = jnp.sum(unit * back, axis=1, keepdims=True)
    rows = (back - unit * radial) / norm_ref[...]
    spots = lax.broadcasted_iota(jnp.int32, (out_ref.shape[0], rows.shape[0]), 0)
    here = (spots == chosen_ref[...]).astype(F32)
    out_ref[...] = jnp.dot(here, rows, precision=lax.Precision.HIGHEST, preferred_element_type=F32)


def call(kernel, outs, in_specs, out_specs, scratch=(), cost=0):
    return pl.pallas_call(
        kernel,
        out_shape=tuple(jax.ShapeDtypeStruct(shape, dtype) for shape, dtype in outs),
        in_specs=in_specs,
        out_specs=out_specs,
        scratch_shapes=list(scratch),
        compiler_params=PARAMS,
        cost_estimate=pl.CostEstimate(flops=cost, bytes_accessed=2_000_000, transcendentals=0),
    )


def shards(image_cand, text_cand, selection, head_weight, logit_temp, logit_offset, loss_scale):
    pairs = selection.shape[0]
    cands, depth = image_cand.shape
    own_rows, width = head_weight.shape
    rows = 2 * pairs
    n_y, n_x = lax.axis_size("y"), lax.axis_size("x")
    my_zl, my_y, core = (lax.axis_index(a) for a in ("zl", "y", "c"))
    total = pairs * lax.axis_size(ALL)
    spot = jnp.stack([my_zl * pairs, my_y * pairs, core])
    scalars = jnp.stack([logit_temp[0], logit_offset[0], loss_scale[0] / total])

    text_unit, txt_norm = call(
        text_kernel, [((pairs, width), BF16), ((pairs, 1), F32)], [VMEM, VMEM], (VMEM, VMEM), cost=2 * pairs * cands * width,
    )(selection[:, None], text_cand)
    text_all = lax.all_gather(text_unit, "y", axis=0, tiled=True)

    both = lax.all_gather(head_weight, "c", axis=0, tiled=True)
    part = lax.dynamic_slice(both, (0, core * (width - WIDE)), (2 * own_rows, WIDE))
    slab = lax.all_gather(part, "zh", axis=0, tiled=True)
    (picked,) = call(
        image_kernel, [((pairs, depth), BF16)], [VMEM, VMEM], (VMEM,), cost=2 * pairs * cands * depth,
    )(selection[:, None], image_cand)
    slab, picked = lax.optimization_barrier((slab, picked))
    there = hop(picked, "zl", 1)
    slabs = lax.all_to_all(jnp.broadcast_to(slab[None], (n_x,) + slab.shape), "x", 0, 0)
    mine = slabs.reshape(depth, WIDE)
    other = hop(mine, "c", 1)

    blocks = depth // own_rows
    images, cols_mine, cols_other = call(
        lambda *refs: pair_kernel(blocks, *refs),
        [((rows, depth), BF16), ((depth // 2, rows), BF16), ((depth // 2, rows), BF16)],
        [SMEM, VMEM, VMEM], (VMEM, VMEM, VMEM),
        [pltpu.VMEM((depth, rows), F32), pltpu.VMEM((2, depth // 2, rows), F32)],
    )(spot, picked, there)

    send, proj_back, text_part = call(
        main_kernel,
        [((depth // 2, width), BF16), ((rows, width), BF16), ((n_y * pairs, width), BF16)],
        [SMEM, SMEM, VMEM, VMEM, VMEM, VMEM, ANY], (VMEM, VMEM, ANY),
        [pltpu.VMEM((n_y * pairs, width), BF16), pltpu.VMEM((n_y * pairs, width), BF16),
         pltpu.VMEM((rows, width), F32), pltpu.VMEM((rows, width), F32),
         pltpu.SemaphoreType.DMA, pltpu.SemaphoreType.DMA((n_y * pairs // CHUNK,))],
        cost=6 * rows * n_y * pairs * width,
    )(scalars, spot, images, mine, other, cols_other, text_all)

    text_back = lax.psum_scatter(text_part.reshape(n_y, pairs, width), "y", scatter_dimension=0)
    got = hop(send, "c", 1)
    head = nn(cols_mine, proj_back) + got.astype(F32)

    def spread(values, axis):
        count = lax.axis_size(axis)
        parts = values.astype(BF16).reshape(count, values.shape[0] // count, values.shape[1])
        return jnp.sum(lax.all_to_all(parts, axis, 0, 0).astype(F32), axis=0)

    head = spread(head, "x")
    head = spread(head, ("zh", "zl"))
    copies = jnp.broadcast_to(head.astype(BF16)[None], (n_y,) + head.shape)
    head = jnp.sum(lax.all_to_all(copies, "y", 0, 0).astype(F32), axis=0)
    head_grad = lax.all_gather(head, "zl", axis=0, tiled=True)

    (text_grad,) = call(
        place_kernel, [((cands, width), F32)], [VMEM] * 4, (VMEM,), cost=12 * cands * pairs * width,
    )(selection[None, :], text_back, text_unit, txt_norm)
    return head_grad, text_grad


def solution(mesh):
    devices = mesh.devices
    fine = Mesh(devices.reshape(2, devices.shape[0] // 2, 4, devices.shape[1] // 8, 2), ALL)
    return jax.shard_map(
        shards,
        mesh=fine,
        in_specs=(P(ALL, None), P(ALL, None), P(ALL), P(("x", "zh", "c"), None), P(), P(), P()),
        out_specs=(P(("x", "zh", "c"), None), P(ALL, None)),
        check_vma=False,
    )
```

time: 182 us -> 166 us (0.912)
  starting transfers between devices: 28.1 us -> 7.8 us
  blocking collectives: 91 us -> 111 us
  local copies, waits for them, and re-layouts: 23.5 us -> 7.82 us
  other arithmetic: 8.64 us -> 0.65 us
  Pallas kernels: 6.86 us -> 13.5 us
  waiting for transfers between devices: 3.75 us -> 8.64 us
  matrix products: 2.89 us -> 0.55 us
    ppermute x11 -> x3, starting transfers between devices: 28.1 us -> 7.72 us  [hop(): lax.ppermute(value, axis, [(s, (s + steps) % count) for s in range(count)])]
    all_to_all x3 -> x4, blocking collectives: 63.2 us -> 82.5 us  [the longest x2 40.4 us: spread(): return jnp.sum(lax.all_to_all(parts, axis, 0, 0).astype(F32), axis=0)]
    pallas_call x2 -> x5, Pallas kernels: 6.86 us -> 13.5 us  [the longest x1 7.96 us: shards(): call(main_kernel, [((depth // 2, width), BF16), ((rows, width), BF16), ((...]
    another operation x5 -> x0, local copies, waits for them, and re-layouts: 5.83 us -> none
    ppermute x11 -> x3, waiting for transfers between devices: 3.71 us -> 8.58 us  [hop(): lax.ppermute(value, axis, [(s, (s + steps) % count) for s in range(count)])]
    scatter x1 -> x0, other arithmetic: 2.71 us -> none  [shards(): jnp.zeros((text_cand.shape[0], width), jnp.float32).at[selection]]
    dot_general x2 -> x1, matrix products: 2.89 us -> 0.55 us  [nn(): return jnp.dot(a, b, preferred_element_type=F32)]
    dynamic_slice x2 -> x1, local copies, waits for them, and re-layouts: 2.25 us -> 0.02 us  [shards(): lax.dynamic_slice(both, (0, core * (width - WIDE)), (2 * own_rows, WIDE))]
  transfers between devices with their start and end apart: 13 -> 5, of which waited for: 2 -> 2; matrix products, arithmetic and copies ran while one was open for 11% -> 1% of each run, Pallas kernels for 2% -> 1%
where the time goes in v3:
time: 166 us
  blocking collectives  111 us (67%)
  between operations  16.1 us (10%)
  Pallas kernels  13.5 us (8%)
  waiting for transfers between devices  8.64 us (5%)
  local copies, waits for them, and re-layouts  7.82 us (5%)
  starting transfers between devices  7.8 us (5%)
    all_to_all x2, blocking collectives, spread(): return jnp.sum(lax.all_to_all(parts, axis, 0, 0).astype(F32), axis=0)  40.4 us
    all_to_all x1, blocking collectives, shards(): lax.all_to_all(jnp.broadcast_to(slab[None], (n_x,) + slab.shape), 'x', 0, 0)  21.4 us
    all_to_all x1, blocking collectives, shards(): head = jnp.sum(lax.all_to_all(copies, 'y', 0, 0).astype(F32), axis=0)  20.7 us
    all_gather x1, blocking collectives, shards(): slab = lax.all_gather(part, 'zh', axis=0, tiled=True)  20.5 us
    ppermute x3, waiting for transfers between devices, hop(): lax.ppermute(value, axis, [(s, (s + steps) % count) for s in range(count)])  8.58 us
    pallas_call x1, Pallas kernels, shards(): call(main_kernel, [((depth // 2, width), BF16), ((rows, width), BF16), ((...  7.96 us
    ppermute x3, starting transfers between devices, hop(): lax.ppermute(value, axis, [(s, (s + steps) % count) for s in range(count)])  7.72 us
    unnamed x16, local copies, waits for them, and re-layouts  6.79 us
  transfers between devices with their start and end apart: 5, of which 2 were waited for; matrix products, arithmetic and copies ran while one was open for 1% of the time, Pallas kernels for 1%

profile of v3, /device:TPU:2, one launch (start us, length us, event | category | flops | bytes accessed | tf_op | source)
XLA Modules:
  0.0 165.8 jit_solution(1032701537916022677)
XLA Ops:
  7.2 0.0 all-gather.4.cloned.1.call-start
  7.2 0.8 copy.20.chosen_ref
  8.0 0.0 copy-start
  8.0 1.1 copy-done
  9.0 0.0 copy-start.1
  9.0 1.1 shard_map.88
  10.2 0.0 all-gather.4.cloned.1.call-update
  10.2 0.0 reduce-scatter.2.cloned.1.call-start
  10.2 2.1 %all-gather = bf16[2,36,1152]{2,1,0:T(8,128)(2,1)S(1)} all-gather(bf16[1,36,1152]{2,1,0:T(8,128)(2,1)} %bitcast.20), channel_id=1, replica_groups=mesh['zl'=2,'y'=8,'x'=4,'zh'=4,'c'=2] {'c'}, dimensions={0}, use_global_device_ids=true | all-gather | bytes 248832 | tf_op jit(solution)/shard_map/all_gather | solution.py:149
  12.4 0.0 copy-done.1
  12.5 0.3 shard_map.86.refs_1_
  12.8 20.5 %all_gather.13 = bf16[288,640]{1,0:T(8,128)(2,1)S(1)} all-gather(bf16[72,640]{1,0:T(8,128)(2,1)S(1)} %constant_dynamic-slice_fusion), channel_id=1, replica_groups=mesh['zl'=2,'y'=8,'x'=4,'zh'=4,'c'=2] {'zh'}, dimensions={0}, use_global_device_ids=true | all-gather | bytes 460800 | tf_op jit(solution)/shard_map/all_gather | solution.py:151
  33.3 0.1 broadcast_in_dim.9
  33.4 21.4 %all_to_all.20 = bf16[4,288,640]{2,1,0:T(8,128)(2,1)S(1)} all-to-all(bf16[4,288,640]{2,1,0:T(8,128)(2,1)S(1)} %broadcast_in_dim.9), channel_id=1, replica_groups=mesh['zl'=2,'y'=8,'x'=4,'zh'=4,'c'=2] {'x'}, dimensions={0} | all-to-all | bytes 2949120 | tf_op jit(solution)/shard_map/all_to_all | solution.py:157
  54.8 1.9 %collective-permute-start.1 = (bf16[1152,640]{1,0:T(8,128)(2,1)S(1)}, bf16[1152,640]{1,0:T(8,128)(2,1)}, u32[]{:S(2)}, u32[]{:S(2)}) collective-permute-start(bf16[1152,640]{1,0:T(8,128)(2,1)S(1)} %bitcast.13), channel_id=1, source_target_pairs={{0,1},{1,0},{2,3},{3,2},{4,5},{5,4},{6,7},{7,6},{8,9},{9,8},{10,11... | collective-permute-start | bytes 4423688 | tf_op jit(solution)/shard_map/ppermute | solution.py:21
  56.7 3.9 %collective-permute-start = (bf16[128,1152]{1,0:T(8,128)(2,1)S(1)}, bf16[128,1152]{1,0:T(8,128)(2,1)S(1)}, u32[]{:S(2)}, u32[]{:S(2)}) collective-permute-start(bf16[128,1152]{1,0:T(8,128)(2,1)S(1)} %shard_map.86.refs_1_), channel_id=1, source_target_pairs={{0,256},{256,0},{1,257},{257,1},{2,258},{258,2},{3,259},{259,3},{4... | collective-permute-start | bytes 884744 | tf_op jit(solution)/shard_map/ppermute | solution.py:21
  62.6 0.1 pad_add_fusion.refs_0_.spot_ref
  62.6 0.1 pad_maximum_fusion.scal_ref
  62.7 5.6 %collective-permute-done.refs_2_ = bf16[128,1152]{1,0:T(8,128)(2,1)S(1)} collective-permute-done((bf16[128,1152]{1,0:T(8,128)(2,1)S(1)}, bf16[128,1152]{1,0:T(8,128)(2,1)S(1)}, u32[]{:S(2)}, u32[]{:S(2)}) %collective-permute-start) | collective-permute-done | bytes 294944 | tf_op jit(solution)/shard_map/ppermute | solution.py:21
  68.3 0.9 shard_map.87
  69.2 0.0 collective-permute-done.1.other_ref
  69.2 0.0 all-gather.4.cloned.1.call-done.text_hbm
  69.2 0.0 copy-start.4
  69.2 1.7 copy-done.4
  70.9 8.0 %shard_map.89 = (bf16[576,1152]{1,0:T(8,128)(2,1)S(1)}, bf16[256,1152]{1,0:T(8,128)(2,1)S(1)}, bf16[1024,1152]{1,0:T(8,128)(2,1)}) custom-call(f32[3]{0:T(128)S(1)} %pad_maximum_fusion.scal_ref, s32[3]{0:T(128)S(1)} %pad_add_fusion.refs_0_.spot_ref, bf16[256,1152]{1,0:T(8,128)(2,1)S(1)} %get-tuple-element.14.images_ref, bf16[1152,640]{1,0:T(8,128)(2,1)S(1)} %bitcast.14, ...), custom_call_target="tpu_custom_call" | custom-call | flops 1811939328 | bytes 2000000 | tf_op jit(solution)/shard_map/pallas_call | solution.py:169
  78.8 0.0 copy-start.5
  78.8 1.1 copy-done.5
  79.9 0.0 copy-start.6
  79.9 0.0 reduce-scatter.2.cloned.1.call-update
  80.0 1.3 copy-done.6
  81.2 1.9 %collective-permute-start.2 = (bf16[576,1152]{1,0:T(8,128)(2,1)S(1)}, bf16[576,1152]{1,0:T(8,128)(2,1)S(1)}, u32[]{:S(2)}, u32[]{:S(2)}) collective-permute-start(bf16[576,1152]{1,0:T(8,128)(2,1)S(1)} %copy-done.6), channel_id=1, source_target_pairs={{0,1},{1,0},{2,3},{3,2},{4,5},{5,4},{6,7},{7,6},{8,9},{9,8},{10,11... | collective-permute-start | bytes 3981320 | tf_op jit(solution)/shard_map/ppermute | solution.py:21
  83.2 3.0 %collective-permute-done.2 = bf16[576,1152]{1,0:T(8,128)(2,1)S(1)} collective-permute-done((bf16[576,1152]{1,0:T(8,128)(2,1)S(1)}, bf16[576,1152]{1,0:T(8,128)(2,1)S(1)}, u32[]{:S(2)}, u32[]{:S(2)}) %collective-permute-start.2) | collective-permute-done | bytes 1327136 | tf_op jit(solution)/shard_map/ppermute | solution.py:21
  86.2 0.6 fusion
  86.7 21.1 %all_to_all.21 = bf16[4,144,1152]{2,1,0:T(8,128)(2,1)S(1)} all-to-all(bf16[4,144,1152]{2,1,0:T(8,128)(2,1)S(1)} %bitcast.18), channel_id=1, replica_groups=mesh['zl'=2,'y'=8,'x'=4,'zh'=4,'c'=2] {'x'}, dimensions={0} | all-to-all | bytes 2654208 | tf_op jit(solution)/shard_map/all_to_all | solution.py:186
  107.8 0.2 reduce_sum.33
  108.0 0.1 reshape.23
  108.1 19.4 %all_to_all.22 = bf16[8,18,1152]{2,1,0:T(8,128)(2,1)S(1)} all-to-all(bf16[8,18,1152]{2,1,0:T(8,128)(2,1)S(1)} %reshape.23), channel_id=1, replica_groups=mesh['zl'=2,'y'=8,'x'=4,'zh'=4,'c'=2] {'zh','zl'}, dimensions={0} | all-to-all | bytes 663552 | tf_op jit(solution)/shard_map/all_to_all | solution.py:186
  127.5 0.0 copy-start.3
  127.5 0.1 reduce_sum.34
  127.6 20.7 %all_to_all.23 = bf16[8,18,1152]{2,1,0:T(8,128)(2,1)S(1)} all-to-all(bf16[8,18,1152]{2,1,0:T(8,128)(2,1)S(1)} %broadcast_in_dim.10), channel_id=1, replica_groups=mesh['zl'=2,'y'=8,'x'=4,'zh'=4,'c'=2] {'y'}, dimensions={0} | all-to-all | bytes 663552 | tf_op jit(solution)/shard_map/all_to_all | solution.py:191
  148.3 0.2 convert_reduce_fusion
  148.6 5.4 %all-gather.1 = f32[2,18,1152]{2,1,0:T(8,128)S(1)} all-gather(f32[1,18,1152]{2,1,0:T(8,128)S(1)} %bitcast.19), channel_id=1, replica_groups=mesh['zl'=2,'y'=8,'x'=4,'zh'=4,'c'=2] {'zl'}, dimensions={0}, use_global_device_ids=true | all-gather | bytes 248832 | tf_op jit(solution)/shard_map/all_gather | solution.py:192
  154.0 0.7 reshape.28
  154.7 0.0 reduce-scatter.2.cloned.1.call-done
  154.7 0.0 copy-done.3
  154.7 0.0 copy-start.2
  154.7 1.0 copy-done.2
  155.6 3.3 %shard_map.90 = f32[256,1152]{1,0:T(8,128)} custom-call(s32[1,128]{1,0:T(1,128)S(1)} %bitcast.17, bf16[128,1152]{1,0:T(8,128)(2,1)S(1)} %bitcast.15, bf16[128,1152]{1,0:T(8,128)(2,1)} %get-tuple-element.17.unit_ref, f32[128,1]{1,0:T(8,128)S(1)} %get-tuple-element.21.norm_ref), custom_call_target="tpu_custom_call" | custom-call | flops 452984832 | bytes 2000000 | tf_op jit(solution)/shard_map/pallas_call | solution.py:194
  (3 shorter events, 0.1 us)
Async XLA Ops:
  7.2 62.0 %all-gather.4.cloned.1.call-start = ((), (), s32[]{:S(2)}) async-start(), calls=%async_computation.5 | async-start | bytes 2654208 | tf_op jit(solution)/shard_map/all_gather | solution.py:147
  8.0 1.1 copy-start
  9.0 3.4 %copy-start.1 = (bf16[256,1152]{1,0:T(8,128)(2,1)S(1)}, bf16[256,1152]{1,0:T(8,128)(2,1)}, u32[]{:S(2)}) copy-start(bf16[256,1152]{1,0:T(8,128)(2,1)} %cand_ref.2) | copy-start | bytes 1769476
  10.2 144.5 %reduce-scatter.2.cloned.1.call-start = ((), (), s32[]{:S(2)}) async-start(), calls=%async_computation.6 | async-start | bytes 2654208 | tf_op jit(solution)/shard_map/reduce_scatter | solution.py:179
  54.8 14.4 %collective-permute-start.1 = (bf16[1152,640]{1,0:T(8,128)(2,1)S(1)}, bf16[1152,640]{1,0:T(8,128)(2,1)}, u32[]{:S(2)}, u32[]{:S(2)}) collective-permute-start(bf16[1152,640]{1,0:T(8,128)(2,1)S(1)} %bitcast.13), channel_id=1, source_target_pairs={{0,1},{1,0},{2,3},{3,2},{4,5},{5,4},{6,7},{7,6},{8,9},{9,8},{10,11... | collective-permute-start | bytes 4423688 | tf_op jit(solution)/shard_map/ppermute | solution.py:21
  56.7 11.6 %collective-permute-start = (bf16[128,1152]{1,0:T(8,128)(2,1)S(1)}, bf16[128,1152]{1,0:T(8,128)(2,1)S(1)}, u32[]{:S(2)}, u32[]{:S(2)}) collective-permute-start(bf16[128,1152]{1,0:T(8,128)(2,1)S(1)} %shard_map.86.refs_1_), channel_id=1, source_target_pairs={{0,256},{256,0},{1,257},{257,1},{2,258},{258,2},{3,259},{259,3},{4... | collective-permute-start | bytes 884744 | tf_op jit(solution)/shard_map/ppermute | solution.py:21
  69.2 1.7 %copy-start.4 = (bf16[1024,1152]{1,0:T(8,128)(2,1)S(1)}, bf16[1024,1152]{1,0:T(8,128)(2,1)}, u32[]{:S(2)}) copy-start(bf16[1024,1152]{1,0:T(8,128)(2,1)} %all-gather.4.cloned.1.call-done.text_hbm) | copy-start | bytes 7077892
  78.8 1.1 copy-start.5
  79.9 1.3 copy-start.6
  81.2 4.9 %collective-permute-start.2 = (bf16[576,1152]{1,0:T(8,128)(2,1)S(1)}, bf16[576,1152]{1,0:T(8,128)(2,1)S(1)}, u32[]{:S(2)}, u32[]{:S(2)}) collective-permute-start(bf16[576,1152]{1,0:T(8,128)(2,1)S(1)} %copy-done.6), channel_id=1, source_target_pairs={{0,1},{1,0},{2,3},{3,2},{4,5},{5,4},{6,7},{7,6},{8,9},{9,8},{10,11... | collective-permute-start | bytes 3981320 | tf_op jit(solution)/shard_map/ppermute | solution.py:21
  127.5 27.2 %copy-start.3 = (s32[128]{0:T(128)S(1)}, s32[128]{0:T(128)}, u32[]{:S(2)}) copy-start(s32[128]{0:T(128)} %param.9) | copy-start | bytes 1540
  154.7 1.0 copy-start.2
Sparse Core Ops, SparseCore 0:
  10.3 48.9 all-gather.3
  80.1 43.1 reduce-scatter.1

commit v4 on v3

--- a/solution.py
+++ b/solution.py
@@ -11,7 +11,8 @@
 CHUNK = 256
 VMEM = pl.BlockSpec(memory_space=pltpu.VMEM)
 SMEM = pl.BlockSpec(memory_space=pltpu.SMEM)
-ANY = pl.BlockSpec(memory_space=pl.ANY)
+HBM = pl.BlockSpec(memory_space=pltpu.HBM)
+LANES = 128
 PARAMS = pltpu.CompilerParams(vmem_limit_bytes=40 * 1024 * 1024)
 F32, BF16 = jnp.float32, jnp.bfloat16
 
@@ -34,9 +35,9 @@
 
 
 def pick_rows(chosen_ref, cand_ref):
-    pairs, cands = chosen_ref.shape[0], cand_ref.shape[0]
-    spots = lax.broadcasted_iota(jnp.int32, (pairs, cands), 1)
-    return nn((spots == chosen_ref[...]).astype(BF16), cand_ref[...])
+    pairs, cands = chosen_ref.shape[1], cand_ref.shape[0]
+    spots = lax.broadcasted_iota(jnp.int32, (cands, pairs), 0)
+    return tn((spots == chosen_ref[...]).astype(BF16), cand_ref[...])
 
 
 def text_kernel(chosen_ref, cand_ref, unit_ref, norm_ref):
@@ -65,47 +66,83 @@
     cols_other_ref[...] = group_ref[1 - core].astype(BF16)
 
 
-def main_kernel(scal_ref, spot_ref, images_ref, mine_ref, other_ref, cols_ref, text_hbm, send_ref, back_ref, part_hbm,
-                text_ref, part_ref, proj_ref, total_ref, in_sem, out_sem):
-    load = pltpu.make_async_copy(text_hbm, text_ref, in_sem)
+def half_kernel(images_ref, mine_ref, out_ref):
+    out_ref[...] = nn(images_ref[...], mine_ref[...])
+
+
+def main_kernel(scal_ref, spot_ref, images_ref, half_ref, other_ref, cols_ref, text_hbm, send_ref, back_ref, unit_ref, grad_ref,
+                text_ref, proj_ref, total_ref, sem):
+    load = pltpu.make_async_copy(text_hbm, text_ref, sem)
     load.start()
     temper, offset, factor = scal_ref[0], scal_ref[1], scal_ref[2]
     rows, width = proj_ref.shape
     first = spot_ref[2] == 0
-    proj_mine, proj_other = nn(images_ref[...], mine_ref[...]), nn(images_ref[...], other_ref[...])
+    proj_mine, proj_other = half_ref[...], nn(images_ref[...], other_ref[...])
     proj_ref[:, :WIDE] = jnp.where(first, proj_mine, proj_other)
     proj_ref[:, WIDE:] = jnp.where(first, proj_other, proj_mine)[:, 2 * WIDE - width:]
     proj = proj_ref[...]
     norm = jnp.sqrt(jnp.sum(proj * proj, axis=1, keepdims=True) + EPS)
     unit = (proj / norm).astype(BF16)
+    unit_ref[...] = unit
     pair = rows // 2
     row_id = lax.broadcasted_iota(jnp.int32, (rows, CHUNK), 0) - spot_ref[0]
     col_id = lax.broadcasted_iota(jnp.int32, (rows, CHUNK), 1) - spot_ref[1]
     inside = (row_id >= 0) & (row_id < pair)
     load.wait()
-    stores = []
     for k in range(text_ref.shape[0] // CHUNK):
-        block = pl.ds(k * CHUNK, CHUNK)
+        block = slice(k * CHUNK, (k + 1) * CHUNK)
         text = text_ref[block, :]
         logits = temper * nt(unit, text) + offset
         sign = jnp.where(inside & (col_id + k * CHUNK == row_id), 1.0, -1.0)
         grad = (-factor * sign / (1.0 + jnp.exp(sign * logits))).astype(BF16)
+        grad_ref[:, block] = grad
         if k == 0:
             total_ref[...] = nn(grad, text)
         else:
             total_ref[...] += nn(grad, text)
-        part_ref[block, :] = (temper * tn(grad, unit)).astype(BF16)
-        store = pltpu.make_async_copy(part_ref.at[block], part_hbm.at[block], out_sem.at[k])
-        store.start()
-        stores.append(store)
     image_back = temper * total_ref[...]
     unit_float = unit.astype(F32)
     radial = jnp.sum(unit_float * image_back, axis=1, keepdims=True)
     back = ((image_back - unit_float * radial) / norm).astype(BF16)
     back_ref[...] = back
     send_ref[...] = nn(cols_ref[...], back).astype(BF16)
+
+
+def part_kernel(scal_ref, grad_ref, unit_ref, part_hbm, part_ref, sem):
+    unit = unit_ref[...]
+    stores = []
+    for k in range(part_ref.shape[0] // CHUNK):
+        block = pl.ds(k * CHUNK, CHUNK)
+        part_ref[block, :] = (scal_ref[0] * tn(grad_ref[:, k * CHUNK:(k + 1) * CHUNK], unit)).astype(BF16)
+        store = pltpu.make_async_copy(part_ref.at[block], part_hbm.at[block], sem.at[k])
+        store.start()
+        stores.append(store)
     for store in stores:
         store.wait()
+
+
+def fold_kernel(came_ref, out_ref, sum_ref, flat_ref):
+    total = came_ref[0].astype(F32)
+    for k in range(1, came_ref.shape[0]):
+        total += came_ref[k].astype(F32)
+    sum_ref[...] = total
+    flat_ref[...] = jnp.zeros_like(flat_ref)
+    pieces = flat_ref.shape[0]
+    size = sum_ref.shape[0] // pieces
+    for p in range(pieces):
+        for t in range(sum_ref.shape[1] // LANES):
+            flat_ref[p, t * size:(t + 1) * size, :] = sum_ref[p * size:(p + 1) * size, t * LANES:(t + 1) * LANES]
+    out_ref[...] = flat_ref[...].astype(BF16)
+
+
+def unfold_kernel(came_ref, out_ref, sum_ref):
+    total = came_ref[0].astype(F32)
+    for k in range(1, came_ref.shape[0]):
+        total += came_ref[k].astype(F32)
+    sum_ref[...] = total
+    size = out_ref.shape[0]
+    for t in range(out_ref.shape[1] // LANES):
+        out_ref[:, t * LANES:(t + 1) * LANES] = sum_ref[t * size:(t + 1) * size, :]
 
 
 def place_kernel(chosen_ref, back_ref, unit_ref, norm_ref, out_ref):
@@ -143,17 +180,18 @@
 
     text_unit, txt_norm = call(
         text_kernel, [((pairs, width), BF16), ((pairs, 1), F32)], [VMEM, VMEM], (VMEM, VMEM), cost=2 * pairs * cands * width,
-    )(selection[:, None], text_cand)
+    )(selection[None, :], text_cand)
     text_all = lax.all_gather(text_unit, "y", axis=0, tiled=True)
+
+    (picked,) = call(
+        image_kernel, [((pairs, depth), BF16)], [VMEM, VMEM], (VMEM,), cost=2 * pairs * cands * depth,
+    )(selection[None, :], image_cand)
+    there = hop(picked, "zl", 1)
 
     both = lax.all_gather(head_weight, "c", axis=0, tiled=True)
     part = lax.dynamic_slice(both, (0, core * (width - WIDE)), (2 * own_rows, WIDE))
     slab = lax.all_gather(part, "zh", axis=0, tiled=True)
-    (picked,) = call(
-        image_kernel, [((pairs, depth), BF16)], [VMEM, VMEM], (VMEM,), cost=2 * pairs * cands * depth,
-    )(selection[:, None], image_cand)
-    slab, picked = lax.optimization_barrier((slab, picked))
-    there = hop(picked, "zl", 1)
+    slab, there = lax.optimization_barrier((slab, there))
     slabs = lax.all_to_all(jnp.broadcast_to(slab[None], (n_x,) + slab.shape), "x", 0, 0)
     mine = slabs.reshape(depth, WIDE)
     other = hop(mine, "c", 1)
@@ -166,34 +204,47 @@
         [pltpu.VMEM((depth, rows), F32), pltpu.VMEM((2, depth // 2, rows), F32)],
     )(spot, picked, there)
 
-    send, proj_back, text_part = call(
+    (half,) = call(
+        half_kernel, [((rows, WIDE), F32)], [VMEM, VMEM], (VMEM,), cost=2 * rows * depth * WIDE,
+    )(images, mine)
+    send, proj_back, image_unit, grad_tile = call(
         main_kernel,
-        [((depth // 2, width), BF16), ((rows, width), BF16), ((n_y * pairs, width), BF16)],
-        [SMEM, SMEM, VMEM, VMEM, VMEM, VMEM, ANY], (VMEM, VMEM, ANY),
-        [pltpu.VMEM((n_y * pairs, width), BF16), pltpu.VMEM((n_y * pairs, width), BF16),
-         pltpu.VMEM((rows, width), F32), pltpu.VMEM((rows, width), F32),
-         pltpu.SemaphoreType.DMA, pltpu.SemaphoreType.DMA((n_y * pairs // CHUNK,))],
-        cost=6 * rows * n_y * pairs * width,
-    )(scalars, spot, images, mine, other, cols_other, text_all)
+        [((depth // 2, width), BF16), ((rows, width), BF16), ((rows, width), BF16), ((rows, n_y * pairs), BF16)],
+        [SMEM, SMEM, VMEM, VMEM, VMEM, VMEM, HBM], (VMEM,) * 4,
+        [pltpu.VMEM((n_y * pairs, width), BF16), pltpu.VMEM((rows, width), F32), pltpu.VMEM((rows, width), F32),
+         pltpu.SemaphoreType.DMA],
+        cost=5 * rows * n_y * pairs * width,
+    )(scalars, spot, images, half, other, cols_other, text_all)
+    (text_part,) = call(
+        part_kernel, [((n_y * pairs, width), BF16)], [SMEM, VMEM, VMEM], (HBM,),
+        [pltpu.VMEM((n_y * pairs, width), BF16), pltpu.SemaphoreType.DMA((n_y * pairs // CHUNK,))],
+        cost=2 * rows * n_y * pairs * width,
+    )(scalars, grad_tile, image_unit)
 
     text_back = lax.psum_scatter(text_part.reshape(n_y, pairs, width), "y", scatter_dimension=0)
     got = hop(send, "c", 1)
     head = nn(cols_mine, proj_back) + got.astype(F32)
 
-    def spread(values, axis):
-        count = lax.axis_size(axis)
-        parts = values.astype(BF16).reshape(count, values.shape[0] // count, values.shape[1])
-        return jnp.sum(lax.all_to_all(parts, axis, 0, 0).astype(F32), axis=0)
-
-    head = spread(head, "x")
-    head = spread(head, ("zh", "zl"))
-    copies = jnp.broadcast_to(head.astype(BF16)[None], (n_y,) + head.shape)
-    head = jnp.sum(lax.all_to_all(copies, "y", 0, 0).astype(F32), axis=0)
-    head_grad = lax.all_gather(head, "zl", axis=0, tiled=True)
+    share = depth // 2 // n_x
+    came = lax.all_to_all(head.astype(BF16).reshape(n_x, share, width), "x", 0, 0)
+    n_z = lax.axis_size(("zh", "zl"))
+    piece = share // n_z
+    strips = piece * (width // LANES)
+    strips += -strips % 8
+    (folded,) = call(
+        fold_kernel, [((n_z, strips, LANES), BF16)], [VMEM], (VMEM,),
+        [pltpu.VMEM((share, width), F32), pltpu.VMEM((n_z, strips, LANES), F32)],
+    )(came)
+    came = lax.all_to_all(folded, ("zh", "zl"), 0, 0)
+    head = jnp.sum(came.astype(F32), axis=0).astype(BF16)
+    came = lax.all_to_all(jnp.broadcast_to(head[None], (n_y,) + head.shape), "y", 0, 0)
+    (head,) = call(unfold_kernel, [((piece, width), F32)], [VMEM], (VMEM,), [pltpu.VMEM((strips, LANES), F32)])(came)
 
     (text_grad,) = call(
         place_kernel, [((cands, width), F32)], [VMEM] * 4, (VMEM,), cost=12 * cands * pairs * width,
     )(selection[None, :], text_back, text_unit, txt_norm)
+    head, text_grad = lax.optimization_barrier((head, text_grad))
+    head_grad = lax.all_gather(head, "zl", axis=0, tiled=True)
     return head_grad, text_grad
 
 

time: 166 us -> 158 us (0.952)
  waiting for transfers between devices: 8.64 us -> 2.74 us
  blocking collectives: 111 us -> 106 us
    ppermute x3, waiting for transfers between devices: 8.58 us -> 2.67 us  [hop(): lax.ppermute(value, axis, [(s, (s + steps) % count) for s in range(count)])]
    all_to_all x3, blocking collectives: 61.1 us -> 56.5 us  [the longest x1 21.3 us: shards(): lax.all_to_all(head.astype(BF16).reshape(n_x, share, width), 'x', 0, 0)]
    pallas_call x0 -> x4, Pallas kernels: none -> 3.51 us  [the longest x1 2.42 us: shards(): call(part_kernel, [((n_y * pairs, width), BF16)], [SMEM, VMEM, VMEM], (HB...]
    pallas_call x1, Pallas kernels: 7.96 us -> 5.17 us  [shards(): call(main_kernel, [((depth // 2, width), BF16), ((rows, width), BF16), ((...]
    all_gather x1, blocking collectives: 20.5 us -> 22.7 us  [shards(): slab = lax.all_gather(part, 'zh', axis=0, tiled=True)]
    all_to_all x1, blocking collectives: 21.4 us -> 19.7 us  [shards(): lax.all_to_all(jnp.broadcast_to(slab[None], (n_x,) + slab.shape), 'x', 0, 0)]
    unnamed x16 -> x22, local copies, waits for them, and re-layouts: 6.79 us -> 8.08 us
  transfers between devices with their start and end apart: 5 -> 5, of which waited for: 2 -> 1; matrix products, arithmetic and copies ran while one was open for 1% -> 1% of each run, Pallas kernels for 1% -> 1%
where the time goes in v4:
time: 158 us; the launch traced here: 157 us
  blocking collectives  106 us (67%)
  between operations  16.2 us (10%)
  Pallas kernels  14.2 us (9%)
  starting transfers between devices  8.66 us (5%)
  local copies, waits for them, and re-layouts  8.25 us (5%)
  waiting for transfers between devices  2.74 us (2%)
    all_gather x1, blocking collectives, shards(): slab = lax.all_gather(part, 'zh', axis=0, tiled=True)  22.7 us
    all_to_all x1, blocking collectives, shards(): lax.all_to_all(head.astype(BF16).reshape(n_x, share, width), 'x', 0, 0)  21.3 us
    all_to_all x1, blocking collectives, shards(): lax.all_to_all(jnp.broadcast_to(slab[None], (n_x,) + slab.shape), 'x', 0, 0)  19.7 us
    all_to_all x1, blocking collectives, shards(): lax.all_to_all(jnp.broadcast_to(head[None], (n_y,) + head.shape), 'y', 0, 0)  17.9 us
    all_to_all x1, blocking collectives, shards(): came = lax.all_to_all(folded, ('zh', 'zl'), 0, 0)  17.2 us
    ppermute x3, starting transfers between devices, hop(): lax.ppermute(value, axis, [(s, (s + steps) % count) for s in range(count)])  8.58 us
    unnamed x22, local copies, waits for them, and re-layouts  8.08 us
    all_gather x1, blocking collectives, shards(): head_grad = lax.all_gather(head, 'zl', axis=0, tiled=True)  5.41 us
  transfers between devices with their start and end apart: 5, of which 1 were waited for; matrix products, arithmetic and copies ran while one was open for 1% of the time, Pallas kernels for 1%

profile of v4, /device:TPU:2, one launch (start us, length us, event | category | flops | bytes accessed | tf_op | source)
XLA Modules:
  0.0 157.0 jit_solution(8217094972939504942)
XLA Ops:
  7.2 0.0 all-gather.4.cloned.1.call-start
  7.2 0.0 copy-start
  7.2 1.1 copy-done
  8.3 0.0 copy-start.3
  8.3 0.7 copy-done.3
  8.9 0.0 copy-start.9
  8.9 1.1 shard_map.89
  10.1 0.0 all-gather.4.cloned.1.call-update
  10.1 0.0 reduce-scatter.2.cloned.1.call-start
  10.1 0.0 copy-start.1
  10.1 1.1 copy-done.1
  11.2 0.0 copy-start.4
  11.2 0.7 copy-done.4
  11.9 0.3 shard_map.86.refs_1_
  12.1 4.3 %collective-permute-start = (bf16[128,1152]{1,0:T(8,128)(2,1)S(1)}, bf16[128,1152]{1,0:T(8,128)(2,1)S(1)}, u32[]{:S(2)}, u32[]{:S(2)}) collective-permute-start(bf16[128,1152]{1,0:T(8,128)(2,1)S(1)} %shard_map.86.refs_1_), channel_id=1, source_target_pairs={{0,256},{256,0},{1,257},{257,1},{2,258},{258,2},{3,259},{259,3},{4... | collective-permute-start | bytes 884744 | tf_op jit(solution)/shard_map/ppermute | solution.py:22
  16.4 0.0 copy-done.9
  16.4 1.9 %all-gather = bf16[2,36,1152]{2,1,0:T(8,128)(2,1)S(1)} all-gather(bf16[1,36,1152]{2,1,0:T(8,128)(2,1)S(1)} %bitcast.20), channel_id=1, replica_groups=mesh['zl'=2,'y'=8,'x'=4,'zh'=4,'c'=2] {'c'}, dimensions={0}, use_global_device_ids=true | all-gather | bytes 248832 | tf_op jit(solution)/shard_map/all_gather | solution.py:191
  18.4 22.7 %all_gather.13 = bf16[288,640]{1,0:T(8,128)(2,1)S(1)} all-gather(bf16[72,640]{1,0:T(8,128)(2,1)S(1)} %constant_dynamic-slice_fusion), channel_id=1, replica_groups=mesh['zl'=2,'y'=8,'x'=4,'zh'=4,'c'=2] {'zh'}, dimensions={0}, use_global_device_ids=true | all-gather | bytes 460800 | tf_op jit(solution)/shard_map/all_gather | solution.py:193
  41.1 0.0 collective-permute-done.refs_2_
  41.1 0.1 broadcast_in_dim.7
  41.3 19.7 %all_to_all.20 = bf16[4,288,640]{2,1,0:T(8,128)(2,1)S(1)} all-to-all(bf16[4,288,640]{2,1,0:T(8,128)(2,1)S(1)} %broadcast_in_dim.7), channel_id=1, replica_groups=mesh['zl'=2,'y'=8,'x'=4,'zh'=4,'c'=2] {'x'}, dimensions={0} | all-to-all | bytes 2949120 | tf_op jit(solution)/shard_map/all_to_all | solution.py:195
  60.9 1.9 %collective-permute-start.1 = (bf16[1152,640]{1,0:T(8,128)(2,1)S(1)}, bf16[1152,640]{1,0:T(8,128)(2,1)}, u32[]{:S(2)}, u32[]{:S(2)}) collective-permute-start(bf16[1152,640]{1,0:T(8,128)(2,1)S(1)} %bitcast.12), channel_id=1, source_target_pairs={{0,1},{1,0},{2,3},{3,2},{4,5},{5,4},{6,7},{7,6},{8,9},{9,8},{10,11... | collective-permute-start | bytes 4423688 | tf_op jit(solution)/shard_map/ppermute | solution.py:22
  64.8 0.1 pad_maximum_fusion.scal_ref
  64.9 0.1 pad_add_fusion.refs_0_.spot_ref
  64.9 0.9 shard_map.87
  65.8 0.7 shard_map.88.half_ref
  66.5 0.0 collective-permute-done.1.other_ref
  66.5 0.0 all-gather.4.cloned.1.call-done.text_hbm
  66.5 0.0 copy-start.6
  66.6 1.7 %copy-done.6 = bf16[1024,1152]{1,0:T(8,128)(2,1)S(1)} copy-done((bf16[1024,1152]{1,0:T(8,128)(2,1)S(1)}, bf16[1024,1152]{1,0:T(8,128)(2,1)}, u32[]{:S(2)}) %copy-start.6) | copy-done | bytes 2359320
  68.2 5.2 %shard_map.90 = (bf16[576,1152]{1,0:T(8,128)(2,1)S(1)}, bf16[256,1152]{1,0:T(8,128)(2,1)S(1)}, bf16[256,1152]{1,0:T(8,128)(2,1)S(1)}, bf16[256,1024]{1,0:T(8,128)(2,1)S(1)}) custom-call(f32[3]{0:T(128)S(1)} %pad_maximum_fusion.scal_ref, s32[3]{0:T(128)S(1)} %pad_add_fusion.refs_0_.spot_ref, bf16[256,1152]{1,0:T(8,128)(2,1)S(1)} %get-tuple-element.17.images_ref, ...), custom_call_target="tpu_custom_call" | custom-call | flops 1509949440 | bytes 2000000 | tf_op jit(solution)/shard_map/pallas_call | solution.py:210
  73.4 0.0 copy-start.7
  73.4 2.4 %shard_map.93 = bf16[1024,1152]{1,0:T(8,128)(2,1)} custom-call(f32[3]{0:T(128)S(1)} %pad_maximum_fusion.scal_ref, bf16[256,1024]{1,0:T(8,128)(2,1)S(1)} %get-tuple-element.23.grad_ref, bf16[256,1152]{1,0:T(8,128)(2,1)S(1)} %get-tuple-element.24.unit_ref), custom_call_target="tpu_custom_call" | custom-call | flops 603979776 | bytes 2000000 | tf_op jit(solution)/shard_map/pallas_call | solution.py:218
  75.8 0.0 copy-done.7
  75.8 0.0 copy-start.8
  75.8 0.0 reduce-scatter.2.cloned.1.call-update
  75.9 1.3 copy-done.8
  77.2 2.4 %collective-permute-start.2 = (bf16[576,1152]{1,0:T(8,128)(2,1)S(1)}, bf16[576,1152]{1,0:T(8,128)(2,1)S(1)}, u32[]{:S(2)}, u32[]{:S(2)}) collective-permute-start(bf16[576,1152]{1,0:T(8,128)(2,1)S(1)} %copy-done.8), channel_id=1, source_target_pairs={{0,1},{1,0},{2,3},{3,2},{4,5},{5,4},{6,7},{7,6},{8,9},{9,8},{10,11... | collective-permute-start | bytes 3981320 | tf_op jit(solution)/shard_map/ppermute | solution.py:22
  79.6 2.7 %collective-permute-done.2 = bf16[576,1152]{1,0:T(8,128)(2,1)S(1)} collective-permute-done((bf16[576,1152]{1,0:T(8,128)(2,1)S(1)}, bf16[576,1152]{1,0:T(8,128)(2,1)S(1)}, u32[]{:S(2)}, u32[]{:S(2)}) %collective-permute-start.2) | collective-permute-done | bytes 1327136 | tf_op jit(solution)/shard_map/ppermute | solution.py:22
  82.2 0.6 fusion
  82.8 21.3 %all_to_all.21.came_ref = bf16[4,144,1152]{2,1,0:T(8,128)(2,1)S(1)} all-to-all(bf16[4,144,1152]{2,1,0:T(8,128)(2,1)S(1)} %bitcast.19), channel_id=1, replica_groups=mesh['zl'=2,'y'=8,'x'=4,'zh'=4,'c'=2] {'x'}, dimensions={0} | all-to-all | bytes 2654208 | tf_op jit(solution)/shard_map/all_to_all | solution.py:229
  104.1 0.4 shard_map.91
  104.5 0.0 copy-start.5
  104.5 17.2 %all_to_all.22 = bf16[8,168,128]{2,1,0:T(8,128)(2,1)S(1)} all-to-all(bf16[8,168,128]{2,1,0:T(8,128)(2,1)S(1)} %shard_map.91), channel_id=1, replica_groups=mesh['zl'=2,'y'=8,'x'=4,'zh'=4,'c'=2] {'zh','zl'}, dimensions={0} | all-to-all | bytes 688128 | tf_op jit(solution)/shard_map/all_to_all | solution.py:238
  121.7 0.1 reduce_sum.12
  121.8 17.9 %all_to_all.23.came_ref = bf16[8,168,128]{2,1,0:T(8,128)(2,1)S(1)} all-to-all(bf16[8,168,128]{2,1,0:T(8,128)(2,1)S(1)} %broadcast_in_dim.8), channel_id=1, replica_groups=mesh['zl'=2,'y'=8,'x'=4,'zh'=4,'c'=2] {'y'}, dimensions={0} | all-to-all | bytes 688128 | tf_op jit(solution)/shard_map/all_to_all | solution.py:240
  139.7 0.1 shard_map.92
  139.8 0.0 reduce-scatter.2.cloned.1.call-done
  139.8 0.0 copy-done.5
  139.8 0.0 copy-start.2
  139.9 1.0 copy-done.2
  140.8 3.3 %shard_map.94 = f32[256,1152]{1,0:T(8,128)} custom-call(s32[1,128]{1,0:T(1,128)S(1)} %bitcast.18, bf16[128,1152]{1,0:T(8,128)(2,1)S(1)} %bitcast.15, bf16[128,1152]{1,0:T(8,128)(2,1)} %get-tuple-element.20.unit_ref, f32[128,1]{1,0:T(8,128)S(1)} %get-tuple-element.25.norm_ref), custom_call_target="tpu_custom_call" | custom-call | flops 452984832 | bytes 2000000 | tf_op jit(solution)/shard_map/pallas_call | solution.py:243
  144.1 5.4 %all-gather.1 = f32[2,18,1152]{2,1,0:T(8,128)S(1)} all-gather(f32[1,18,1152]{2,1,0:T(8,128)S(1)} %bitcast.14), channel_id=1, replica_groups=mesh['zl'=2,'y'=8,'x'=4,'zh'=4,'c'=2] {'zl'}, dimensions={0}, use_global_device_ids=true | all-gather | bytes 248832 | tf_op jit(solution)/shard_map/all_gather | solution.py:247
  149.5 0.7 reshape.24
  (3 shorter events, 0.1 us)
Async XLA Ops:
  7.2 59.4 %all-gather.4.cloned.1.call-start = ((), (), s32[]{:S(2)}) async-start(), calls=%async_computation.5 | async-start | bytes 2654208 | tf_op jit(solution)/shard_map/all_gather | solution.py:184
  7.2 1.1 copy-start
  8.3 0.7 copy-start.3
  8.9 7.5 %copy-start.9 = (bf16[36,1152]{1,0:T(8,128)(2,1)S(1)}, bf16[36,1152]{1,0:T(8,128)(2,1)}, u32[]{:S(2)}) copy-start(bf16[36,1152]{1,0:T(8,128)(2,1)} %param.10) | copy-start | bytes 248836
  10.1 129.7 %reduce-scatter.2.cloned.1.call-start = ((), (), s32[]{:S(2)}) async-start(), calls=%async_computation.6 | async-start | bytes 2654208 | tf_op jit(solution)/shard_map/reduce_scatter | solution.py:224
  10.1 1.1 copy-start.1
  11.2 0.7 copy-start.4
  12.1 29.0 %collective-permute-start = (bf16[128,1152]{1,0:T(8,128)(2,1)S(1)}, bf16[128,1152]{1,0:T(8,128)(2,1)S(1)}, u32[]{:S(2)}, u32[]{:S(2)}) collective-permute-start(bf16[128,1152]{1,0:T(8,128)(2,1)S(1)} %shard_map.86.refs_1_), channel_id=1, source_target_pairs={{0,256},{256,0},{1,257},{257,1},{2,258},{258,2},{3,259},{259,3},{4... | collective-permute-start | bytes 884744 | tf_op jit(solution)/shard_map/ppermute | solution.py:22
  60.9 5.6 %collective-permute-start.1 = (bf16[1152,640]{1,0:T(8,128)(2,1)S(1)}, bf16[1152,640]{1,0:T(8,128)(2,1)}, u32[]{:S(2)}, u32[]{:S(2)}) collective-permute-start(bf16[1152,640]{1,0:T(8,128)(2,1)S(1)} %bitcast.12), channel_id=1, source_target_pairs={{0,1},{1,0},{2,3},{3,2},{4,5},{5,4},{6,7},{7,6},{8,9},{9,8},{10,11... | collective-permute-start | bytes 4423688 | tf_op jit(solution)/shard_map/ppermute | solution.py:22
  66.5 1.7 %copy-start.6 = (bf16[1024,1152]{1,0:T(8,128)(2,1)S(1)}, bf16[1024,1152]{1,0:T(8,128)(2,1)}, u32[]{:S(2)}) copy-start(bf16[1024,1152]{1,0:T(8,128)(2,1)} %all-gather.4.cloned.1.call-done.text_hbm) | copy-start | bytes 7077892
  73.4 2.4 %copy-start.7 = (bf16[576,1152]{1,0:T(8,128)(2,1)}, bf16[576,1152]{1,0:T(8,128)(2,1)S(1)}, u32[]{:S(2)}) copy-start(bf16[576,1152]{1,0:T(8,128)(2,1)S(1)} %get-tuple-element.22) | copy-start | bytes 3981316
  75.8 1.3 copy-start.8
  77.2 5.1 %collective-permute-start.2 = (bf16[576,1152]{1,0:T(8,128)(2,1)S(1)}, bf16[576,1152]{1,0:T(8,128)(2,1)S(1)}, u32[]{:S(2)}, u32[]{:S(2)}) collective-permute-start(bf16[576,1152]{1,0:T(8,128)(2,1)S(1)} %copy-done.8), channel_id=1, source_target_pairs={{0,1},{1,0},{2,3},{3,2},{4,5},{5,4},{6,7},{7,6},{8,9},{9,8},{10,11... | collective-permute-start | bytes 3981320 | tf_op jit(solution)/shard_map/ppermute | solution.py:22
  104.5 35.4 %copy-start.5 = (s32[128]{0:T(128)S(1)}, s32[128]{0:T(128)}, u32[]{:S(2)}) copy-start(s32[128]{0:T(128)} %param.9) | copy-start | bytes 1540
  139.8 1.0 copy-start.2
Sparse Core Ops, SparseCore 0:
  10.2 48.9 all-gather.3
  76.0 42.9 reduce-scatter.1

commit v5 on v4

--- a/solution.py
+++ b/solution.py
@@ -40,15 +40,12 @@
     return tn((spots == chosen_ref[...]).astype(BF16), cand_ref[...])
 
 
-def text_kernel(chosen_ref, cand_ref, unit_ref, norm_ref):
-    texts = pick_rows(chosen_ref, cand_ref)
+def pick_kernel(chosen_ref, text_cand_ref, image_cand_ref, unit_ref, norm_ref, picked_ref):
+    texts = pick_rows(chosen_ref, text_cand_ref)
     norm = jnp.sqrt(jnp.sum(texts * texts, axis=1, keepdims=True) + EPS)
     unit_ref[...] = (texts / norm).astype(BF16)
     norm_ref[...] = norm
-
-
-def image_kernel(chosen_ref, cand_ref, out_ref):
-    out_ref[...] = pick_rows(chosen_ref, cand_ref).astype(BF16)
+    picked_ref[...] = pick_rows(chosen_ref, image_cand_ref).astype(BF16)
 
 
 def pair_kernel(blocks, spot_ref, mine_ref, there_ref, images_ref, cols_mine_ref, cols_other_ref, flat_ref, group_ref):
@@ -70,10 +67,8 @@
     out_ref[...] = nn(images_ref[...], mine_ref[...])
 
 
-def main_kernel(scal_ref, spot_ref, images_ref, half_ref, other_ref, cols_ref, text_hbm, send_ref, back_ref, unit_ref, grad_ref,
-                text_ref, proj_ref, total_ref, sem):
-    load = pltpu.make_async_copy(text_hbm, text_ref, sem)
-    load.start()
+def main_kernel(scal_ref, spot_ref, images_ref, half_ref, other_ref, cols_ref, text_ref, send_ref, back_ref, unit_ref, grad_ref,
+                proj_ref):
     temper, offset, factor = scal_ref[0], scal_ref[1], scal_ref[2]
     rows, width = proj_ref.shape
     first = spot_ref[2] == 0
@@ -88,7 +83,6 @@
     row_id = lax.broadcasted_iota(jnp.int32, (rows, CHUNK), 0) - spot_ref[0]
     col_id = lax.broadcasted_iota(jnp.int32, (rows, CHUNK), 1) - spot_ref[1]
     inside = (row_id >= 0) & (row_id < pair)
-    load.wait()
     for k in range(text_ref.shape[0] // CHUNK):
         block = slice(k * CHUNK, (k + 1) * CHUNK)
         text = text_ref[block, :]
@@ -96,11 +90,7 @@
         sign = jnp.where(inside & (col_id + k * CHUNK == row_id), 1.0, -1.0)
         grad = (-factor * sign / (1.0 + jnp.exp(sign * logits))).astype(BF16)
         grad_ref[:, block] = grad
-        if k == 0:
-            total_ref[...] = nn(grad, text)
-        else:
-            total_ref[...] += nn(grad, text)
-    image_back = temper * total_ref[...]
+    image_back = temper * nn(grad_ref[...], text_ref[...])
     unit_float = unit.astype(F32)
     radial = jnp.sum(unit_float * image_back, axis=1, keepdims=True)
     back = ((image_back - unit_float * radial) / norm).astype(BF16)
@@ -149,10 +139,15 @@
     back = back_ref[...].astype(F32)
     unit = unit_ref[...].astype(F32)
     radial = jnp.sum(unit * back, axis=1, keepdims=True)
-    rows = (back - unit * radial) / norm_ref[...]
-    spots = lax.broadcasted_iota(jnp.int32, (out_ref.shape[0], rows.shape[0]), 0)
-    here = (spots == chosen_ref[...]).astype(F32)
-    out_ref[...] = jnp.dot(here, rows, precision=lax.Precision.HIGHEST, preferred_element_type=F32)
+    rest = (back - unit * radial) / norm_ref[...]
+    spots = lax.broadcasted_iota(jnp.int32, (out_ref.shape[0], rest.shape[0]), 0)
+    here = (spots == chosen_ref[...]).astype(BF16)
+    placed = None
+    for _ in range(3):
+        part = rest.astype(BF16)
+        rest = rest - part.astype(F32)
+        placed = nn(here, part) if placed is None else placed + nn(here, part)
+    out_ref[...] = placed
 
 
 def call(kernel, outs, in_specs, out_specs, scratch=(), cost=0):
@@ -178,17 +173,16 @@
     spot = jnp.stack([my_zl * pairs, my_y * pairs, core])
     scalars = jnp.stack([logit_temp[0], logit_offset[0], loss_scale[0] / total])
 
-    text_unit, txt_norm = call(
-        text_kernel, [((pairs, width), BF16), ((pairs, 1), F32)], [VMEM, VMEM], (VMEM, VMEM), cost=2 * pairs * cands * width,
-    )(selection[None, :], text_cand)
+    both = lax.all_gather(head_weight, "c", axis=0, tiled=True)
+    both, selection = lax.optimization_barrier((both, selection))
+    chosen = selection[None, :]
+    text_unit, txt_norm, picked = call(
+        pick_kernel, [((pairs, width), BF16), ((pairs, 1), F32), ((pairs, depth), BF16)], [VMEM] * 3, (VMEM,) * 3,
+        cost=2 * pairs * cands * (width + depth),
+    )(chosen, text_cand, image_cand)
     text_all = lax.all_gather(text_unit, "y", axis=0, tiled=True)
-
-    (picked,) = call(
-        image_kernel, [((pairs, depth), BF16)], [VMEM, VMEM], (VMEM,), cost=2 * pairs * cands * depth,
-    )(selection[None, :], image_cand)
     there = hop(picked, "zl", 1)
 
-    both = lax.all_gather(head_weight, "c", axis=0, tiled=True)
     part = lax.dynamic_slice(both, (0, core * (width - WIDE)), (2 * own_rows, WIDE))
     slab = lax.all_gather(part, "zh", axis=0, tiled=True)
     slab, there = lax.optimization_barrier((slab, there))
@@ -196,6 +190,7 @@
     mine = slabs.reshape(depth, WIDE)
     other = hop(mine, "c", 1)
 
+    there, text_all = lax.optimization_barrier((there, text_all))
     blocks = depth // own_rows
     images, cols_mine, cols_other = call(
         lambda *refs: pair_kernel(blocks, *refs),
@@ -210,23 +205,22 @@
     send, proj_back, image_unit, grad_tile = call(
         main_kernel,
         [((depth // 2, width), BF16), ((rows, width), BF16), ((rows, width), BF16), ((rows, n_y * pairs), BF16)],
-        [SMEM, SMEM, VMEM, VMEM, VMEM, VMEM, HBM], (VMEM,) * 4,
-        [pltpu.VMEM((n_y * pairs, width), BF16), pltpu.VMEM((rows, width), F32), pltpu.VMEM((rows, width), F32),
-         pltpu.SemaphoreType.DMA],
+        [SMEM, SMEM] + [VMEM] * 5, (VMEM,) * 4, [pltpu.VMEM((rows, width), F32)],
         cost=5 * rows * n_y * pairs * width,
     )(scalars, spot, images, half, other, cols_other, text_all)
+    got = hop(send, "c", 1)
+    got, grad_tile = lax.optimization_barrier((got, grad_tile))
+    head = (nn(cols_mine, proj_back) + got.astype(F32)).astype(BF16)
     (text_part,) = call(
         part_kernel, [((n_y * pairs, width), BF16)], [SMEM, VMEM, VMEM], (HBM,),
         [pltpu.VMEM((n_y * pairs, width), BF16), pltpu.SemaphoreType.DMA((n_y * pairs // CHUNK,))],
         cost=2 * rows * n_y * pairs * width,
     )(scalars, grad_tile, image_unit)
 
+    head, text_part = lax.optimization_barrier((head, text_part))
     text_back = lax.psum_scatter(text_part.reshape(n_y, pairs, width), "y", scatter_dimension=0)
-    got = hop(send, "c", 1)
-    head = nn(cols_mine, proj_back) + got.astype(F32)
-
     share = depth // 2 // n_x
-    came = lax.all_to_all(head.astype(BF16).reshape(n_x, share, width), "x", 0, 0)
+    came = lax.all_to_all(head.reshape(n_x, share, width), "x", 0, 0)
     n_z = lax.axis_size(("zh", "zl"))
     piece = share // n_z
     strips = piece * (width // LANES)
@@ -240,11 +234,12 @@
     came = lax.all_to_all(jnp.broadcast_to(head[None], (n_y,) + head.shape), "y", 0, 0)
     (head,) = call(unfold_kernel, [((piece, width), F32)], [VMEM], (VMEM,), [pltpu.VMEM((strips, LANES), F32)])(came)
 
+    there = hop(head, "zl", 1)
     (text_grad,) = call(
-        place_kernel, [((cands, width), F32)], [VMEM] * 4, (VMEM,), cost=12 * cands * pairs * width,
-    )(selection[None, :], text_back, text_unit, txt_norm)
-    head, text_grad = lax.optimization_barrier((head, text_grad))
-    head_grad = lax.all_gather(head, "zl", axis=0, tiled=True)
+        place_kernel, [((cands, width), F32)], [VMEM] * 4, (VMEM,), cost=6 * cands * pairs * width,
+    )(chosen, text_back, text_unit, txt_norm)
+    there, text_grad = lax.optimization_barrier((there, text_grad))
+    head_grad = jnp.concatenate([jnp.where(my_zl == 0, head, there), jnp.where(my_zl == 0, there, head)], axis=0)
     return head_grad, text_grad
 
 

time: 158 us -> 154 us (0.975)
  local copies, waits for them, and re-layouts: 8.25 us -> 4.94 us
  starting transfers between devices: 8.66 us -> 11.1 us
  blocking collectives: 106 us -> 104 us
    all_gather x1 -> x0, blocking collectives: 5.41 us -> none  [shards(): head_grad = lax.all_gather(head, 'zl', axis=0, tiled=True)]
    unnamed x22 -> x12, local copies, waits for them, and re-layouts: 8.08 us -> 4.72 us
    all_gather x1, blocking collectives: 22.7 us -> 25.2 us  [shards(): slab = lax.all_gather(part, 'zh', axis=0, tiled=True)]
    ppermute x3 -> x4, starting transfers between devices: 8.58 us -> 11 us  [hop(): lax.ppermute(value, axis, [(s, (s + steps) % count) for s in range(count)])]
    pallas_call x3 -> x2, Pallas kernels: 4.68 us -> 3.92 us  [the longest x1 2.8 us: shards(): call(place_kernel, [((cands, width), F32)], [VMEM] * 4, (VMEM,), cost=6 *...]
  transfers between devices with their start and end apart: 5 -> 6, of which waited for: 1 -> 2; matrix products, arithmetic and copies ran while one was open for 1% -> 0% of each run, Pallas kernels for 1% -> 3%
where the time goes in v5:
time: 154 us; the launch traced here: 153 us
  blocking collectives  104 us (68%)
  between operations  16.2 us (11%)
  Pallas kernels  12.9 us (8%)
  starting transfers between devices  11.1 us (7%)
  local copies, waits for them, and re-layouts  4.94 us (3%)
  waiting for transfers between devices  3.12 us (2%)
    all_gather x1, blocking collectives, shards(): slab = lax.all_gather(part, 'zh', axis=0, tiled=True)  25.2 us
    all_to_all x1, blocking collectives, shards(): came = lax.all_to_all(head.reshape(n_x, share, width), 'x', 0, 0)  21.3 us
    all_to_all x1, blocking collectives, shards(): lax.all_to_all(jnp.broadcast_to(slab[None], (n_x,) + slab.shape), 'x', 0, 0)  19.7 us
    all_to_all x1, blocking collectives, shards(): lax.all_to_all(jnp.broadcast_to(head[None], (n_y,) + head.shape), 'y', 0, 0)  18 us
    all_to_all x1, blocking collectives, shards(): came = lax.all_to_all(folded, ('zh', 'zl'), 0, 0)  17.3 us
    ppermute x4, starting transfers between devices, hop(): lax.ppermute(value, axis, [(s, (s + steps) % count) for s in range(count)])  11 us
    unnamed x12, local copies, waits for them, and re-layouts  4.72 us
    pallas_call x1, Pallas kernels, shards(): call(main_kernel, [((depth // 2, width), BF16), ((rows, width), BF16), ((...  4.62 us
  transfers between devices with their start and end apart: 6, of which 2 were waited for; matrix products, arithmetic and copies ran while one was open for 0% of the time, Pallas kernels for 3%

profile of v5, /device:TPU:2, one launch (start us, length us, event | category | flops | bytes accessed | tf_op | source)
XLA Modules:
  0.0 153.3 jit_solution(14155723528697290757)
XLA Ops:
  7.2 0.0 all-gather.3.cloned.1.call-start
  7.2 2.1 %all-gather = bf16[2,36,1152]{2,1,0:T(8,128)(2,1)S(1)} all-gather(bf16[1,36,1152]{2,1,0:T(8,128)(2,1)} %bitcast.17), channel_id=1, replica_groups=mesh['zl'=2,'y'=8,'x'=4,'zh'=4,'c'=2] {'c'}, dimensions={0}, use_global_device_ids=true | all-gather | bytes 248832 | tf_op jit(solution)/shard_map/all_gather | solution.py:176
  9.4 0.0 copy-start
  9.4 1.1 copy-done
  10.5 0.0 copy-start.1
  10.5 1.1 copy-done.1
  11.5 0.0 copy-start.3
  11.5 0.7 copy-done.3
  12.2 1.1 shard_map.86
  13.3 0.0 all-gather.3.cloned.1.call-update
  13.3 0.0 reduce-scatter.2.cloned.1.call-start
  13.4 4.3 %collective-permute-start = (bf16[128,1152]{1,0:T(8,128)(2,1)S(1)}, bf16[128,1152]{1,0:T(8,128)(2,1)S(1)}, u32[]{:S(2)}, u32[]{:S(2)}) collective-permute-start(bf16[128,1152]{1,0:T(8,128)(2,1)S(1)} %get-tuple-element.25.refs_1_), channel_id=1, source_target_pairs={{0,256},{256,0},{1,257},{257,1},{2,258},{258,2},{3,259},{259,3},{4... | collective-permute-start | bytes 884744 | tf_op jit(solution)/shard_map/ppermute | solution.py:22
  17.7 25.2 %all_gather.10 = bf16[288,640]{1,0:T(8,128)(2,1)S(1)} all-gather(bf16[72,640]{1,0:T(8,128)(2,1)S(1)} %constant_dynamic-slice_fusion), channel_id=1, replica_groups=mesh['zl'=2,'y'=8,'x'=4,'zh'=4,'c'=2] {'zh'}, dimensions={0}, use_global_device_ids=true | all-gather | bytes 460800 | tf_op jit(solution)/shard_map/all_gather | solution.py:187
  42.9 0.0 collective-permute-done.refs_2_
  42.9 0.1 broadcast_in_dim.7
  43.0 19.7 %all_to_all.20 = bf16[4,288,640]{2,1,0:T(8,128)(2,1)S(1)} all-to-all(bf16[4,288,640]{2,1,0:T(8,128)(2,1)S(1)} %broadcast_in_dim.7), channel_id=1, replica_groups=mesh['zl'=2,'y'=8,'x'=4,'zh'=4,'c'=2] {'x'}, dimensions={0} | all-to-all | bytes 2949120 | tf_op jit(solution)/shard_map/all_to_all | solution.py:189
  62.7 1.9 %collective-permute-start.1 = (bf16[1152,640]{1,0:T(8,128)(2,1)S(1)}, bf16[1152,640]{1,0:T(8,128)(2,1)}, u32[]{:S(2)}, u32[]{:S(2)}) collective-permute-start(bf16[1152,640]{1,0:T(8,128)(2,1)S(1)} %bitcast.11), channel_id=1, source_target_pairs={{0,1},{1,0},{2,3},{3,2},{4,5},{5,4},{6,7},{7,6},{8,9},{9,8},{10,11... | collective-permute-start | bytes 4423688 | tf_op jit(solution)/shard_map/ppermute | solution.py:22
  66.6 0.1 pad_maximum_fusion.1.scal_ref
  66.6 0.1 pad_add_fusion.refs_0_.spot_ref
  66.7 0.0 all-gather.3.cloned.1.call-done.text_ref
  66.7 0.9 shard_map.87
  67.6 0.0 copy-start.5
  67.6 0.7 shard_map.88.half_ref
  68.3 0.0 collective-permute-done.1.other_ref
  68.3 1.0 copy-done.5
  69.3 4.6 %shard_map.89 = (bf16[576,1152]{1,0:T(8,128)(2,1)S(1)}, bf16[256,1152]{1,0:T(8,128)(2,1)S(1)}, bf16[256,1152]{1,0:T(8,128)(2,1)S(1)}, bf16[256,1024]{1,0:T(8,128)(2,1)S(1)}) custom-call(f32[3]{0:T(128)S(1)} %pad_maximum_fusion.1.scal_ref, s32[3]{0:T(128)S(1)} %pad_add_fusion.refs_0_.spot_ref, bf16[256,1152]{1,0:T(8,128)(2,1)S(1)} %get-tuple-element.31.images_ref, ...), custom_call_target="tpu_custom_call" | custom-call | flops 1509949440 | bytes 2000000 | tf_op jit(solution)/shard_map/pallas_call | solution.py:205
  73.9 2.4 %collective-permute-start.2 = (bf16[576,1152]{1,0:T(8,128)(2,1)S(1)}, bf16[576,1152]{1,0:T(8,128)(2,1)S(1)}, u32[]{:S(2)}, u32[]{:S(2)}) collective-permute-start(bf16[576,1152]{1,0:T(8,128)(2,1)S(1)} %get-tuple-element.36), channel_id=1, source_target_pairs={{0,1},{1,0},{2,3},{3,2},{4,5},{5,4},{6,7},{7,6},{8,9},{9,8},{10,11... | collective-permute-start | bytes 3981320 | tf_op jit(solution)/shard_map/ppermute | solution.py:22
  76.3 2.7 %collective-permute-done.2 = bf16[576,1152]{1,0:T(8,128)(2,1)S(1)} collective-permute-done((bf16[576,1152]{1,0:T(8,128)(2,1)S(1)}, bf16[576,1152]{1,0:T(8,128)(2,1)S(1)}, u32[]{:S(2)}, u32[]{:S(2)}) %collective-permute-start.2) | collective-permute-done | bytes 1327136 | tf_op jit(solution)/shard_map/ppermute | solution.py:22
  79.0 2.4 %shard_map.90 = bf16[1024,1152]{1,0:T(8,128)(2,1)} custom-call(f32[3]{0:T(128)S(1)} %pad_maximum_fusion.1.scal_ref, bf16[256,1024]{1,0:T(8,128)(2,1)S(1)} %get-tuple-element.39.grad_ref, bf16[256,1152]{1,0:T(8,128)(2,1)S(1)} %get-tuple-element.40.unit_ref), custom_call_target="tpu_custom_call" | custom-call | flops 603979776 | bytes 2000000 | tf_op jit(solution)/shard_map/pallas_call | solution.py:214
  81.4 0.6 fusion
  82.0 0.0 reduce-scatter.2.cloned.1.call-update
  82.0 21.3 %all_to_all.21.came_ref = bf16[4,144,1152]{2,1,0:T(8,128)(2,1)S(1)} all-to-all(bf16[4,144,1152]{2,1,0:T(8,128)(2,1)S(1)} %bitcast.16), channel_id=1, replica_groups=mesh['zl'=2,'y'=8,'x'=4,'zh'=4,'c'=2] {'x'}, dimensions={0} | all-to-all | bytes 2654208 | tf_op jit(solution)/shard_map/all_to_all | solution.py:223
  103.3 0.4 shard_map.91
  103.7 0.0 copy-start.4
  103.7 17.3 %all_to_all.22 = bf16[8,168,128]{2,1,0:T(8,128)(2,1)S(1)} all-to-all(bf16[8,168,128]{2,1,0:T(8,128)(2,1)S(1)} %shard_map.91), channel_id=1, replica_groups=mesh['zl'=2,'y'=8,'x'=4,'zh'=4,'c'=2] {'zh','zl'}, dimensions={0} | all-to-all | bytes 688128 | tf_op jit(solution)/shard_map/all_to_all | solution.py:232
  121.0 0.1 reduce_sum.12
  121.1 18.0 %all_to_all.23.came_ref = bf16[8,168,128]{2,1,0:T(8,128)(2,1)S(1)} all-to-all(bf16[8,168,128]{2,1,0:T(8,128)(2,1)S(1)} %broadcast_in_dim.8), channel_id=1, replica_groups=mesh['zl'=2,'y'=8,'x'=4,'zh'=4,'c'=2] {'y'}, dimensions={0} | all-to-all | bytes 688128 | tf_op jit(solution)/shard_map/all_to_all | solution.py:234
  139.0 0.1 shard_map.92
  139.1 2.4 %collective-permute-start.3 = (f32[18,1152]{1,0:T(8,128)S(1)}, f32[18,1152]{1,0:T(8,128)S(1)}, u32[]{:S(2)}, u32[]{:S(2)}) collective-permute-start(f32[18,1152]{1,0:T(8,128)S(1)} %shard_map.92), channel_id=1, source_target_pairs={{0,256},{256,0},{1,257},{257,1},{2,258},{258,2},{3,259},{259,3},{4... | collective-permute-start | bytes 248840 | tf_op jit(solution)/shard_map/ppermute | solution.py:22
  141.5 0.0 reduce-scatter.2.cloned.1.call-done
  141.6 0.0 copy-done.4
  141.6 0.0 copy-start.2
  141.6 1.0 copy-done.2
  142.6 2.8 %shard_map.93 = f32[256,1152]{1,0:T(8,128)} custom-call(s32[1,128]{1,0:T(1,128)S(1)} %bitcast.15, bf16[128,1152]{1,0:T(8,128)(2,1)S(1)} %bitcast.13, bf16[128,1152]{1,0:T(8,128)(2,1)} %get-tuple-element.28.unit_ref, f32[128,1]{1,0:T(8,128)S(1)} %get-tuple-element.43.norm_ref), custom_call_target="tpu_custom_call" | custom-call | flops 226492416 | bytes 2000000 | tf_op jit(solution)/shard_map/pallas_call | solution.py:238
  145.4 0.4 collective-permute-done.3
  145.8 0.7 pad_maximum_fusion
  (4 shorter events, 0.1 us)
Async XLA Ops:
  7.2 59.6 %all-gather.3.cloned.1.call-start = ((), (), s32[]{:S(2)}) async-start(), calls=%async_computation.5 | async-start | bytes 2654208 | tf_op jit(solution)/shard_map/all_gather | solution.py:183
  9.4 1.1 copy-start
  10.5 1.1 copy-start.1
  11.5 0.7 copy-start.3
  13.3 128.2 %reduce-scatter.2.cloned.1.call-start = ((), (), s32[]{:S(2)}) async-start(), calls=%async_computation.6 | async-start | bytes 2654208 | tf_op jit(solution)/shard_map/reduce_scatter | solution.py:221
  13.4 29.5 %collective-permute-start = (bf16[128,1152]{1,0:T(8,128)(2,1)S(1)}, bf16[128,1152]{1,0:T(8,128)(2,1)S(1)}, u32[]{:S(2)}, u32[]{:S(2)}) collective-permute-start(bf16[128,1152]{1,0:T(8,128)(2,1)S(1)} %get-tuple-element.25.refs_1_), channel_id=1, source_target_pairs={{0,256},{256,0},{1,257},{257,1},{2,258},{258,2},{3,259},{259,3},{4... | collective-permute-start | bytes 884744 | tf_op jit(solution)/shard_map/ppermute | solution.py:22
  62.7 5.6 %collective-permute-start.1 = (bf16[1152,640]{1,0:T(8,128)(2,1)S(1)}, bf16[1152,640]{1,0:T(8,128)(2,1)}, u32[]{:S(2)}, u32[]{:S(2)}) collective-permute-start(bf16[1152,640]{1,0:T(8,128)(2,1)S(1)} %bitcast.11), channel_id=1, source_target_pairs={{0,1},{1,0},{2,3},{3,2},{4,5},{5,4},{6,7},{7,6},{8,9},{9,8},{10,11... | collective-permute-start | bytes 4423688 | tf_op jit(solution)/shard_map/ppermute | solution.py:22
  67.6 1.7 %copy-start.5 = (bf16[1024,1152]{1,0:T(8,128)(2,1)S(1)}, bf16[1024,1152]{1,0:T(8,128)(2,1)}, u32[]{:S(2)}) copy-start(bf16[1024,1152]{1,0:T(8,128)(2,1)} %all-gather.3.cloned.1.call-done.text_ref) | copy-start | bytes 7077892
  73.9 5.1 %collective-permute-start.2 = (bf16[576,1152]{1,0:T(8,128)(2,1)S(1)}, bf16[576,1152]{1,0:T(8,128)(2,1)S(1)}, u32[]{:S(2)}, u32[]{:S(2)}) collective-permute-start(bf16[576,1152]{1,0:T(8,128)(2,1)S(1)} %get-tuple-element.36), channel_id=1, source_target_pairs={{0,1},{1,0},{2,3},{3,2},{4,5},{5,4},{6,7},{7,6},{8,9},{9,8},{10,11... | collective-permute-start | bytes 3981320 | tf_op jit(solution)/shard_map/ppermute | solution.py:22
  103.7 37.9 %copy-start.4 = (s32[128]{0:T(128)S(1)}, s32[128]{0:T(128)}, u32[]{:S(2)}) copy-start(s32[128]{0:T(128)} %param.9) | copy-start | bytes 1540
  139.1 6.6 %collective-permute-start.3 = (f32[18,1152]{1,0:T(8,128)S(1)}, f32[18,1152]{1,0:T(8,128)S(1)}, u32[]{:S(2)}, u32[]{:S(2)}) collective-permute-start(f32[18,1152]{1,0:T(8,128)S(1)} %shard_map.92), channel_id=1, source_target_pairs={{0,256},{256,0},{1,257},{257,1},{2,258},{258,2},{3,259},{259,3},{4... | collective-permute-start | bytes 248840 | tf_op jit(solution)/shard_map/ppermute | solution.py:22
  141.6 1.0 copy-start.2
Sparse Core Ops, SparseCore 0:
  13.5 48.9 all-gather.2
  82.1 42.8 reduce-scatter.1

commit v6 on v5

--- a/solution.py
+++ b/solution.py
@@ -7,13 +7,14 @@
 
 EPS = 1e-06
 ALL = ("zl", "y", "x", "zh", "c")
-WIDE = 640
+PADDED = 40
 CHUNK = 256
 VMEM = pl.BlockSpec(memory_space=pltpu.VMEM)
 SMEM = pl.BlockSpec(memory_space=pltpu.SMEM)
 HBM = pl.BlockSpec(memory_space=pltpu.HBM)
 LANES = 128
-PARAMS = pltpu.CompilerParams(vmem_limit_bytes=40 * 1024 * 1024)
+LIMIT = 40 * 1024 * 1024
+WHOLE = 61 * 1024 * 1024
 F32, BF16 = jnp.float32, jnp.bfloat16
 
 
@@ -34,48 +35,60 @@
     return lax.dot_general(a, b, (((0,), (0,)), ((), ())), preferred_element_type=F32)
 
 
-def pick_rows(chosen_ref, cand_ref):
-    pairs, cands = chosen_ref.shape[1], cand_ref.shape[0]
-    spots = lax.broadcasted_iota(jnp.int32, (cands, pairs), 0)
-    return tn((spots == chosen_ref[...]).astype(BF16), cand_ref[...])
-
-
-def pick_kernel(chosen_ref, text_cand_ref, image_cand_ref, unit_ref, norm_ref, picked_ref):
-    texts = pick_rows(chosen_ref, text_cand_ref)
+def pick_rows(chosen, cands):
+    spots = lax.broadcasted_iota(jnp.int32, (cands.shape[0], chosen.shape[1]), 0)
+    return tn((spots == chosen).astype(BF16), cands)
+
+
+def text_kernel(chosen_hbm, cand_hbm, unit_ref, norm_ref, chosen_ref, cand_ref, sem):
+    loads = [pltpu.make_async_copy(chosen_hbm, chosen_ref, sem.at[0]), pltpu.make_async_copy(cand_hbm, cand_ref, sem.at[1])]
+    for load in loads:
+        load.start()
+    for load in loads:
+        load.wait()
+    texts = pick_rows(chosen_ref[...], cand_ref[...])
     norm = jnp.sqrt(jnp.sum(texts * texts, axis=1, keepdims=True) + EPS)
     unit_ref[...] = (texts / norm).astype(BF16)
     norm_ref[...] = norm
-    picked_ref[...] = pick_rows(chosen_ref, image_cand_ref).astype(BF16)
-
-
-def pair_kernel(blocks, spot_ref, mine_ref, there_ref, images_ref, cols_mine_ref, cols_other_ref, flat_ref, group_ref):
+
+
+def image_kernel(chosen_hbm, cand_hbm, out_ref, chosen_ref, cand_ref, sem):
+    loads = [pltpu.make_async_copy(chosen_hbm, chosen_ref, sem.at[0]), pltpu.make_async_copy(cand_hbm, cand_ref, sem.at[1])]
+    for load in loads:
+        load.start()
+    for load in loads:
+        load.wait()
+    out_ref[...] = pick_rows(chosen_ref[...], cand_ref[...]).astype(BF16)
+
+
+def pair_kernel(size, spot_ref, mine_ref, there_ref, deep_mine_ref, deep_other_ref, cols_mine_ref, cols_other_ref,
+                flat_ref, group_ref, deep_ref):
     pairs, depth = mine_ref.shape
     first = spot_ref[0] == 0
-    images_ref[:pairs, :] = jnp.where(first, mine_ref[...], there_ref[...])
-    images_ref[pairs:, :] = jnp.where(first, there_ref[...], mine_ref[...])
-    flat_ref[...] = images_ref[...].astype(F32).T
-    size = depth // blocks
-    for block in range(blocks):
-        place = block // 2 * size
-        group_ref[block % 2, place:place + size, :] = flat_ref[block * size:(block + 1) * size, :]
+    mine, there = mine_ref[...].astype(F32).T, there_ref[...].astype(F32).T
+    flat_ref[:, :pairs] = jnp.where(first, mine, there)
+    flat_ref[:, pairs:] = jnp.where(first, there, mine)
+    deep_ref[...] = jnp.zeros_like(deep_ref)
+    for block in range(depth // size):
+        core, place = block % 2, block // 2
+        rows = flat_ref[block * size:(block + 1) * size, :]
+        group_ref[core, place * size:(place + 1) * size, :] = rows
+        deep_ref[core, place * PADDED:place * PADDED + size, :] = rows
     core = spot_ref[2]
     cols_mine_ref[...] = group_ref[core].astype(BF16)
     cols_other_ref[...] = group_ref[1 - core].astype(BF16)
-
-
-def half_kernel(images_ref, mine_ref, out_ref):
-    out_ref[...] = nn(images_ref[...], mine_ref[...])
-
-
-def main_kernel(scal_ref, spot_ref, images_ref, half_ref, other_ref, cols_ref, text_ref, send_ref, back_ref, unit_ref, grad_ref,
-                proj_ref):
+    deep_mine_ref[...] = deep_ref[core].T.astype(BF16)
+    deep_other_ref[...] = deep_ref[1 - core].T.astype(BF16)
+
+
+def half_kernel(deep_ref, weight_ref, out_ref):
+    out_ref[...] = nn(deep_ref[...], weight_ref[...])
+
+
+def main_kernel(scal_ref, spot_ref, deep_ref, half_ref, weight_ref, cols_ref, text_ref, send_ref, back_ref, unit_ref, grad_ref):
     temper, offset, factor = scal_ref[0], scal_ref[1], scal_ref[2]
-    rows, width = proj_ref.shape
-    first = spot_ref[2] == 0
-    proj_mine, proj_other = half_ref[...], nn(images_ref[...], other_ref[...])
-    proj_ref[:, :WIDE] = jnp.where(first, proj_mine, proj_other)
-    proj_ref[:, WIDE:] = jnp.where(first, proj_other, proj_mine)[:, 2 * WIDE - width:]
-    proj = proj_ref[...]
+    proj = half_ref[...] + nn(deep_ref[...], weight_ref[...])
+    rows = proj.shape[0]
     norm = jnp.sqrt(jnp.sum(proj * proj, axis=1, keepdims=True) + EPS)
     unit = (proj / norm).astype(BF16)
     unit_ref[...] = unit
@@ -98,12 +111,12 @@
     send_ref[...] = nn(cols_ref[...], back).astype(BF16)
 
 
-def part_kernel(scal_ref, grad_ref, unit_ref, part_hbm, part_ref, sem):
+def part_kernel(grad_ref, unit_ref, part_hbm, part_ref, sem):
     unit = unit_ref[...]
     stores = []
     for k in range(part_ref.shape[0] // CHUNK):
         block = pl.ds(k * CHUNK, CHUNK)
-        part_ref[block, :] = (scal_ref[0] * tn(grad_ref[:, k * CHUNK:(k + 1) * CHUNK], unit)).astype(BF16)
+        part_ref[block, :] = tn(grad_ref[:, k * CHUNK:(k + 1) * CHUNK], unit).astype(BF16)
         store = pltpu.make_async_copy(part_ref.at[block], part_hbm.at[block], sem.at[k])
         store.start()
         stores.append(store)
@@ -135,8 +148,8 @@
         out_ref[:, t * LANES:(t + 1) * LANES] = sum_ref[t * size:(t + 1) * size, :]
 
 
-def place_kernel(chosen_ref, back_ref, unit_ref, norm_ref, out_ref):
-    back = back_ref[...].astype(F32)
+def place_kernel(scal_ref, chosen_ref, back_ref, unit_ref, norm_ref, out_ref):
+    back = scal_ref[0] * back_ref[...].astype(F32)
     unit = unit_ref[...].astype(F32)
     radial = jnp.sum(unit * back, axis=1, keepdims=True)
     rest = (back - unit * radial) / norm_ref[...]
@@ -150,14 +163,14 @@
     out_ref[...] = placed
 
 
-def call(kernel, outs, in_specs, out_specs, scratch=(), cost=0):
+def call(kernel, outs, in_specs, out_specs, scratch=(), cost=0, limit=LIMIT):
     return pl.pallas_call(
         kernel,
         out_shape=tuple(jax.ShapeDtypeStruct(shape, dtype) for shape, dtype in outs),
         in_specs=in_specs,
         out_specs=out_specs,
         scratch_shapes=list(scratch),
-        compiler_params=PARAMS,
+        compiler_params=pltpu.CompilerParams(vmem_limit_bytes=limit),
         cost_estimate=pl.CostEstimate(flops=cost, bytes_accessed=2_000_000, transcendentals=0),
     )
 
@@ -173,49 +186,51 @@
     spot = jnp.stack([my_zl * pairs, my_y * pairs, core])
     scalars = jnp.stack([logit_temp[0], logit_offset[0], loss_scale[0] / total])
 
-    both = lax.all_gather(head_weight, "c", axis=0, tiled=True)
-    both, selection = lax.optimization_barrier((both, selection))
     chosen = selection[None, :]
-    text_unit, txt_norm, picked = call(
-        pick_kernel, [((pairs, width), BF16), ((pairs, 1), F32), ((pairs, depth), BF16)], [VMEM] * 3, (VMEM,) * 3,
-        cost=2 * pairs * cands * (width + depth),
-    )(chosen, text_cand, image_cand)
+    pick_scratch = [pltpu.VMEM((1, pairs), jnp.int32), pltpu.VMEM((cands, depth), BF16), pltpu.SemaphoreType.DMA((2,))]
+    text_unit, txt_norm = call(
+        text_kernel, [((pairs, width), BF16), ((pairs, 1), F32)], [HBM, HBM], (VMEM, VMEM), pick_scratch,
+        cost=2 * pairs * cands * width, limit=WHOLE,
+    )(chosen, text_cand)
     text_all = lax.all_gather(text_unit, "y", axis=0, tiled=True)
+
+    part = jnp.pad(head_weight, ((0, PADDED - own_rows), (0, 0)))
+    slab = lax.all_gather(part, "zh", axis=0, tiled=True)
+    (picked,) = call(
+        image_kernel, [((pairs, depth), BF16)], [HBM, HBM], (VMEM,), pick_scratch, cost=2 * pairs * cands * depth, limit=WHOLE,
+    )(chosen, image_cand)
+    slab, picked = lax.optimization_barrier((slab, picked))
     there = hop(picked, "zl", 1)
-
-    part = lax.dynamic_slice(both, (0, core * (width - WIDE)), (2 * own_rows, WIDE))
-    slab = lax.all_gather(part, "zh", axis=0, tiled=True)
-    slab, there = lax.optimization_barrier((slab, there))
     slabs = lax.all_to_all(jnp.broadcast_to(slab[None], (n_x,) + slab.shape), "x", 0, 0)
-    mine = slabs.reshape(depth, WIDE)
+    mine = slabs.reshape(n_x * slab.shape[0], width)
+    mine, there = lax.optimization_barrier((mine, there))
     other = hop(mine, "c", 1)
 
     there, text_all = lax.optimization_barrier((there, text_all))
-    blocks = depth // own_rows
-    images, cols_mine, cols_other = call(
-        lambda *refs: pair_kernel(blocks, *refs),
-        [((rows, depth), BF16), ((depth // 2, rows), BF16), ((depth // 2, rows), BF16)],
-        [SMEM, VMEM, VMEM], (VMEM, VMEM, VMEM),
-        [pltpu.VMEM((depth, rows), F32), pltpu.VMEM((2, depth // 2, rows), F32)],
+    deep = mine.shape[0]
+    deep_mine, deep_other, cols_mine, cols_other = call(
+        lambda *refs: pair_kernel(own_rows, *refs),
+        [((rows, deep), BF16), ((rows, deep), BF16), ((depth // 2, rows), BF16), ((depth // 2, rows), BF16)],
+        [SMEM, VMEM, VMEM], (VMEM,) * 4,
+        [pltpu.VMEM((depth, rows), F32), pltpu.VMEM((2, depth // 2, rows), F32), pltpu.VMEM((2, deep, rows), F32)],
     )(spot, picked, there)
-
     (half,) = call(
-        half_kernel, [((rows, WIDE), F32)], [VMEM, VMEM], (VMEM,), cost=2 * rows * depth * WIDE,
-    )(images, mine)
+        half_kernel, [((rows, width), F32)], [VMEM, VMEM], (VMEM,), cost=2 * rows * deep * width,
+    )(deep_mine, mine)
     send, proj_back, image_unit, grad_tile = call(
         main_kernel,
         [((depth // 2, width), BF16), ((rows, width), BF16), ((rows, width), BF16), ((rows, n_y * pairs), BF16)],
-        [SMEM, SMEM] + [VMEM] * 5, (VMEM,) * 4, [pltpu.VMEM((rows, width), F32)],
+        [SMEM, SMEM] + [VMEM] * 5, (VMEM,) * 4,
         cost=5 * rows * n_y * pairs * width,
-    )(scalars, spot, images, half, other, cols_other, text_all)
+    )(scalars, spot, deep_other, half, other, cols_other, text_all)
     got = hop(send, "c", 1)
     got, grad_tile = lax.optimization_barrier((got, grad_tile))
     head = (nn(cols_mine, proj_back) + got.astype(F32)).astype(BF16)
     (text_part,) = call(
-        part_kernel, [((n_y * pairs, width), BF16)], [SMEM, VMEM, VMEM], (HBM,),
+        part_kernel, [((n_y * pairs, width), BF16)], [VMEM, VMEM], (HBM,),
         [pltpu.VMEM((n_y * pairs, width), BF16), pltpu.SemaphoreType.DMA((n_y * pairs // CHUNK,))],
         cost=2 * rows * n_y * pairs * width,
-    )(scalars, grad_tile, image_unit)
+    )(grad_tile, image_unit)
 
     head, text_part = lax.optimization_barrier((head, text_part))
     text_back = lax.psum_scatter(text_part.reshape(n_y, pairs, width), "y", scatter_dimension=0)
@@ -236,8 +251,8 @@
 
     there = hop(head, "zl", 1)
     (text_grad,) = call(
-        place_kernel, [((cands, width), F32)], [VMEM] * 4, (VMEM,), cost=6 * cands * pairs * width,
-    )(chosen, text_back, text_unit, txt_norm)
+        place_kernel, [((cands, width), F32)], [SMEM] + [VMEM] * 4, (VMEM,), cost=6 * cands * pairs * width,
+    )(scalars, chosen, text_back, text_unit, txt_norm)
     there, text_grad = lax.optimization_barrier((there, text_grad))
     head_grad = jnp.concatenate([jnp.where(my_zl == 0, head, there), jnp.where(my_zl == 0, there, head)], axis=0)
     return head_grad, text_grad

time: 154 us -> 147 us (0.955)
  blocking collectives: 104 us -> 78.2 us
  waiting for transfers between devices: 3.12 us -> 16.9 us
  starting transfers between devices: 11.1 us -> 14.8 us
  Pallas kernels: 12.9 us -> 14.8 us
    all_to_all x1 -> x0, blocking collectives: 19.7 us -> none  [shards(): lax.all_to_all(jnp.broadcast_to(slab[None], (n_x,) + slab.shape), 'x', 0, 0)]
    all_to_all x0 -> x1, waiting for transfers between devices: none -> 7.91 us  [shards(): lax.all_to_all(jnp.broadcast_to(slab[None], (n_x,) + slab.shape), 'x', 0, 0)]
    ppermute x4, waiting for transfers between devices: 3.06 us -> 8.96 us  [hop(): lax.ppermute(value, axis, [(s, (s + steps) % count) for s in range(count)])]
    all_to_all x0 -> x1, starting transfers between devices: none -> 4.96 us  [shards(): lax.all_to_all(jnp.broadcast_to(slab[None], (n_x,) + slab.shape), 'x', 0, 0)]
    all_gather x1, blocking collectives: 25.2 us -> 20.6 us  [shards(): slab = lax.all_gather(part, 'zh', axis=0, tiled=True)]
    unnamed x12, local copies, waits for them, and re-layouts: 4.72 us -> 1.95 us
    pallas_call x5 -> x6, Pallas kernels: 7.88 us -> 10.6 us  [the longest x1 2.42 us: shards(): call(place_kernel, [((cands, width), F32)], [SMEM] + [VMEM] * 4, (VMEM,),...]
    all_to_all x1, blocking collectives: 17.3 us -> 19.6 us  [shards(): came = lax.all_to_all(folded, ('zh', 'zl'), 0, 0)]
  transfers between devices with their start and end apart: 6 -> 7, of which waited for: 2 -> 4; matrix products, arithmetic and copies ran while one was open for 0% -> 2% of each run, Pallas kernels for 3% -> 5%
where the time goes in v6:
time: 147 us
  blocking collectives  78.2 us (53%)
  waiting for transfers between devices  16.9 us (11%)
  between operations  16.2 us (11%)
  starting transfers between devices  14.8 us (10%)
  Pallas kernels  14.8 us (10%)
  local copies, waits for them, and re-layouts  4.11 us (3%)
    all_to_all x1, blocking collectives, shards(): came = lax.all_to_all(head.reshape(n_x, share, width), 'x', 0, 0)  21.3 us
    all_gather x1, blocking collectives, shards(): slab = lax.all_gather(part, 'zh', axis=0, tiled=True)  20.6 us
    all_to_all x1, blocking collectives, shards(): came = lax.all_to_all(folded, ('zh', 'zl'), 0, 0)  19.6 us
    all_to_all x1, blocking collectives, shards(): lax.all_to_all(jnp.broadcast_to(head[None], (n_y,) + head.shape), 'y', 0, 0)  16.7 us
    ppermute x4, starting transfers between devices, hop(): lax.ppermute(value, axis, [(s, (s + steps) % count) for s in range(count)])  9.8 us
    ppermute x4, waiting for transfers between devices, hop(): lax.ppermute(value, axis, [(s, (s + steps) % count) for s in range(count)])  8.96 us
    all_to_all x1, waiting for transfers between devices, shards(): lax.all_to_all(jnp.broadcast_to(slab[None], (n_x,) + slab.shape), 'x', 0, 0)  7.91 us
    all_to_all x1, starting transfers between devices, shards(): lax.all_to_all(jnp.broadcast_to(slab[None], (n_x,) + slab.shape), 'x', 0, 0)  4.96 us
  transfers between devices with their start and end apart: 7, of which 4 were waited for; matrix products, arithmetic and copies ran while one was open for 2% of the time, Pallas kernels for 5%

profile of v6, /device:TPU:2, one launch (start us, length us, event | category | flops | bytes accessed | tf_op | source)
XLA Modules:
  0.0 146.5 jit_solution(11607720317979297228)
XLA Ops:
  7.2 0.0 all-gather.2.cloned.1.call-start
  7.2 2.2 %shard_map.87 = (bf16[128,1152]{1,0:T(8,128)(2,1)}, f32[128,1]{1,0:T(8,128)}) custom-call(s32[1,128]{1,0:T(1,128)} %bitcast.13, bf16[256,1152]{1,0:T(8,128)(2,1)} %cand_hbm.3), custom_call_target="tpu_custom_call" | custom-call | flops 75497472 | bytes 2000000 | tf_op jit(solution)/shard_map/pallas_call | solution.py:191
  9.4 0.0 all-gather.2.cloned.1.call-update
  9.5 0.9 pad.4
  10.4 2.1 %shard_map.86.refs_1_ = bf16[128,1152]{1,0:T(8,128)(2,1)} custom-call(s32[1,128]{1,0:T(1,128)} %bitcast.14, bf16[256,1152]{1,0:T(8,128)(2,1)} %cand_hbm.2), custom_call_target="tpu_custom_call" | custom-call | flops 75497472 | bytes 2000000 | tf_op jit(solution)/shard_map/pallas_call | solution.py:199
  12.5 20.6 %all_gather.6 = bf16[160,1152]{1,0:T(8,128)(2,1)S(1)} all-gather(bf16[40,1152]{1,0:T(8,128)(2,1)S(1)} %pad.4), channel_id=1, replica_groups=mesh['zl'=2,'y'=8,'x'=4,'zh'=4,'c'=2] {'zh'}, dimensions={0}, use_global_device_ids=true | all-gather | bytes 460800 | tf_op jit(solution)/shard_map/all_gather | solution.py:198
  33.1 1.2 broadcast_in_dim.7
  34.3 0.0 copy-start.2
  34.3 5.0 %all-to-all-start = ((bf16[4,160,1152]{2,1,0:T(8,128)(2,1)}), bf16[4,160,1152]{2,1,0:T(8,128)(2,1)S(1)}, u32[]{:S(2)}, u32[]{:S(2)}) async-start(bf16[4,160,1152]{2,1,0:T(8,128)(2,1)} %broadcast_in_dim.7), calls=%async_computation | async-start | bytes 2949120 | tf_op jit(solution)/shard_map/all_to_all | solution.py:204
  39.2 0.0 reduce-scatter.2.cloned.1.call-start
  39.2 0.0 copy-done.2
  39.2 3.4 %collective-permute-start = (bf16[128,1152]{1,0:T(8,128)(2,1)S(1)}, bf16[128,1152]{1,0:T(8,128)(2,1)S(1)}, u32[]{:S(2)}, u32[]{:S(2)}) collective-permute-start(bf16[128,1152]{1,0:T(8,128)(2,1)S(1)} %copy-done.2), channel_id=1, source_target_pairs={{0,256},{256,0},{1,257},{257,1},{2,258},{258,2},{3,259},{259,3},{4... | collective-permute-start | bytes 884744 | tf_op jit(solution)/shard_map/ppermute | solution.py:23
  42.6 5.2 %collective-permute-done.refs_2_ = bf16[128,1152]{1,0:T(8,128)(2,1)S(1)} collective-permute-done((bf16[128,1152]{1,0:T(8,128)(2,1)S(1)}, bf16[128,1152]{1,0:T(8,128)(2,1)S(1)}, u32[]{:S(2)}, u32[]{:S(2)}) %collective-permute-start) | collective-permute-done | bytes 294944 | tf_op jit(solution)/shard_map/ppermute | solution.py:23
  47.8 7.9 %all-to-all-done = bf16[4,160,1152]{2,1,0:T(8,128)(2,1)S(1)} async-done(((bf16[4,160,1152]{2,1,0:T(8,128)(2,1)}), bf16[4,160,1152]{2,1,0:T(8,128)(2,1)S(1)}, u32[]{:S(2)}, u32[]{:S(2)}) %all-to-all-start) | async-done | bytes 1474592 | tf_op jit(solution)/shard_map/all_to_all | solution.py:204
  55.8 1.9 %collective-permute-start.1 = (bf16[640,1152]{1,0:T(8,128)(2,1)S(1)}, bf16[640,1152]{1,0:T(8,128)(2,1)S(1)}, u32[]{:S(2)}, u32[]{:S(2)}) collective-permute-start(bf16[640,1152]{1,0:T(8,128)(2,1)S(1)} %bitcast.10), channel_id=1, source_target_pairs={{0,1},{1,0},{2,3},{3,2},{4,5},{5,4},{6,7},{7,6},{8,9},{9,8},{10,11... | collective-permute-start | bytes 4423688 | tf_op jit(solution)/shard_map/ppermute | solution.py:23
  59.6 0.1 pad_maximum_fusion.1.scal_ref
  59.7 0.1 pad_add_fusion.refs_0_.spot_ref
  59.8 0.0 all-gather.2.cloned.1.call-done.text_ref
  59.8 1.3 shard_map.88
  61.1 0.0 copy-start
  61.1 0.7 shard_map.89.half_ref
  61.7 0.0 collective-permute-done.1.weight_ref
  61.8 1.0 copy-done
  62.7 3.8 %shard_map.90 = (bf16[576,1152]{1,0:T(8,128)(2,1)S(1)}, bf16[256,1152]{1,0:T(8,128)(2,1)S(1)}, bf16[256,1152]{1,0:T(8,128)(2,1)S(1)}, bf16[256,1024]{1,0:T(8,128)(2,1)S(1)}) custom-call(f32[3]{0:T(128)S(1)} %pad_maximum_fusion.1.scal_ref, s32[3]{0:T(128)S(1)} %pad_add_fusion.refs_0_.spot_ref, bf16[256,640]{1,0:T(8,128)(2,1)S(1)} %get-tuple-element.30.deep_ref, ...), custom_call_target="tpu_custom_call" | custom-call | flops 1509949440 | bytes 2000000 | tf_op jit(solution)/shard_map/pallas_call | solution.py:220
  66.6 2.4 %collective-permute-start.2 = (bf16[576,1152]{1,0:T(8,128)(2,1)S(1)}, bf16[576,1152]{1,0:T(8,128)(2,1)S(1)}, u32[]{:S(2)}, u32[]{:S(2)}) collective-permute-start(bf16[576,1152]{1,0:T(8,128)(2,1)S(1)} %get-tuple-element.36), channel_id=1, source_target_pairs={{0,1},{1,0},{2,3},{3,2},{4,5},{5,4},{6,7},{7,6},{8,9},{9,8},{10,11... | collective-permute-start | bytes 3981320 | tf_op jit(solution)/shard_map/ppermute | solution.py:23
  69.0 2.7 %collective-permute-done.2 = bf16[576,1152]{1,0:T(8,128)(2,1)S(1)} collective-permute-done((bf16[576,1152]{1,0:T(8,128)(2,1)S(1)}, bf16[576,1152]{1,0:T(8,128)(2,1)S(1)}, u32[]{:S(2)}, u32[]{:S(2)}) %collective-permute-start.2) | collective-permute-done | bytes 1327136 | tf_op jit(solution)/shard_map/ppermute | solution.py:23
  71.6 1.9 %shard_map.91 = bf16[1024,1152]{1,0:T(8,128)(2,1)} custom-call(bf16[256,1024]{1,0:T(8,128)(2,1)S(1)} %get-tuple-element.39.grad_ref, bf16[256,1152]{1,0:T(8,128)(2,1)S(1)} %get-tuple-element.40.unit_ref), custom_call_target="tpu_custom_call" | custom-call | flops 603979776 | bytes 2000000 | tf_op jit(solution)/shard_map/pallas_call | solution.py:229
  73.5 0.6 fusion
  74.1 0.0 reduce-scatter.2.cloned.1.call-update
  74.1 21.3 %all_to_all.20.came_ref = bf16[4,144,1152]{2,1,0:T(8,128)(2,1)S(1)} all-to-all(bf16[4,144,1152]{2,1,0:T(8,128)(2,1)S(1)} %bitcast.16), channel_id=1, replica_groups=mesh['zl'=2,'y'=8,'x'=4,'zh'=4,'c'=2] {'x'}, dimensions={0} | all-to-all | bytes 2654208 | tf_op jit(solution)/shard_map/all_to_all | solution.py:238
  95.4 0.4 shard_map.92
  95.8 0.0 copy-start.1
  95.8 0.0 copy-start.4
  95.8 0.0 copy-start.5
  95.8 19.6 %all_to_all.21 = bf16[8,168,128]{2,1,0:T(8,128)(2,1)S(1)} all-to-all(bf16[8,168,128]{2,1,0:T(8,128)(2,1)S(1)} %shard_map.92), channel_id=1, replica_groups=mesh['zl'=2,'y'=8,'x'=4,'zh'=4,'c'=2] {'zh','zl'}, dimensions={0} | all-to-all | bytes 688128 | tf_op jit(solution)/shard_map/all_to_all | solution.py:247
  115.4 0.1 reduce_sum.12
  115.5 16.7 %all_to_all.22.came_ref = bf16[8,168,128]{2,1,0:T(8,128)(2,1)S(1)} all-to-all(bf16[8,168,128]{2,1,0:T(8,128)(2,1)S(1)} %broadcast_in_dim.8), channel_id=1, replica_groups=mesh['zl'=2,'y'=8,'x'=4,'zh'=4,'c'=2] {'y'}, dimensions={0} | all-to-all | bytes 688128 | tf_op jit(solution)/shard_map/all_to_all | solution.py:249
  132.3 0.1 shard_map.93
  132.3 2.1 %collective-permute-start.3 = (f32[18,1152]{1,0:T(8,128)S(1)}, f32[18,1152]{1,0:T(8,128)S(1)}, u32[]{:S(2)}, u32[]{:S(2)}) collective-permute-start(f32[18,1152]{1,0:T(8,128)S(1)} %shard_map.93), channel_id=1, source_target_pairs={{0,256},{256,0},{1,257},{257,1},{2,258},{258,2},{3,259},{259,3},{4... | collective-permute-start | bytes 248840 | tf_op jit(solution)/shard_map/ppermute | solution.py:23
  134.4 0.0 reduce-scatter.2.cloned.1.call-done
  134.4 0.0 copy-done.1
  134.4 0.0 copy-done.4
  134.5 0.0 copy-done.5
  134.5 0.0 copy-start.3
  134.5 1.0 copy-done.3
  135.4 2.4 %shard_map.94 = f32[256,1152]{1,0:T(8,128)} custom-call(f32[3]{0:T(128)S(1)} %pad_maximum_fusion.1.scal_ref, s32[1,128]{1,0:T(1,128)S(1)} %bitcast.15, bf16[128,1152]{1,0:T(8,128)(2,1)S(1)} %bitcast.12, bf16[128,1152]{1,0:T(8,128)(2,1)S(1)} %copy-done.1, f32[128,1]{1,0:T(8,128)S(1)} %copy-done.4), custom_call_target="tpu_custom_call" | custom-call | flops 226492416 | bytes 2000000 | tf_op jit(solution)/shard_map/pallas_call | solution.py:253
  137.9 1.1 collective-permute-done.3
  139.0 0.7 pad_maximum_fusion
  (2 shorter events, 0.1 us)
Async XLA Ops:
  7.2 52.6 %all-gather.2.cloned.1.call-start = ((), (), s32[]{:S(2)}) async-start(), calls=%async_computation.5 | async-start | bytes 2654208 | tf_op jit(solution)/shard_map/all_gather | solution.py:195
  34.3 5.0 %copy-start.2 = (bf16[128,1152]{1,0:T(8,128)(2,1)S(1)}, bf16[128,1152]{1,0:T(8,128)(2,1)}, u32[]{:S(2)}) copy-start(bf16[128,1152]{1,0:T(8,128)(2,1)} %shard_map.86.refs_1_) | copy-start | bytes 884740
  34.3 21.5 %all-to-all-start = ((bf16[4,160,1152]{2,1,0:T(8,128)(2,1)}), bf16[4,160,1152]{2,1,0:T(8,128)(2,1)S(1)}, u32[]{:S(2)}, u32[]{:S(2)}) async-start(bf16[4,160,1152]{2,1,0:T(8,128)(2,1)} %broadcast_in_dim.7), calls=%async_computation | async-start | bytes 2949120 | tf_op jit(solution)/shard_map/all_to_all | solution.py:204
  39.2 95.2 %reduce-scatter.2.cloned.1.call-start = ((), (), s32[]{:S(2)}) async-start(), calls=%async_computation.6 | async-start | bytes 2654208 | tf_op jit(solution)/shard_map/reduce_scatter | solution.py:236
  39.2 8.6 %collective-permute-start = (bf16[128,1152]{1,0:T(8,128)(2,1)S(1)}, bf16[128,1152]{1,0:T(8,128)(2,1)S(1)}, u32[]{:S(2)}, u32[]{:S(2)}) collective-permute-start(bf16[128,1152]{1,0:T(8,128)(2,1)S(1)} %copy-done.2), channel_id=1, source_target_pairs={{0,256},{256,0},{1,257},{257,1},{2,258},{258,2},{3,259},{259,3},{4... | collective-permute-start | bytes 884744 | tf_op jit(solution)/shard_map/ppermute | solution.py:23
  55.8 6.0 %collective-permute-start.1 = (bf16[640,1152]{1,0:T(8,128)(2,1)S(1)}, bf16[640,1152]{1,0:T(8,128)(2,1)S(1)}, u32[]{:S(2)}, u32[]{:S(2)}) collective-permute-start(bf16[640,1152]{1,0:T(8,128)(2,1)S(1)} %bitcast.10), channel_id=1, source_target_pairs={{0,1},{1,0},{2,3},{3,2},{4,5},{5,4},{6,7},{7,6},{8,9},{9,8},{10,11... | collective-permute-start | bytes 4423688 | tf_op jit(solution)/shard_map/ppermute | solution.py:23
  61.1 1.7 %copy-start = (bf16[1024,1152]{1,0:T(8,128)(2,1)S(1)}, bf16[1024,1152]{1,0:T(8,128)(2,1)}, u32[]{:S(2)}) copy-start(bf16[1024,1152]{1,0:T(8,128)(2,1)} %all-gather.2.cloned.1.call-done.text_ref) | copy-start | bytes 7077892
  66.6 5.1 %collective-permute-start.2 = (bf16[576,1152]{1,0:T(8,128)(2,1)S(1)}, bf16[576,1152]{1,0:T(8,128)(2,1)S(1)}, u32[]{:S(2)}, u32[]{:S(2)}) collective-permute-start(bf16[576,1152]{1,0:T(8,128)(2,1)S(1)} %get-tuple-element.36), channel_id=1, source_target_pairs={{0,1},{1,0},{2,3},{3,2},{4,5},{5,4},{6,7},{7,6},{8,9},{9,8},{10,11... | collective-permute-start | bytes 3981320 | tf_op jit(solution)/shard_map/ppermute | solution.py:23
  95.8 38.6 %copy-start.1 = (bf16[128,1152]{1,0:T(8,128)(2,1)S(1)}, bf16[128,1152]{1,0:T(8,128)(2,1)}, u32[]{:S(2)}) copy-start(bf16[128,1152]{1,0:T(8,128)(2,1)} %get-tuple-element.27.unit_ref) | copy-start | bytes 884740
  95.8 38.6 %copy-start.4 = (f32[128,1]{1,0:T(8,128)S(1)}, f32[128,1]{1,0:T(8,128)}, u32[]{:S(2)}) copy-start(f32[128,1]{1,0:T(8,128)} %get-tuple-element.43.norm_ref) | copy-start | bytes 1540
  95.8 38.6 %copy-start.5 = (s32[128]{0:T(128)S(1)}, s32[128]{0:T(128)}, u32[]{:S(2)}) copy-start(s32[128]{0:T(128)} %param.9) | copy-start | bytes 1540
  132.3 6.6 %collective-permute-start.3 = (f32[18,1152]{1,0:T(8,128)S(1)}, f32[18,1152]{1,0:T(8,128)S(1)}, u32[]{:S(2)}, u32[]{:S(2)}) collective-permute-start(f32[18,1152]{1,0:T(8,128)S(1)} %shard_map.93), channel_id=1, source_target_pairs={{0,256},{256,0},{1,257},{257,1},{2,258},{258,2},{3,259},{259,3},{4... | collective-permute-start | bytes 248840 | tf_op jit(solution)/shard_map/ppermute | solution.py:23
  134.5 1.0 copy-start.3
Sparse Core Ops, SparseCore 0:
  10.1 48.9 all-gather.1
  74.2 43.3 reduce-scatter.1

commit v7 on v6

--- a/solution.py
+++ b/solution.py
@@ -13,7 +13,8 @@
 SMEM = pl.BlockSpec(memory_space=pltpu.SMEM)
 HBM = pl.BlockSpec(memory_space=pltpu.HBM)
 LANES = 128
-LIMIT = 40 * 1024 * 1024
+LIMIT = 8 * 1024 * 1024
+ROOMY = 12 * 1024 * 1024
 WHOLE = 61 * 1024 * 1024
 F32, BF16 = jnp.float32, jnp.bfloat16
 
@@ -40,24 +41,23 @@
     return tn((spots == chosen).astype(BF16), cands)
 
 
-def text_kernel(chosen_hbm, cand_hbm, unit_ref, norm_ref, chosen_ref, cand_ref, sem):
-    loads = [pltpu.make_async_copy(chosen_hbm, chosen_ref, sem.at[0]), pltpu.make_async_copy(cand_hbm, cand_ref, sem.at[1])]
+def text_kernel(chosen_hbm, cand_hbm, weight_hbm, unit_ref, norm_ref, padded_ref, chosen_ref, cand_ref, weight_ref, wide_ref, sem):
+    loads = [pltpu.make_async_copy(source, target, sem.at[k]) for k, (source, target) in enumerate(
+        ((chosen_hbm, chosen_ref), (cand_hbm, cand_ref), (weight_hbm, weight_ref)))]
     for load in loads:
         load.start()
+    wide_ref[...] = jnp.zeros_like(wide_ref)
     for load in loads:
         load.wait()
     texts = pick_rows(chosen_ref[...], cand_ref[...])
     norm = jnp.sqrt(jnp.sum(texts * texts, axis=1, keepdims=True) + EPS)
     unit_ref[...] = (texts / norm).astype(BF16)
     norm_ref[...] = norm
-
-
-def image_kernel(chosen_hbm, cand_hbm, out_ref, chosen_ref, cand_ref, sem):
-    loads = [pltpu.make_async_copy(chosen_hbm, chosen_ref, sem.at[0]), pltpu.make_async_copy(cand_hbm, cand_ref, sem.at[1])]
-    for load in loads:
-        load.start()
-    for load in loads:
-        load.wait()
+    wide_ref[:weight_ref.shape[0], :] = weight_ref[...].astype(F32)
+    padded_ref[...] = wide_ref[...].astype(BF16)
+
+
+def image_kernel(chosen_ref, cand_ref, out_ref):
     out_ref[...] = pick_rows(chosen_ref[...], cand_ref[...]).astype(BF16)
 
 
@@ -85,41 +85,39 @@
     out_ref[...] = nn(deep_ref[...], weight_ref[...])
 
 
-def main_kernel(scal_ref, spot_ref, deep_ref, half_ref, weight_ref, cols_ref, text_ref, send_ref, back_ref, unit_ref, grad_ref):
+def unit_kernel(half_ref, deep_ref, weight_ref, unit_ref, norm_ref):
+    proj = half_ref[...] + nn(deep_ref[...], weight_ref[...])
+    norm = jnp.sqrt(jnp.sum(proj * proj, axis=1, keepdims=True) + EPS)
+    unit_ref[...] = (proj / norm).astype(BF16)
+    norm_ref[...] = norm
+
+
+def main_kernel(scal_ref, spot_ref, unit_ref, norm_ref, cols_ref, text_ref, send_ref, back_ref, part_hbm,
+                grad_ref, part_ref, sem):
     temper, offset, factor = scal_ref[0], scal_ref[1], scal_ref[2]
-    proj = half_ref[...] + nn(deep_ref[...], weight_ref[...])
-    rows = proj.shape[0]
-    norm = jnp.sqrt(jnp.sum(proj * proj, axis=1, keepdims=True) + EPS)
-    unit = (proj / norm).astype(BF16)
-    unit_ref[...] = unit
+    unit = unit_ref[...]
+    rows = unit.shape[0]
     pair = rows // 2
     row_id = lax.broadcasted_iota(jnp.int32, (rows, CHUNK), 0) - spot_ref[0]
     col_id = lax.broadcasted_iota(jnp.int32, (rows, CHUNK), 1) - spot_ref[1]
     inside = (row_id >= 0) & (row_id < pair)
+    stores = []
     for k in range(text_ref.shape[0] // CHUNK):
-        block = slice(k * CHUNK, (k + 1) * CHUNK)
-        text = text_ref[block, :]
-        logits = temper * nt(unit, text) + offset
+        block = pl.ds(k * CHUNK, CHUNK)
+        logits = temper * nt(unit, text_ref[block, :]) + offset
         sign = jnp.where(inside & (col_id + k * CHUNK == row_id), 1.0, -1.0)
         grad = (-factor * sign / (1.0 + jnp.exp(sign * logits))).astype(BF16)
         grad_ref[:, block] = grad
+        part_ref[block, :] = tn(grad, unit).astype(BF16)
+        store = pltpu.make_async_copy(part_ref.at[block], part_hbm.at[block], sem.at[k])
+        store.start()
+        stores.append(store)
     image_back = temper * nn(grad_ref[...], text_ref[...])
     unit_float = unit.astype(F32)
     radial = jnp.sum(unit_float * image_back, axis=1, keepdims=True)
-    back = ((image_back - unit_float * radial) / norm).astype(BF16)
+    back = ((image_back - unit_float * radial) / norm_ref[...]).astype(BF16)
     back_ref[...] = back
     send_ref[...] = nn(cols_ref[...], back).astype(BF16)
-
-
-def part_kernel(grad_ref, unit_ref, part_hbm, part_ref, sem):
-    unit = unit_ref[...]
-    stores = []
-    for k in range(part_ref.shape[0] // CHUNK):
-        block = pl.ds(k * CHUNK, CHUNK)
-        part_ref[block, :] = tn(grad_ref[:, k * CHUNK:(k + 1) * CHUNK], unit).astype(BF16)
-        store = pltpu.make_async_copy(part_ref.at[block], part_hbm.at[block], sem.at[k])
-        store.start()
-        stores.append(store)
     for store in stores:
         store.wait()
 
@@ -187,26 +185,22 @@
     scalars = jnp.stack([logit_temp[0], logit_offset[0], loss_scale[0] / total])
 
     chosen = selection[None, :]
-    pick_scratch = [pltpu.VMEM((1, pairs), jnp.int32), pltpu.VMEM((cands, depth), BF16), pltpu.SemaphoreType.DMA((2,))]
-    text_unit, txt_norm = call(
-        text_kernel, [((pairs, width), BF16), ((pairs, 1), F32)], [HBM, HBM], (VMEM, VMEM), pick_scratch,
+    text_unit, txt_norm, part = call(
+        text_kernel, [((pairs, width), BF16), ((pairs, 1), F32), ((PADDED, width), BF16)], [HBM] * 3, (VMEM,) * 3,
+        [pltpu.VMEM((1, pairs), jnp.int32), pltpu.VMEM((cands, depth), BF16), pltpu.VMEM((own_rows, width), BF16),
+         pltpu.VMEM((PADDED, width), F32), pltpu.SemaphoreType.DMA((3,))],
         cost=2 * pairs * cands * width, limit=WHOLE,
-    )(chosen, text_cand)
+    )(chosen, text_cand, head_weight)
     text_all = lax.all_gather(text_unit, "y", axis=0, tiled=True)
 
-    part = jnp.pad(head_weight, ((0, PADDED - own_rows), (0, 0)))
     slab = lax.all_gather(part, "zh", axis=0, tiled=True)
+    slab, chosen = lax.optimization_barrier((slab, chosen))
     (picked,) = call(
-        image_kernel, [((pairs, depth), BF16)], [HBM, HBM], (VMEM,), pick_scratch, cost=2 * pairs * cands * depth, limit=WHOLE,
+        image_kernel, [((pairs, depth), BF16)], [VMEM, VMEM], (VMEM,), cost=2 * pairs * cands * depth,
     )(chosen, image_cand)
-    slab, picked = lax.optimization_barrier((slab, picked))
     there = hop(picked, "zl", 1)
     slabs = lax.all_to_all(jnp.broadcast_to(slab[None], (n_x,) + slab.shape), "x", 0, 0)
     mine = slabs.reshape(n_x * slab.shape[0], width)
-    mine, there = lax.optimization_barrier((mine, there))
-    other = hop(mine, "c", 1)
-
-    there, text_all = lax.optimization_barrier((there, text_all))
     deep = mine.shape[0]
     deep_mine, deep_other, cols_mine, cols_other = call(
         lambda *refs: pair_kernel(own_rows, *refs),
@@ -214,26 +208,26 @@
         [SMEM, VMEM, VMEM], (VMEM,) * 4,
         [pltpu.VMEM((depth, rows), F32), pltpu.VMEM((2, depth // 2, rows), F32), pltpu.VMEM((2, deep, rows), F32)],
     )(spot, picked, there)
+    mine, deep_mine = lax.optimization_barrier((mine, deep_mine))
+    other = hop(mine, "c", 1)
     (half,) = call(
-        half_kernel, [((rows, width), F32)], [VMEM, VMEM], (VMEM,), cost=2 * rows * deep * width,
+        half_kernel, [((rows, width), F32)], [VMEM, VMEM], (VMEM,), cost=2 * rows * deep * width, limit=4 * 1024 * 1024,
     )(deep_mine, mine)
-    send, proj_back, image_unit, grad_tile = call(
+    image_unit, img_norm = call(
+        unit_kernel, [((rows, width), BF16), ((rows, 1), F32)], [VMEM] * 3, (VMEM,) * 2, cost=2 * rows * deep * width,
+    )(half, deep_other, other)
+    send, proj_back, text_part = call(
         main_kernel,
-        [((depth // 2, width), BF16), ((rows, width), BF16), ((rows, width), BF16), ((rows, n_y * pairs), BF16)],
-        [SMEM, SMEM] + [VMEM] * 5, (VMEM,) * 4,
-        cost=5 * rows * n_y * pairs * width,
-    )(scalars, spot, deep_other, half, other, cols_other, text_all)
+        [((depth // 2, width), BF16), ((rows, width), BF16), ((n_y * pairs, width), BF16)],
+        [SMEM, SMEM] + [VMEM] * 4, (VMEM, VMEM, HBM),
+        [pltpu.VMEM((rows, n_y * pairs), BF16), pltpu.VMEM((n_y * pairs, width), BF16),
+         pltpu.SemaphoreType.DMA((n_y * pairs // CHUNK,))],
+        cost=6 * rows * n_y * pairs * width, limit=ROOMY,
+    )(scalars, spot, image_unit, img_norm, cols_other, text_all)
+    text_back = lax.psum_scatter(text_part.reshape(n_y, pairs, width), "y", scatter_dimension=0)
     got = hop(send, "c", 1)
-    got, grad_tile = lax.optimization_barrier((got, grad_tile))
     head = (nn(cols_mine, proj_back) + got.astype(F32)).astype(BF16)
-    (text_part,) = call(
-        part_kernel, [((n_y * pairs, width), BF16)], [VMEM, VMEM], (HBM,),
-        [pltpu.VMEM((n_y * pairs, width), BF16), pltpu.SemaphoreType.DMA((n_y * pairs // CHUNK,))],
-        cost=2 * rows * n_y * pairs * width,
-    )(grad_tile, image_unit)
-
-    head, text_part = lax.optimization_barrier((head, text_part))
-    text_back = lax.psum_scatter(text_part.reshape(n_y, pairs, width), "y", scatter_dimension=0)
+
     share = depth // 2 // n_x
     came = lax.all_to_all(head.reshape(n_x, share, width), "x", 0, 0)
     n_z = lax.axis_size(("zh", "zl"))

time: 147 us -> 144 us (0.980)
  Pallas kernels: 14.8 us -> 13 us
    pallas_call x3, Pallas kernels: 6.2 us -> 3.41 us  [the longest x1 2.29 us: shards(): call(text_kernel, [((pairs, width), BF16), ((pairs, 1), F32), ((PADDED, w...]
    all_to_all x1, waiting for transfers between devices: 7.91 us -> 6.32 us  [shards(): lax.all_to_all(jnp.broadcast_to(slab[None], (n_x,) + slab.shape), 'x', 0, 0)]
    all_to_all x1, blocking collectives: 16.7 us -> 15.3 us  [shards(): lax.all_to_all(jnp.broadcast_to(head[None], (n_y,) + head.shape), 'y', 0, 0)]
  transfers between devices with their start and end apart: 7 -> 7, of which waited for: 4 -> 6; matrix products, arithmetic and copies ran while one was open for 2% -> 1% of each run, Pallas kernels for 5% -> 4%
where the time goes in v7:
time: 144 us; the launch traced here: 143 us
  blocking collectives  77.7 us (54%)
  waiting for transfers between devices  16.4 us (11%)
  between operations  16.1 us (11%)
  starting transfers between devices  14.7 us (10%)
  Pallas kernels  13 us (9%)
  local copies, waits for them, and re-layouts  3.89 us (3%)
    all_to_all x1, blocking collectives, shards(): came = lax.all_to_all(head.reshape(n_x, share, width), 'x', 0, 0)  21.5 us
    all_gather x1, blocking collectives, shards(): slab = lax.all_gather(part, 'zh', axis=0, tiled=True)  20.8 us
    all_to_all x1, blocking collectives, shards(): came = lax.all_to_all(folded, ('zh', 'zl'), 0, 0)  20.1 us
    all_to_all x1, blocking collectives, shards(): lax.all_to_all(jnp.broadcast_to(head[None], (n_y,) + head.shape), 'y', 0, 0)  15.3 us
    ppermute x4, starting transfers between devices, hop(): lax.ppermute(value, axis, [(s, (s + steps) % count) for s in range(count)])  9.72 us
    ppermute x4, waiting for transfers between devices, hop(): lax.ppermute(value, axis, [(s, (s + steps) % count) for s in range(count)])  9.39 us
    all_to_all x1, waiting for transfers between devices, shards(): lax.all_to_all(jnp.broadcast_to(slab[None], (n_x,) + slab.shape), 'x', 0, 0)  6.32 us
    all_to_all x1, starting transfers between devices, shards(): lax.all_to_all(jnp.broadcast_to(slab[None], (n_x,) + slab.shape), 'x', 0, 0)  4.95 us
  transfers between devices with their start and end apart: 7, of which 6 were waited for; matrix products, arithmetic and copies ran while one was open for 1% of the time, Pallas kernels for 4%

profile of v7, /device:TPU:2, one launch (start us, length us, event | category | flops | bytes accessed | tf_op | source)
XLA Modules:
  0.0 143.3 jit_solution(4128245849573085118)
XLA Ops:
  7.2 0.0 all-gather.2.cloned.1.call-start
  7.2 2.3 %shard_map.86 = (bf16[128,1152]{1,0:T(8,128)(2,1)}, f32[128,1]{1,0:T(8,128)}, bf16[40,1152]{1,0:T(8,128)(2,1)}) custom-call(s32[1,128]{1,0:T(1,128)} %bitcast.13, bf16[256,1152]{1,0:T(8,128)(2,1)} %cand_hbm.1, bf16[36,1152]{1,0:T(8,128)(2,1)} %weight_hbm.1), custom_call_target="tpu_custom_call" | custom-call | flops 75497472 | bytes 2000000 | tf_op jit(solution)/shard_map/pallas_call | solution.py:188
  9.5 0.0 all-gather.2.cloned.1.call-update
  9.5 20.8 %all_gather.6 = bf16[160,1152]{1,0:T(8,128)(2,1)S(1)} all-gather(bf16[40,1152]{1,0:T(8,128)(2,1)} %get-tuple-element.20), channel_id=1, replica_groups=mesh['zl'=2,'y'=8,'x'=4,'zh'=4,'c'=2] {'zh'}, dimensions={0}, use_global_device_ids=true | all-gather | bytes 460800 | tf_op jit(solution)/shard_map/all_gather | solution.py:196
  30.3 1.2 broadcast_in_dim.7
  31.5 0.0 copy-start.1
  31.5 0.0 copy-start.4
  31.5 5.0 %all-to-all-start = ((bf16[4,160,1152]{2,1,0:T(8,128)(2,1)}), bf16[4,160,1152]{2,1,0:T(8,128)(2,1)S(1)}, u32[]{:S(2)}, u32[]{:S(2)}) async-start(bf16[4,160,1152]{2,1,0:T(8,128)(2,1)} %broadcast_in_dim.7), calls=%async_computation | async-start | bytes 2949120 | tf_op jit(solution)/shard_map/all_to_all | solution.py:202
  36.5 0.0 reduce-scatter.2.cloned.1.call-start
  36.5 0.0 copy-done.1
  36.5 0.0 copy-done.4
  36.5 0.3 shard_map.87.refs_1_
  36.8 3.4 %collective-permute-start = (bf16[128,1152]{1,0:T(8,128)(2,1)S(1)}, bf16[128,1152]{1,0:T(8,128)(2,1)S(1)}, u32[]{:S(2)}, u32[]{:S(2)}) collective-permute-start(bf16[128,1152]{1,0:T(8,128)(2,1)S(1)} %shard_map.87.refs_1_), channel_id=1, source_target_pairs={{0,256},{256,0},{1,257},{257,1},{2,258},{258,2},{3,259},{259,3},{4... | collective-permute-start | bytes 884744 | tf_op jit(solution)/shard_map/ppermute | solution.py:24
  40.2 0.1 pad_add_fusion.refs_0_.spot_ref
  40.3 5.1 %collective-permute-done.refs_2_ = bf16[128,1152]{1,0:T(8,128)(2,1)S(1)} collective-permute-done((bf16[128,1152]{1,0:T(8,128)(2,1)S(1)}, bf16[128,1152]{1,0:T(8,128)(2,1)S(1)}, u32[]{:S(2)}, u32[]{:S(2)}) %collective-permute-start) | collective-permute-done | bytes 294944 | tf_op jit(solution)/shard_map/ppermute | solution.py:24
  45.4 1.3 shard_map.88
  46.7 6.3 %all-to-all-done = bf16[4,160,1152]{2,1,0:T(8,128)(2,1)S(1)} async-done(((bf16[4,160,1152]{2,1,0:T(8,128)(2,1)}), bf16[4,160,1152]{2,1,0:T(8,128)(2,1)S(1)}, u32[]{:S(2)}, u32[]{:S(2)}) %all-to-all-start) | async-done | bytes 1474592 | tf_op jit(solution)/shard_map/all_to_all | solution.py:202
  53.0 1.9 %collective-permute-start.1 = (bf16[640,1152]{1,0:T(8,128)(2,1)S(1)}, bf16[640,1152]{1,0:T(8,128)(2,1)S(1)}, u32[]{:S(2)}, u32[]{:S(2)}) collective-permute-start(bf16[640,1152]{1,0:T(8,128)(2,1)S(1)} %bitcast.10), channel_id=1, source_target_pairs={{0,1},{1,0},{2,3},{3,2},{4,5},{5,4},{6,7},{7,6},{8,9},{9,8},{10,11... | collective-permute-start | bytes 4423688 | tf_op jit(solution)/shard_map/ppermute | solution.py:24
  56.9 0.1 pad_maximum_fusion.1.scal_ref
  57.0 0.7 shard_map.89.half_ref
  57.6 0.5 collective-permute-done.1.weight_ref
  58.2 0.8 shard_map.90
  59.0 0.6 all-gather.2.cloned.1.call-done.text_ref
  59.6 0.0 copy-start.5
  59.6 1.7 %copy-done.5 = bf16[1024,1152]{1,0:T(8,128)(2,1)S(1)} copy-done((bf16[1024,1152]{1,0:T(8,128)(2,1)S(1)}, bf16[1024,1152]{1,0:T(8,128)(2,1)}, u32[]{:S(2)}) %copy-start.5) | copy-done | bytes 2359320
  61.3 4.8 %shard_map.91 = (bf16[576,1152]{1,0:T(8,128)(2,1)S(1)}, bf16[256,1152]{1,0:T(8,128)(2,1)S(1)}, bf16[1024,1152]{1,0:T(8,128)(2,1)}) custom-call(f32[3]{0:T(128)S(1)} %pad_maximum_fusion.1.scal_ref, s32[3]{0:T(128)S(1)} %pad_add_fusion.refs_0_.spot_ref, bf16[256,1152]{1,0:T(8,128)(2,1)S(1)} %get-tuple-element.28.unit_ref, ...), custom_call_target="tpu_custom_call" | custom-call | flops 1811939328 | bytes 2000000 | tf_op jit(solution)/shard_map/pallas_call | solution.py:219
  66.1 0.0 reduce-scatter.2.cloned.1.call-update
  66.1 1.9 %collective-permute-start.2 = (bf16[576,1152]{1,0:T(8,128)(2,1)S(1)}, bf16[576,1152]{1,0:T(8,128)(2,1)S(1)}, u32[]{:S(2)}, u32[]{:S(2)}) collective-permute-start(bf16[576,1152]{1,0:T(8,128)(2,1)S(1)} %get-tuple-element.33), channel_id=1, source_target_pairs={{0,1},{1,0},{2,3},{3,2},{4,5},{5,4},{6,7},{7,6},{8,9},{9,8},{10,11... | collective-permute-start | bytes 3981320 | tf_op jit(solution)/shard_map/ppermute | solution.py:24
  68.1 3.0 %collective-permute-done.2 = bf16[576,1152]{1,0:T(8,128)(2,1)S(1)} collective-permute-done((bf16[576,1152]{1,0:T(8,128)(2,1)S(1)}, bf16[576,1152]{1,0:T(8,128)(2,1)S(1)}, u32[]{:S(2)}, u32[]{:S(2)}) %collective-permute-start.2) | collective-permute-done | bytes 1327136 | tf_op jit(solution)/shard_map/ppermute | solution.py:24
  71.1 0.6 fusion
  71.7 21.5 %all_to_all.20.came_ref = bf16[4,144,1152]{2,1,0:T(8,128)(2,1)S(1)} all-to-all(bf16[4,144,1152]{2,1,0:T(8,128)(2,1)S(1)} %bitcast.16), channel_id=1, replica_groups=mesh['zl'=2,'y'=8,'x'=4,'zh'=4,'c'=2] {'x'}, dimensions={0} | all-to-all | bytes 2654208 | tf_op jit(solution)/shard_map/all_to_all | solution.py:232
  93.2 0.4 shard_map.92
  93.6 0.0 copy-start
  93.6 0.0 copy-start.3
  93.6 20.1 %all_to_all.21 = bf16[8,168,128]{2,1,0:T(8,128)(2,1)S(1)} all-to-all(bf16[8,168,128]{2,1,0:T(8,128)(2,1)S(1)} %shard_map.92), channel_id=1, replica_groups=mesh['zl'=2,'y'=8,'x'=4,'zh'=4,'c'=2] {'zh','zl'}, dimensions={0} | all-to-all | bytes 688128 | tf_op jit(solution)/shard_map/all_to_all | solution.py:241
  113.7 0.1 reduce_sum.12
  113.8 15.3 %all_to_all.22.came_ref = bf16[8,168,128]{2,1,0:T(8,128)(2,1)S(1)} all-to-all(bf16[8,168,128]{2,1,0:T(8,128)(2,1)S(1)} %broadcast_in_dim.8), channel_id=1, replica_groups=mesh['zl'=2,'y'=8,'x'=4,'zh'=4,'c'=2] {'y'}, dimensions={0} | all-to-all | bytes 688128 | tf_op jit(solution)/shard_map/all_to_all | solution.py:243
  129.1 0.1 shard_map.93
  129.1 2.5 %collective-permute-start.3 = (f32[18,1152]{1,0:T(8,128)S(1)}, f32[18,1152]{1,0:T(8,128)S(1)}, u32[]{:S(2)}, u32[]{:S(2)}) collective-permute-start(f32[18,1152]{1,0:T(8,128)S(1)} %shard_map.93), channel_id=1, source_target_pairs={{0,256},{256,0},{1,257},{257,1},{2,258},{258,2},{3,259},{259,3},{4... | collective-permute-start | bytes 248840 | tf_op jit(solution)/shard_map/ppermute | solution.py:24
  131.6 0.0 reduce-scatter.2.cloned.1.call-done
  131.6 0.0 copy-done
  131.6 0.0 copy-done.3
  131.7 0.0 copy-start.2
  131.7 1.0 copy-done.2
  132.6 2.4 %shard_map.94 = f32[256,1152]{1,0:T(8,128)} custom-call(f32[3]{0:T(128)S(1)} %pad_maximum_fusion.1.scal_ref, s32[1,128]{1,0:T(1,128)S(1)} %bitcast.15, bf16[128,1152]{1,0:T(8,128)(2,1)S(1)} %bitcast.12, bf16[128,1152]{1,0:T(8,128)(2,1)S(1)} %copy-done, f32[128,1]{1,0:T(8,128)S(1)} %copy-done.3), custom_call_target="tpu_custom_call" | custom-call | flops 226492416 | bytes 2000000 | tf_op jit(solution)/shard_map/pallas_call | solution.py:247
  135.0 0.7 collective-permute-done.3
  135.8 0.7 pad_maximum_fusion
  (2 shorter events, 0.1 us)
Async XLA Ops:
  7.2 52.5 %all-gather.2.cloned.1.call-start = ((), (), s32[]{:S(2)}) async-start(), calls=%async_computation.5 | async-start | bytes 2654208 | tf_op jit(solution)/shard_map/all_gather | solution.py:194
  31.5 5.0 %copy-start.1 = (bf16[256,1152]{1,0:T(8,128)(2,1)S(1)}, bf16[256,1152]{1,0:T(8,128)(2,1)}, u32[]{:S(2)}) copy-start(bf16[256,1152]{1,0:T(8,128)(2,1)} %cand_ref.1) | copy-start | bytes 1769476
  31.5 5.0 %copy-start.4 = (s32[128]{0:T(128)S(1)}, s32[128]{0:T(128)}, u32[]{:S(2)}) copy-start(s32[128]{0:T(128)} %param.9) | copy-start | bytes 1540
  31.5 21.5 %all-to-all-start = ((bf16[4,160,1152]{2,1,0:T(8,128)(2,1)}), bf16[4,160,1152]{2,1,0:T(8,128)(2,1)S(1)}, u32[]{:S(2)}, u32[]{:S(2)}) async-start(bf16[4,160,1152]{2,1,0:T(8,128)(2,1)} %broadcast_in_dim.7), calls=%async_computation | async-start | bytes 2949120 | tf_op jit(solution)/shard_map/all_to_all | solution.py:202
  36.5 95.1 %reduce-scatter.2.cloned.1.call-start = ((), (), s32[]{:S(2)}) async-start(), calls=%async_computation.6 | async-start | bytes 2654208 | tf_op jit(solution)/shard_map/reduce_scatter | solution.py:227
  36.8 8.6 %collective-permute-start = (bf16[128,1152]{1,0:T(8,128)(2,1)S(1)}, bf16[128,1152]{1,0:T(8,128)(2,1)S(1)}, u32[]{:S(2)}, u32[]{:S(2)}) collective-permute-start(bf16[128,1152]{1,0:T(8,128)(2,1)S(1)} %shard_map.87.refs_1_), channel_id=1, source_target_pairs={{0,256},{256,0},{1,257},{257,1},{2,258},{258,2},{3,259},{259,3},{4... | collective-permute-start | bytes 884744 | tf_op jit(solution)/shard_map/ppermute | solution.py:24
  53.0 5.2 %collective-permute-start.1 = (bf16[640,1152]{1,0:T(8,128)(2,1)S(1)}, bf16[640,1152]{1,0:T(8,128)(2,1)S(1)}, u32[]{:S(2)}, u32[]{:S(2)}) collective-permute-start(bf16[640,1152]{1,0:T(8,128)(2,1)S(1)} %bitcast.10), channel_id=1, source_target_pairs={{0,1},{1,0},{2,3},{3,2},{4,5},{5,4},{6,7},{7,6},{8,9},{9,8},{10,11... | collective-permute-start | bytes 4423688 | tf_op jit(solution)/shard_map/ppermute | solution.py:24
  59.6 1.7 %copy-start.5 = (bf16[1024,1152]{1,0:T(8,128)(2,1)S(1)}, bf16[1024,1152]{1,0:T(8,128)(2,1)}, u32[]{:S(2)}) copy-start(bf16[1024,1152]{1,0:T(8,128)(2,1)} %all-gather.2.cloned.1.call-done.text_ref) | copy-start | bytes 7077892
  66.1 5.0 %collective-permute-start.2 = (bf16[576,1152]{1,0:T(8,128)(2,1)S(1)}, bf16[576,1152]{1,0:T(8,128)(2,1)S(1)}, u32[]{:S(2)}, u32[]{:S(2)}) collective-permute-start(bf16[576,1152]{1,0:T(8,128)(2,1)S(1)} %get-tuple-element.33), channel_id=1, source_target_pairs={{0,1},{1,0},{2,3},{3,2},{4,5},{5,4},{6,7},{7,6},{8,9},{9,8},{10,11... | collective-permute-start | bytes 3981320 | tf_op jit(solution)/shard_map/ppermute | solution.py:24
  93.6 38.1 %copy-start = (bf16[128,1152]{1,0:T(8,128)(2,1)S(1)}, bf16[128,1152]{1,0:T(8,128)(2,1)}, u32[]{:S(2)}) copy-start(bf16[128,1152]{1,0:T(8,128)(2,1)} %get-tuple-element.31.unit_ref) | copy-start | bytes 884740
  93.6 38.1 %copy-start.3 = (f32[128,1]{1,0:T(8,128)S(1)}, f32[128,1]{1,0:T(8,128)}, u32[]{:S(2)}) copy-start(f32[128,1]{1,0:T(8,128)} %get-tuple-element.35.norm_ref) | copy-start | bytes 1540
  129.1 6.6 %collective-permute-start.3 = (f32[18,1152]{1,0:T(8,128)S(1)}, f32[18,1152]{1,0:T(8,128)S(1)}, u32[]{:S(2)}, u32[]{:S(2)}) collective-permute-start(f32[18,1152]{1,0:T(8,128)S(1)} %shard_map.93), channel_id=1, source_target_pairs={{0,256},{256,0},{1,257},{257,1},{2,258},{258,2},{3,259},{259,3},{4... | collective-permute-start | bytes 248840 | tf_op jit(solution)/shard_map/ppermute | solution.py:24
  131.7 1.0 copy-start.2
Sparse Core Ops, SparseCore 0:
  10.7 48.9 all-gather.1
  66.3 44.0 reduce-scatter.1

commit v8 on v7

--- a/solution.py
+++ b/solution.py
@@ -92,7 +92,7 @@
     norm_ref[...] = norm
 
 
-def main_kernel(scal_ref, spot_ref, unit_ref, norm_ref, cols_ref, text_ref, send_ref, back_ref, part_hbm,
+def main_kernel(scal_ref, spot_ref, unit_ref, norm_ref, text_ref, back_ref, part_hbm,
                 grad_ref, part_ref, sem):
     temper, offset, factor = scal_ref[0], scal_ref[1], scal_ref[2]
     unit = unit_ref[...]
@@ -105,21 +105,25 @@
     for k in range(text_ref.shape[0] // CHUNK):
         block = pl.ds(k * CHUNK, CHUNK)
         logits = temper * nt(unit, text_ref[block, :]) + offset
-        sign = jnp.where(inside & (col_id + k * CHUNK == row_id), 1.0, -1.0)
-        grad = (-factor * sign / (1.0 + jnp.exp(sign * logits))).astype(BF16)
+        same = inside & (col_id + k * CHUNK == row_id)
+        weight = jnp.where(same, -factor, factor)
+        grad = (weight / (1.0 + jnp.exp(jnp.where(same, logits, -logits)))).astype(BF16)
         grad_ref[:, block] = grad
         part_ref[block, :] = tn(grad, unit).astype(BF16)
         store = pltpu.make_async_copy(part_ref.at[block], part_hbm.at[block], sem.at[k])
         store.start()
         stores.append(store)
-    image_back = temper * nn(grad_ref[...], text_ref[...])
+    image_back = nn(grad_ref[...], text_ref[...])
     unit_float = unit.astype(F32)
     radial = jnp.sum(unit_float * image_back, axis=1, keepdims=True)
-    back = ((image_back - unit_float * radial) / norm_ref[...]).astype(BF16)
+    back = ((image_back - unit_float * radial) * (temper / norm_ref[...])).astype(BF16)
     back_ref[...] = back
-    send_ref[...] = nn(cols_ref[...], back).astype(BF16)
     for store in stores:
         store.wait()
+
+
+def join_kernel(cols_mine_ref, cols_there_ref, back_ref, there_ref, out_ref):
+    out_ref[...] = (nn(cols_mine_ref[...], back_ref[...]) + nn(cols_there_ref[...], there_ref[...])).astype(BF16)
 
 
 def fold_kernel(came_ref, out_ref, sum_ref, flat_ref):
@@ -208,7 +212,8 @@
         [SMEM, VMEM, VMEM], (VMEM,) * 4,
         [pltpu.VMEM((depth, rows), F32), pltpu.VMEM((2, depth // 2, rows), F32), pltpu.VMEM((2, deep, rows), F32)],
     )(spot, picked, there)
-    mine, deep_mine = lax.optimization_barrier((mine, deep_mine))
+    cols_there = hop(cols_other, "c", 1)
+    mine, cols_there = lax.optimization_barrier((mine, cols_there))
     other = hop(mine, "c", 1)
     (half,) = call(
         half_kernel, [((rows, width), F32)], [VMEM, VMEM], (VMEM,), cost=2 * rows * deep * width, limit=4 * 1024 * 1024,
@@ -216,17 +221,18 @@
     image_unit, img_norm = call(
         unit_kernel, [((rows, width), BF16), ((rows, 1), F32)], [VMEM] * 3, (VMEM,) * 2, cost=2 * rows * deep * width,
     )(half, deep_other, other)
-    send, proj_back, text_part = call(
+    proj_back, text_part = call(
         main_kernel,
-        [((depth // 2, width), BF16), ((rows, width), BF16), ((n_y * pairs, width), BF16)],
-        [SMEM, SMEM] + [VMEM] * 4, (VMEM, VMEM, HBM),
+        [((rows, width), BF16), ((n_y * pairs, width), BF16)],
+        [SMEM, SMEM] + [VMEM] * 3, (VMEM, HBM),
         [pltpu.VMEM((rows, n_y * pairs), BF16), pltpu.VMEM((n_y * pairs, width), BF16),
          pltpu.SemaphoreType.DMA((n_y * pairs // CHUNK,))],
         cost=6 * rows * n_y * pairs * width, limit=ROOMY,
-    )(scalars, spot, image_unit, img_norm, cols_other, text_all)
+    )(scalars, spot, image_unit, img_norm, text_all)
     text_back = lax.psum_scatter(text_part.reshape(n_y, pairs, width), "y", scatter_dimension=0)
-    got = hop(send, "c", 1)
-    head = (nn(cols_mine, proj_back) + got.astype(F32)).astype(BF16)
+    (head,) = call(
+        join_kernel, [((depth // 2, width), BF16)], [VMEM] * 4, (VMEM,), cost=2 * rows * depth * width,
+    )(cols_mine, cols_there, proj_back, hop(proj_back, "c", 1))
 
     share = depth // 2 // n_x
     came = lax.all_to_all(head.reshape(n_x, share, width), "x", 0, 0)

time: 144 us -> 143 us (level)
  waiting for transfers between devices: 16.4 us -> 13.4 us
  starting transfers between devices: 14.7 us -> 16.6 us
    all_to_all x1, waiting for transfers between devices: 6.32 us -> 2.85 us  [shards(): lax.all_to_all(jnp.broadcast_to(slab[None], (n_x,) + slab.shape), 'x', 0, 0)]
    ppermute x4 -> x5, starting transfers between devices: 9.72 us -> 11.6 us  [hop(): lax.ppermute(value, axis, [(s, (s + steps) % count) for s in range(count)])]
    ppermute x4 -> x5, waiting for transfers between devices: 9.39 us -> 9.88 us  [hop(): lax.ppermute(value, axis, [(s, (s + steps) % count) for s in range(count)])]
    pallas_call x1 -> x2, Pallas kernels: 4.8 us -> 5.18 us  [the longest x1 4.24 us: shards(): call(main_kernel, [((rows, width), BF16), ((n_y * pairs, width), BF16)],...]
  transfers between devices with their start and end apart: 7 -> 8, of which waited for: 6 -> 7; matrix products, arithmetic and copies ran while one was open for 1% -> 1% of each run, Pallas kernels for 4% -> 5%
where the time goes in v8:
time: 143 us; the launch traced here: 142 us
  blocking collectives  77.7 us (54%)
  starting transfers between devices  16.6 us (12%)
  between operations  16.1 us (11%)
  Pallas kernels  13.4 us (9%)
  waiting for transfers between devices  13.4 us (9%)
  local copies, waits for them, and re-layouts  3.89 us (3%)
    all_to_all x1, blocking collectives, shards(): came = lax.all_to_all(head.reshape(n_x, share, width), 'x', 0, 0)  21.5 us
    all_gather x1, blocking collectives, shards(): slab = lax.all_gather(part, 'zh', axis=0, tiled=True)  20.8 us
    all_to_all x1, blocking collectives, shards(): came = lax.all_to_all(folded, ('zh', 'zl'), 0, 0)  20.2 us
    all_to_all x1, blocking collectives, shards(): lax.all_to_all(jnp.broadcast_to(head[None], (n_y,) + head.shape), 'y', 0, 0)  15.2 us
    ppermute x5, starting transfers between devices, hop(): lax.ppermute(value, axis, [(s, (s + steps) % count) for s in range(count)])  11.6 us
    ppermute x5, waiting for transfers between devices, hop(): lax.ppermute(value, axis, [(s, (s + steps) % count) for s in range(count)])  9.88 us
    all_to_all x1, starting transfers between devices, shards(): lax.all_to_all(jnp.broadcast_to(slab[None], (n_x,) + slab.shape), 'x', 0, 0)  4.95 us
    pallas_call x1, Pallas kernels, shards(): call(main_kernel, [((rows, width), BF16), ((n_y * pairs, width), BF16)],...  4.24 us
  transfers between devices with their start and end apart: 8, of which 7 were waited for; matrix products, arithmetic and copies ran while one was open for 1% of the time, Pallas kernels for 5%

profile of v8, /device:TPU:2, one launch (start us, length us, event | category | flops | bytes accessed | tf_op | source)
XLA Modules:
  0.0 142.1 jit_solution(7093797599297782249)
XLA Ops:
  7.2 0.0 all-gather.2.cloned.1.call-start
  7.2 2.3 %shard_map.86 = (bf16[128,1152]{1,0:T(8,128)(2,1)}, f32[128,1]{1,0:T(8,128)}, bf16[40,1152]{1,0:T(8,128)(2,1)}) custom-call(s32[1,128]{1,0:T(1,128)} %bitcast.12, bf16[256,1152]{1,0:T(8,128)(2,1)} %cand_hbm.1, bf16[36,1152]{1,0:T(8,128)(2,1)} %weight_hbm.1), custom_call_target="tpu_custom_call" | custom-call | flops 75497472 | bytes 2000000 | tf_op jit(solution)/shard_map/pallas_call | solution.py:192
  9.5 0.0 all-gather.2.cloned.1.call-update
  9.5 20.8 %all_gather.6 = bf16[160,1152]{1,0:T(8,128)(2,1)S(1)} all-gather(bf16[40,1152]{1,0:T(8,128)(2,1)} %get-tuple-element.19), channel_id=1, replica_groups=mesh['zl'=2,'y'=8,'x'=4,'zh'=4,'c'=2] {'zh'}, dimensions={0}, use_global_device_ids=true | all-gather | bytes 460800 | tf_op jit(solution)/shard_map/all_gather | solution.py:200
  30.3 1.2 broadcast_in_dim.7
  31.5 0.0 copy-start.1
  31.5 0.0 copy-start.4
  31.5 5.0 %all-to-all-start = ((bf16[4,160,1152]{2,1,0:T(8,128)(2,1)}), bf16[4,160,1152]{2,1,0:T(8,128)(2,1)S(1)}, u32[]{:S(2)}, u32[]{:S(2)}) async-start(bf16[4,160,1152]{2,1,0:T(8,128)(2,1)} %broadcast_in_dim.7), calls=%async_computation | async-start | bytes 2949120 | tf_op jit(solution)/shard_map/all_to_all | solution.py:206
  36.5 0.0 reduce-scatter.2.cloned.1.call-start
  36.5 0.0 copy-done.1
  36.5 0.0 copy-done.4
  36.5 0.3 shard_map.87.refs_1_
  36.8 3.4 %collective-permute-start = (bf16[128,1152]{1,0:T(8,128)(2,1)S(1)}, bf16[128,1152]{1,0:T(8,128)(2,1)S(1)}, u32[]{:S(2)}, u32[]{:S(2)}) collective-permute-start(bf16[128,1152]{1,0:T(8,128)(2,1)S(1)} %shard_map.87.refs_1_), channel_id=1, source_target_pairs={{0,256},{256,0},{1,257},{257,1},{2,258},{258,2},{3,259},{259,3},{4... | collective-permute-start | bytes 884744 | tf_op jit(solution)/shard_map/ppermute | solution.py:24
  40.2 0.1 pad_add_fusion.refs_0_.spot_ref
  40.3 5.1 %collective-permute-done.refs_2_ = bf16[128,1152]{1,0:T(8,128)(2,1)S(1)} collective-permute-done((bf16[128,1152]{1,0:T(8,128)(2,1)S(1)}, bf16[128,1152]{1,0:T(8,128)(2,1)S(1)}, u32[]{:S(2)}, u32[]{:S(2)}) %collective-permute-start) | collective-permute-done | bytes 294944 | tf_op jit(solution)/shard_map/ppermute | solution.py:24
  45.4 1.3 shard_map.88
  46.7 1.9 %collective-permute-start.1 = (bf16[576,256]{1,0:T(8,128)(2,1)S(1)}, bf16[576,256]{1,0:T(8,128)(2,1)S(1)}, u32[]{:S(2)}, u32[]{:S(2)}) collective-permute-start(bf16[576,256]{1,0:T(8,128)(2,1)S(1)} %get-tuple-element.23), channel_id=1, source_target_pairs={{0,1},{1,0},{2,3},{3,2},{4,5},{5,4},{6,7},{7,6},{8,9},{9,8},{10,11... | collective-permute-start | bytes 884744 | tf_op jit(solution)/shard_map/ppermute | solution.py:24
  48.6 1.5 %collective-permute-done.1.cols_there_ref = bf16[576,256]{1,0:T(8,128)(2,1)S(1)} collective-permute-done((bf16[576,256]{1,0:T(8,128)(2,1)S(1)}, bf16[576,256]{1,0:T(8,128)(2,1)S(1)}, u32[]{:S(2)}, u32[]{:S(2)}) %collective-permute-start.1) | collective-permute-done | bytes 294944 | tf_op jit(solution)/shard_map/ppermute | solution.py:24
  50.2 2.8 %all-to-all-done = bf16[4,160,1152]{2,1,0:T(8,128)(2,1)S(1)} async-done(((bf16[4,160,1152]{2,1,0:T(8,128)(2,1)}), bf16[4,160,1152]{2,1,0:T(8,128)(2,1)S(1)}, u32[]{:S(2)}, u32[]{:S(2)}) %all-to-all-start) | async-done | bytes 1474592 | tf_op jit(solution)/shard_map/all_to_all | solution.py:206
  53.0 1.9 %collective-permute-start.2 = (bf16[640,1152]{1,0:T(8,128)(2,1)S(1)}, bf16[640,1152]{1,0:T(8,128)(2,1)S(1)}, u32[]{:S(2)}, u32[]{:S(2)}) collective-permute-start(bf16[640,1152]{1,0:T(8,128)(2,1)S(1)} %bitcast.8), channel_id=1, source_target_pairs={{0,1},{1,0},{2,3},{3,2},{4,5},{5,4},{6,7},{7,6},{8,9},{9,8},{10,11... | collective-permute-start | bytes 4423688 | tf_op jit(solution)/shard_map/ppermute | solution.py:24
  56.9 0.1 pad_maximum_fusion.1.scal_ref
  57.0 0.7 shard_map.89.half_ref
  57.6 0.5 collective-permute-done.2.weight_ref
  58.2 0.8 shard_map.90
  59.0 0.6 all-gather.2.cloned.1.call-done.text_ref
  59.7 0.0 copy-start.5
  59.7 1.7 %copy-done.5 = bf16[1024,1152]{1,0:T(8,128)(2,1)S(1)} copy-done((bf16[1024,1152]{1,0:T(8,128)(2,1)S(1)}, bf16[1024,1152]{1,0:T(8,128)(2,1)}, u32[]{:S(2)}) %copy-start.5) | copy-done | bytes 2359320
  61.3 4.2 %shard_map.91 = (bf16[256,1152]{1,0:T(8,128)(2,1)S(1)}, bf16[1024,1152]{1,0:T(8,128)(2,1)}) custom-call(f32[3]{0:T(128)S(1)} %pad_maximum_fusion.1.scal_ref, s32[3]{0:T(128)S(1)} %pad_add_fusion.refs_0_.spot_ref, bf16[256,1152]{1,0:T(8,128)(2,1)S(1)} %get-tuple-element.28.unit_ref, f32[256,1]{1,0:T(8,128)S(1)} %get-tuple-element.29.norm_ref, ...), custom_call_target="tpu_custom_call" | custom-call | flops 1811939328 | bytes 2000000 | tf_op jit(solution)/shard_map/pallas_call | solution.py:224
  65.6 0.0 reduce-scatter.2.cloned.1.call-update
  65.6 1.9 %collective-permute-start.3 = (bf16[256,1152]{1,0:T(8,128)(2,1)S(1)}, bf16[256,1152]{1,0:T(8,128)(2,1)S(1)}, u32[]{:S(2)}, u32[]{:S(2)}) collective-permute-start(bf16[256,1152]{1,0:T(8,128)(2,1)S(1)} %get-tuple-element.31.back_ref), channel_id=1, source_target_pairs={{0,1},{1,0},{2,3},{3,2},{4,5},{5,4},{6,7},{7,6},{8,9},{9,8},{10,11... | collective-permute-start | bytes 1769480 | tf_op jit(solution)/shard_map/ppermute | solution.py:24
  67.5 2.0 %collective-permute-done.3.there_ref = bf16[256,1152]{1,0:T(8,128)(2,1)S(1)} collective-permute-done((bf16[256,1152]{1,0:T(8,128)(2,1)S(1)}, bf16[256,1152]{1,0:T(8,128)(2,1)S(1)}, u32[]{:S(2)}, u32[]{:S(2)}) %collective-permute-start.3) | collective-permute-done | bytes 589856 | tf_op jit(solution)/shard_map/ppermute | solution.py:24
  69.5 0.9 shard_map.92
  70.4 21.5 %all_to_all.20.came_ref = bf16[4,144,1152]{2,1,0:T(8,128)(2,1)S(1)} all-to-all(bf16[4,144,1152]{2,1,0:T(8,128)(2,1)S(1)} %bitcast.10), channel_id=1, replica_groups=mesh['zl'=2,'y'=8,'x'=4,'zh'=4,'c'=2] {'x'}, dimensions={0} | all-to-all | bytes 2654208 | tf_op jit(solution)/shard_map/all_to_all | solution.py:238
  92.0 0.4 shard_map.93
  92.3 0.0 copy-start
  92.4 0.0 copy-start.3
  92.4 20.2 %all_to_all.21 = bf16[8,168,128]{2,1,0:T(8,128)(2,1)S(1)} all-to-all(bf16[8,168,128]{2,1,0:T(8,128)(2,1)S(1)} %shard_map.93), channel_id=1, replica_groups=mesh['zl'=2,'y'=8,'x'=4,'zh'=4,'c'=2] {'zh','zl'}, dimensions={0} | all-to-all | bytes 688128 | tf_op jit(solution)/shard_map/all_to_all | solution.py:247
  112.6 0.1 reduce_sum.12
  112.7 15.2 %all_to_all.22.came_ref = bf16[8,168,128]{2,1,0:T(8,128)(2,1)S(1)} all-to-all(bf16[8,168,128]{2,1,0:T(8,128)(2,1)S(1)} %broadcast_in_dim.8), channel_id=1, replica_groups=mesh['zl'=2,'y'=8,'x'=4,'zh'=4,'c'=2] {'y'}, dimensions={0} | all-to-all | bytes 688128 | tf_op jit(solution)/shard_map/all_to_all | solution.py:249
  127.8 0.1 shard_map.94
  127.9 2.5 %collective-permute-start.4 = (f32[18,1152]{1,0:T(8,128)S(1)}, f32[18,1152]{1,0:T(8,128)S(1)}, u32[]{:S(2)}, u32[]{:S(2)}) collective-permute-start(f32[18,1152]{1,0:T(8,128)S(1)} %shard_map.94), channel_id=1, source_target_pairs={{0,256},{256,0},{1,257},{257,1},{2,258},{258,2},{3,259},{259,3},{4... | collective-permute-start | bytes 248840 | tf_op jit(solution)/shard_map/ppermute | solution.py:24
  130.4 0.0 reduce-scatter.2.cloned.1.call-done
  130.4 0.0 copy-done
  130.4 0.0 copy-done.3
  130.4 0.0 copy-start.2
  130.4 1.0 copy-done.2
  131.4 2.4 %shard_map.95 = f32[256,1152]{1,0:T(8,128)} custom-call(f32[3]{0:T(128)S(1)} %pad_maximum_fusion.1.scal_ref, s32[1,128]{1,0:T(1,128)S(1)} %bitcast.14, bf16[128,1152]{1,0:T(8,128)(2,1)S(1)} %bitcast.11, bf16[128,1152]{1,0:T(8,128)(2,1)S(1)} %copy-done, f32[128,1]{1,0:T(8,128)S(1)} %copy-done.3), custom_call_target="tpu_custom_call" | custom-call | flops 226492416 | bytes 2000000 | tf_op jit(solution)/shard_map/pallas_call | solution.py:253
  133.8 0.7 collective-permute-done.4
  134.6 0.7 pad_maximum_fusion
  (2 shorter events, 0.1 us)
Async XLA Ops:
  7.2 52.5 %all-gather.2.cloned.1.call-start = ((), (), s32[]{:S(2)}) async-start(), calls=%async_computation.5 | async-start | bytes 2654208 | tf_op jit(solution)/shard_map/all_gather | solution.py:198
  31.5 5.0 %copy-start.1 = (bf16[256,1152]{1,0:T(8,128)(2,1)S(1)}, bf16[256,1152]{1,0:T(8,128)(2,1)}, u32[]{:S(2)}) copy-start(bf16[256,1152]{1,0:T(8,128)(2,1)} %cand_ref.1) | copy-start | bytes 1769476
  31.5 5.0 %copy-start.4 = (s32[128]{0:T(128)S(1)}, s32[128]{0:T(128)}, u32[]{:S(2)}) copy-start(s32[128]{0:T(128)} %param.9) | copy-start | bytes 1540
  31.5 21.5 %all-to-all-start = ((bf16[4,160,1152]{2,1,0:T(8,128)(2,1)}), bf16[4,160,1152]{2,1,0:T(8,128)(2,1)S(1)}, u32[]{:S(2)}, u32[]{:S(2)}) async-start(bf16[4,160,1152]{2,1,0:T(8,128)(2,1)} %broadcast_in_dim.7), calls=%async_computation | async-start | bytes 2949120 | tf_op jit(solution)/shard_map/all_to_all | solution.py:206
  36.5 93.9 %reduce-scatter.2.cloned.1.call-start = ((), (), s32[]{:S(2)}) async-start(), calls=%async_computation.6 | async-start | bytes 2654208 | tf_op jit(solution)/shard_map/reduce_scatter | solution.py:232
  36.8 8.6 %collective-permute-start = (bf16[128,1152]{1,0:T(8,128)(2,1)S(1)}, bf16[128,1152]{1,0:T(8,128)(2,1)S(1)}, u32[]{:S(2)}, u32[]{:S(2)}) collective-permute-start(bf16[128,1152]{1,0:T(8,128)(2,1)S(1)} %shard_map.87.refs_1_), channel_id=1, source_target_pairs={{0,256},{256,0},{1,257},{257,1},{2,258},{258,2},{3,259},{259,3},{4... | collective-permute-start | bytes 884744 | tf_op jit(solution)/shard_map/ppermute | solution.py:24
  46.7 3.5 %collective-permute-start.1 = (bf16[576,256]{1,0:T(8,128)(2,1)S(1)}, bf16[576,256]{1,0:T(8,128)(2,1)S(1)}, u32[]{:S(2)}, u32[]{:S(2)}) collective-permute-start(bf16[576,256]{1,0:T(8,128)(2,1)S(1)} %get-tuple-element.23), channel_id=1, source_target_pairs={{0,1},{1,0},{2,3},{3,2},{4,5},{5,4},{6,7},{7,6},{8,9},{9,8},{10,11... | collective-permute-start | bytes 884744 | tf_op jit(solution)/shard_map/ppermute | solution.py:24
  53.0 5.2 %collective-permute-start.2 = (bf16[640,1152]{1,0:T(8,128)(2,1)S(1)}, bf16[640,1152]{1,0:T(8,128)(2,1)S(1)}, u32[]{:S(2)}, u32[]{:S(2)}) collective-permute-start(bf16[640,1152]{1,0:T(8,128)(2,1)S(1)} %bitcast.8), channel_id=1, source_target_pairs={{0,1},{1,0},{2,3},{3,2},{4,5},{5,4},{6,7},{7,6},{8,9},{9,8},{10,11... | collective-permute-start | bytes 4423688 | tf_op jit(solution)/shard_map/ppermute | solution.py:24
  59.7 1.7 %copy-start.5 = (bf16[1024,1152]{1,0:T(8,128)(2,1)S(1)}, bf16[1024,1152]{1,0:T(8,128)(2,1)}, u32[]{:S(2)}) copy-start(bf16[1024,1152]{1,0:T(8,128)(2,1)} %all-gather.2.cloned.1.call-done.text_ref) | copy-start | bytes 7077892
  65.6 3.9 %collective-permute-start.3 = (bf16[256,1152]{1,0:T(8,128)(2,1)S(1)}, bf16[256,1152]{1,0:T(8,128)(2,1)S(1)}, u32[]{:S(2)}, u32[]{:S(2)}) collective-permute-start(bf16[256,1152]{1,0:T(8,128)(2,1)S(1)} %get-tuple-element.31.back_ref), channel_id=1, source_target_pairs={{0,1},{1,0},{2,3},{3,2},{4,5},{5,4},{6,7},{7,6},{8,9},{9,8},{10,11... | collective-permute-start | bytes 1769480 | tf_op jit(solution)/shard_map/ppermute | solution.py:24
  92.3 38.1 %copy-start = (bf16[128,1152]{1,0:T(8,128)(2,1)S(1)}, bf16[128,1152]{1,0:T(8,128)(2,1)}, u32[]{:S(2)}) copy-start(bf16[128,1152]{1,0:T(8,128)(2,1)} %get-tuple-element.30.unit_ref) | copy-start | bytes 884740
  92.4 38.1 %copy-start.3 = (f32[128,1]{1,0:T(8,128)S(1)}, f32[128,1]{1,0:T(8,128)}, u32[]{:S(2)}) copy-start(f32[128,1]{1,0:T(8,128)} %get-tuple-element.33.norm_ref) | copy-start | bytes 1540
  127.9 6.6 %collective-permute-start.4 = (f32[18,1152]{1,0:T(8,128)S(1)}, f32[18,1152]{1,0:T(8,128)S(1)}, u32[]{:S(2)}, u32[]{:S(2)}) collective-permute-start(f32[18,1152]{1,0:T(8,128)S(1)} %shard_map.94), channel_id=1, source_target_pairs={{0,256},{256,0},{1,257},{257,1},{2,258},{258,2},{3,259},{259,3},{4... | collective-permute-start | bytes 248840 | tf_op jit(solution)/shard_map/ppermute | solution.py:24
  130.4 1.0 copy-start.2
Sparse Core Ops, SparseCore 0:
  10.7 48.9 all-gather.1
  65.7 43.9 reduce-scatter.1

commit v9 on v8

--- a/solution.py
+++ b/solution.py
@@ -61,7 +61,7 @@
     out_ref[...] = pick_rows(chosen_ref[...], cand_ref[...]).astype(BF16)
 
 
-def pair_kernel(size, spot_ref, mine_ref, there_ref, deep_mine_ref, deep_other_ref, cols_mine_ref, cols_other_ref,
+def pair_kernel(size, n_zh, spot_ref, mine_ref, there_ref, deep_mine_ref, deep_other_ref, cols_mine_ref, cols_other_ref,
                 flat_ref, group_ref, deep_ref):
     pairs, depth = mine_ref.shape
     first = spot_ref[0] == 0
@@ -72,7 +72,10 @@
     for block in range(depth // size):
         core, place = block % 2, block // 2
         rows = flat_ref[block * size:(block + 1) * size, :]
-        group_ref[core, place * size:(place + 1) * size, :] = rows
+        part = size // 2
+        start = (place // n_zh * 2 * n_zh + place % n_zh) * part
+        group_ref[core, start:start + part, :] = rows[:part]
+        group_ref[core, start + n_zh * part:start + (n_zh + 1) * part, :] = rows[part:]
         deep_ref[core, place * PADDED:place * PADDED + size, :] = rows
     core = spot_ref[2]
     cols_mine_ref[...] = group_ref[core].astype(BF16)
@@ -182,7 +185,7 @@
     cands, depth = image_cand.shape
     own_rows, width = head_weight.shape
     rows = 2 * pairs
-    n_y, n_x = lax.axis_size("y"), lax.axis_size("x")
+    n_y, n_x, n_zh = lax.axis_size("y"), lax.axis_size("x"), lax.axis_size("zh")
     my_zl, my_y, core = (lax.axis_index(a) for a in ("zl", "y", "c"))
     total = pairs * lax.axis_size(ALL)
     spot = jnp.stack([my_zl * pairs, my_y * pairs, core])
@@ -207,7 +210,7 @@
     mine = slabs.reshape(n_x * slab.shape[0], width)
     deep = mine.shape[0]
     deep_mine, deep_other, cols_mine, cols_other = call(
-        lambda *refs: pair_kernel(own_rows, *refs),
+        lambda *refs: pair_kernel(own_rows, n_zh, *refs),
         [((rows, deep), BF16), ((rows, deep), BF16), ((depth // 2, rows), BF16), ((depth // 2, rows), BF16)],
         [SMEM, VMEM, VMEM], (VMEM,) * 4,
         [pltpu.VMEM((depth, rows), F32), pltpu.VMEM((2, depth // 2, rows), F32), pltpu.VMEM((2, deep, rows), F32)],
@@ -234,17 +237,16 @@
         join_kernel, [((depth // 2, width), BF16)], [VMEM] * 4, (VMEM,), cost=2 * rows * depth * width,
     )(cols_mine, cols_there, proj_back, hop(proj_back, "c", 1))
 
-    share = depth // 2 // n_x
-    came = lax.all_to_all(head.reshape(n_x, share, width), "x", 0, 0)
-    n_z = lax.axis_size(("zh", "zl"))
-    piece = share // n_z
+    share = depth // 4 // n_x
+    came = lax.all_to_all(head.reshape(2 * n_x, share, width), ("x", "zl"), 0, 0)
+    piece = share // n_zh
     strips = piece * (width // LANES)
     strips += -strips % 8
     (folded,) = call(
-        fold_kernel, [((n_z, strips, LANES), BF16)], [VMEM], (VMEM,),
-        [pltpu.VMEM((share, width), F32), pltpu.VMEM((n_z, strips, LANES), F32)],
+        fold_kernel, [((n_zh, strips, LANES), BF16)], [VMEM], (VMEM,),
+        [pltpu.VMEM((share, width), F32), pltpu.VMEM((n_zh, strips, LANES), F32)],
     )(came)
-    came = lax.all_to_all(folded, ("zh", "zl"), 0, 0)
+    came = lax.all_to_all(folded, "zh", 0, 0)
     head = jnp.sum(came.astype(F32), axis=0).astype(BF16)
     came = lax.all_to_all(jnp.broadcast_to(head[None], (n_y,) + head.shape), "y", 0, 0)
     (head,) = call(unfold_kernel, [((piece, width), F32)], [VMEM], (VMEM,), [pltpu.VMEM((strips, LANES), F32)])(came)

time: 143 us -> 140 us (0.979)
  blocking collectives: 77.7 us -> 75.1 us
    all_to_all x2, blocking collectives: 41.7 us -> 38.9 us  [the longest x1 23.5 us: shards(): lax.all_to_all(head.reshape(2 * n_x, share, width), ('x', 'zl'), 0, 0)]
where the time goes in v9:
time: 140 us; the launch traced here: 139 us
  blocking collectives  75.1 us (54%)
  starting transfers between devices  16.8 us (12%)
  between operations  16.1 us (12%)
  Pallas kernels  13.4 us (10%)
  waiting for transfers between devices  13.2 us (9%)
  local copies, waits for them, and re-layouts  3.89 us (3%)
    all_to_all x1, blocking collectives, shards(): lax.all_to_all(head.reshape(2 * n_x, share, width), ('x', 'zl'), 0, 0)  23.5 us
    all_gather x1, blocking collectives, shards(): slab = lax.all_gather(part, 'zh', axis=0, tiled=True)  20.8 us
    all_to_all x1, blocking collectives, shards(): came = lax.all_to_all(folded, 'zh', 0, 0)  15.5 us
    all_to_all x1, blocking collectives, shards(): lax.all_to_all(jnp.broadcast_to(head[None], (n_y,) + head.shape), 'y', 0, 0)  15.4 us
    ppermute x5, starting transfers between devices, hop(): lax.ppermute(value, axis, [(s, (s + steps) % count) for s in range(count)])  11.8 us
    ppermute x5, waiting for transfers between devices, hop(): lax.ppermute(value, axis, [(s, (s + steps) % count) for s in range(count)])  9.71 us
    all_to_all x1, starting transfers between devices, shards(): lax.all_to_all(jnp.broadcast_to(slab[None], (n_x,) + slab.shape), 'x', 0, 0)  4.95 us
    pallas_call x1, Pallas kernels, shards(): call(main_kernel, [((rows, width), BF16), ((n_y * pairs, width), BF16)],...  4.24 us
  transfers between devices with their start and end apart: 8, of which 7 were waited for; matrix products, arithmetic and copies ran while one was open for 1% of the time, Pallas kernels for 5%

profile of v9, /device:TPU:2, one launch (start us, length us, event | category | flops | bytes accessed | tf_op | source)
XLA Modules:
  0.0 139.4 jit_solution(10618814367413303295)
XLA Ops:
  7.2 0.0 all-gather.2.cloned.1.call-start
  7.2 2.3 %shard_map.86 = (bf16[128,1152]{1,0:T(8,128)(2,1)}, f32[128,1]{1,0:T(8,128)}, bf16[40,1152]{1,0:T(8,128)(2,1)}) custom-call(s32[1,128]{1,0:T(1,128)} %bitcast.12, bf16[256,1152]{1,0:T(8,128)(2,1)} %cand_hbm.1, bf16[36,1152]{1,0:T(8,128)(2,1)} %weight_hbm.1), custom_call_target="tpu_custom_call" | custom-call | flops 75497472 | bytes 2000000 | tf_op jit(solution)/shard_map/pallas_call | solution.py:195
  9.5 0.0 all-gather.2.cloned.1.call-update
  9.5 20.8 %all_gather.6 = bf16[160,1152]{1,0:T(8,128)(2,1)S(1)} all-gather(bf16[40,1152]{1,0:T(8,128)(2,1)} %get-tuple-element.19), channel_id=1, replica_groups=mesh['zl'=2,'y'=8,'x'=4,'zh'=4,'c'=2] {'zh'}, dimensions={0}, use_global_device_ids=true | all-gather | bytes 460800 | tf_op jit(solution)/shard_map/all_gather | solution.py:203
  30.3 1.2 broadcast_in_dim.7
  31.5 0.0 copy-start.1
  31.5 0.0 copy-start.4
  31.5 5.0 %all-to-all-start = ((bf16[4,160,1152]{2,1,0:T(8,128)(2,1)}), bf16[4,160,1152]{2,1,0:T(8,128)(2,1)S(1)}, u32[]{:S(2)}, u32[]{:S(2)}) async-start(bf16[4,160,1152]{2,1,0:T(8,128)(2,1)} %broadcast_in_dim.7), calls=%async_computation | async-start | bytes 2949120 | tf_op jit(solution)/shard_map/all_to_all | solution.py:209
  36.5 0.0 reduce-scatter.2.cloned.1.call-start
  36.5 0.0 copy-done.1
  36.5 0.0 copy-done.4
  36.5 0.3 shard_map.87.refs_1_
  36.8 3.4 %collective-permute-start = (bf16[128,1152]{1,0:T(8,128)(2,1)S(1)}, bf16[128,1152]{1,0:T(8,128)(2,1)S(1)}, u32[]{:S(2)}, u32[]{:S(2)}) collective-permute-start(bf16[128,1152]{1,0:T(8,128)(2,1)S(1)} %shard_map.87.refs_1_), channel_id=1, source_target_pairs={{0,256},{256,0},{1,257},{257,1},{2,258},{258,2},{3,259},{259,3},{4... | collective-permute-start | bytes 884744 | tf_op jit(solution)/shard_map/ppermute | solution.py:24
  40.2 0.1 pad_add_fusion.refs_0_.spot_ref
  40.3 5.1 %collective-permute-done.refs_2_ = bf16[128,1152]{1,0:T(8,128)(2,1)S(1)} collective-permute-done((bf16[128,1152]{1,0:T(8,128)(2,1)S(1)}, bf16[128,1152]{1,0:T(8,128)(2,1)S(1)}, u32[]{:S(2)}, u32[]{:S(2)}) %collective-permute-start) | collective-permute-done | bytes 294944 | tf_op jit(solution)/shard_map/ppermute | solution.py:24
  45.4 1.3 shard_map.88
  46.7 1.9 %collective-permute-start.1 = (bf16[576,256]{1,0:T(8,128)(2,1)S(1)}, bf16[576,256]{1,0:T(8,128)(2,1)S(1)}, u32[]{:S(2)}, u32[]{:S(2)}) collective-permute-start(bf16[576,256]{1,0:T(8,128)(2,1)S(1)} %get-tuple-element.23), channel_id=1, source_target_pairs={{0,1},{1,0},{2,3},{3,2},{4,5},{5,4},{6,7},{7,6},{8,9},{9,8},{10,11... | collective-permute-start | bytes 884744 | tf_op jit(solution)/shard_map/ppermute | solution.py:24
  48.7 1.5 %collective-permute-done.1.cols_there_ref = bf16[576,256]{1,0:T(8,128)(2,1)S(1)} collective-permute-done((bf16[576,256]{1,0:T(8,128)(2,1)S(1)}, bf16[576,256]{1,0:T(8,128)(2,1)S(1)}, u32[]{:S(2)}, u32[]{:S(2)}) %collective-permute-start.1) | collective-permute-done | bytes 294944 | tf_op jit(solution)/shard_map/ppermute | solution.py:24
  50.2 2.8 %all-to-all-done = bf16[4,160,1152]{2,1,0:T(8,128)(2,1)S(1)} async-done(((bf16[4,160,1152]{2,1,0:T(8,128)(2,1)}), bf16[4,160,1152]{2,1,0:T(8,128)(2,1)S(1)}, u32[]{:S(2)}, u32[]{:S(2)}) %all-to-all-start) | async-done | bytes 1474592 | tf_op jit(solution)/shard_map/all_to_all | solution.py:209
  53.0 1.9 %collective-permute-start.2 = (bf16[640,1152]{1,0:T(8,128)(2,1)S(1)}, bf16[640,1152]{1,0:T(8,128)(2,1)S(1)}, u32[]{:S(2)}, u32[]{:S(2)}) collective-permute-start(bf16[640,1152]{1,0:T(8,128)(2,1)S(1)} %bitcast.8), channel_id=1, source_target_pairs={{0,1},{1,0},{2,3},{3,2},{4,5},{5,4},{6,7},{7,6},{8,9},{9,8},{10,11... | collective-permute-start | bytes 4423688 | tf_op jit(solution)/shard_map/ppermute | solution.py:24
  56.9 0.1 pad_maximum_fusion.1.scal_ref
  57.0 0.7 shard_map.89.half_ref
  57.6 0.5 collective-permute-done.2.weight_ref
  58.2 0.8 shard_map.90
  59.0 0.6 all-gather.2.cloned.1.call-done.text_ref
  59.7 0.0 copy-start.5
  59.7 1.7 %copy-done.5 = bf16[1024,1152]{1,0:T(8,128)(2,1)S(1)} copy-done((bf16[1024,1152]{1,0:T(8,128)(2,1)S(1)}, bf16[1024,1152]{1,0:T(8,128)(2,1)}, u32[]{:S(2)}) %copy-start.5) | copy-done | bytes 2359320
  61.3 4.2 %shard_map.91 = (bf16[256,1152]{1,0:T(8,128)(2,1)S(1)}, bf16[1024,1152]{1,0:T(8,128)(2,1)}) custom-call(f32[3]{0:T(128)S(1)} %pad_maximum_fusion.1.scal_ref, s32[3]{0:T(128)S(1)} %pad_add_fusion.refs_0_.spot_ref, bf16[256,1152]{1,0:T(8,128)(2,1)S(1)} %get-tuple-element.28.unit_ref, f32[256,1]{1,0:T(8,128)S(1)} %get-tuple-element.29.norm_ref, ...), custom_call_target="tpu_custom_call" | custom-call | flops 1811939328 | bytes 2000000 | tf_op jit(solution)/shard_map/pallas_call | solution.py:227
  65.6 0.0 reduce-scatter.2.cloned.1.call-update
  65.6 1.9 %collective-permute-start.3 = (bf16[256,1152]{1,0:T(8,128)(2,1)S(1)}, bf16[256,1152]{1,0:T(8,128)(2,1)S(1)}, u32[]{:S(2)}, u32[]{:S(2)}) collective-permute-start(bf16[256,1152]{1,0:T(8,128)(2,1)S(1)} %get-tuple-element.31.back_ref), channel_id=1, source_target_pairs={{0,1},{1,0},{2,3},{3,2},{4,5},{5,4},{6,7},{7,6},{8,9},{9,8},{10,11... | collective-permute-start | bytes 1769480 | tf_op jit(solution)/shard_map/ppermute | solution.py:24
  67.5 2.0 %collective-permute-done.3.there_ref = bf16[256,1152]{1,0:T(8,128)(2,1)S(1)} collective-permute-done((bf16[256,1152]{1,0:T(8,128)(2,1)S(1)}, bf16[256,1152]{1,0:T(8,128)(2,1)S(1)}, u32[]{:S(2)}, u32[]{:S(2)}) %collective-permute-start.3) | collective-permute-done | bytes 589856 | tf_op jit(solution)/shard_map/ppermute | solution.py:24
  69.5 0.9 shard_map.92
  70.4 23.5 %all_to_all.20.came_ref = bf16[8,72,1152]{2,1,0:T(8,128)(2,1)S(1)} all-to-all(bf16[8,72,1152]{2,1,0:T(8,128)(2,1)S(1)} %bitcast.10), channel_id=1, replica_groups=mesh['zl'=2,'y'=8,'x'=4,'zh'=4,'c'=2] {'x','zl'}, dimensions={0} | all-to-all | bytes 2654208 | tf_op jit(solution)/shard_map/all_to_all | solution.py:241
  93.9 0.0 copy-start
  93.9 0.0 copy-start.3
  93.9 0.3 shard_map.93
  94.2 15.5 %all_to_all.21 = bf16[4,168,128]{2,1,0:T(8,128)(2,1)S(1)} all-to-all(bf16[4,168,128]{2,1,0:T(8,128)(2,1)S(1)} %shard_map.93), channel_id=1, replica_groups=mesh['zl'=2,'y'=8,'x'=4,'zh'=4,'c'=2] {'zh'}, dimensions={0} | all-to-all | bytes 344064 | tf_op jit(solution)/shard_map/all_to_all | solution.py:249
  109.8 15.4 %all_to_all.22.came_ref = bf16[8,168,128]{2,1,0:T(8,128)(2,1)S(1)} all-to-all(bf16[8,168,128]{2,1,0:T(8,128)(2,1)S(1)} %broadcast_in_dim.8), channel_id=1, replica_groups=mesh['zl'=2,'y'=8,'x'=4,'zh'=4,'c'=2] {'y'}, dimensions={0} | all-to-all | bytes 688128 | tf_op jit(solution)/shard_map/all_to_all | solution.py:251
  125.2 0.1 shard_map.94
  125.2 2.6 %collective-permute-start.4 = (f32[18,1152]{1,0:T(8,128)S(1)}, f32[18,1152]{1,0:T(8,128)S(1)}, u32[]{:S(2)}, u32[]{:S(2)}) collective-permute-start(f32[18,1152]{1,0:T(8,128)S(1)} %shard_map.94), channel_id=1, source_target_pairs={{0,256},{256,0},{1,257},{257,1},{2,258},{258,2},{3,259},{259,3},{4... | collective-permute-start | bytes 248840 | tf_op jit(solution)/shard_map/ppermute | solution.py:24
  127.9 0.0 reduce-scatter.2.cloned.1.call-done
  127.9 0.0 copy-done
  127.9 0.0 copy-done.3
  127.9 0.0 copy-start.2
  128.0 1.0 copy-done.2
  128.9 2.4 %shard_map.95 = f32[256,1152]{1,0:T(8,128)} custom-call(f32[3]{0:T(128)S(1)} %pad_maximum_fusion.1.scal_ref, s32[1,128]{1,0:T(1,128)S(1)} %bitcast.14, bf16[128,1152]{1,0:T(8,128)(2,1)S(1)} %bitcast.11, bf16[128,1152]{1,0:T(8,128)(2,1)S(1)} %copy-done, f32[128,1]{1,0:T(8,128)S(1)} %copy-done.3), custom_call_target="tpu_custom_call" | custom-call | flops 226492416 | bytes 2000000 | tf_op jit(solution)/shard_map/pallas_call | solution.py:255
  131.3 0.5 collective-permute-done.4
  131.9 0.7 pad_maximum_fusion
  (3 shorter events, 0.1 us)
Async XLA Ops:
  7.2 52.5 %all-gather.2.cloned.1.call-start = ((), (), s32[]{:S(2)}) async-start(), calls=%async_computation.5 | async-start | bytes 2654208 | tf_op jit(solution)/shard_map/all_gather | solution.py:201
  31.5 5.0 %copy-start.1 = (bf16[256,1152]{1,0:T(8,128)(2,1)S(1)}, bf16[256,1152]{1,0:T(8,128)(2,1)}, u32[]{:S(2)}) copy-start(bf16[256,1152]{1,0:T(8,128)(2,1)} %cand_ref.1) | copy-start | bytes 1769476
  31.5 5.0 %copy-start.4 = (s32[128]{0:T(128)S(1)}, s32[128]{0:T(128)}, u32[]{:S(2)}) copy-start(s32[128]{0:T(128)} %param.9) | copy-start | bytes 1540
  31.5 21.5 %all-to-all-start = ((bf16[4,160,1152]{2,1,0:T(8,128)(2,1)}), bf16[4,160,1152]{2,1,0:T(8,128)(2,1)S(1)}, u32[]{:S(2)}, u32[]{:S(2)}) async-start(bf16[4,160,1152]{2,1,0:T(8,128)(2,1)} %broadcast_in_dim.7), calls=%async_computation | async-start | bytes 2949120 | tf_op jit(solution)/shard_map/all_to_all | solution.py:209
  36.5 91.4 %reduce-scatter.2.cloned.1.call-start = ((), (), s32[]{:S(2)}) async-start(), calls=%async_computation.6 | async-start | bytes 2654208 | tf_op jit(solution)/shard_map/reduce_scatter | solution.py:235
  36.8 8.6 %collective-permute-start = (bf16[128,1152]{1,0:T(8,128)(2,1)S(1)}, bf16[128,1152]{1,0:T(8,128)(2,1)S(1)}, u32[]{:S(2)}, u32[]{:S(2)}) collective-permute-start(bf16[128,1152]{1,0:T(8,128)(2,1)S(1)} %shard_map.87.refs_1_), channel_id=1, source_target_pairs={{0,256},{256,0},{1,257},{257,1},{2,258},{258,2},{3,259},{259,3},{4... | collective-permute-start | bytes 884744 | tf_op jit(solution)/shard_map/ppermute | solution.py:24
  46.7 3.5 %collective-permute-start.1 = (bf16[576,256]{1,0:T(8,128)(2,1)S(1)}, bf16[576,256]{1,0:T(8,128)(2,1)S(1)}, u32[]{:S(2)}, u32[]{:S(2)}) collective-permute-start(bf16[576,256]{1,0:T(8,128)(2,1)S(1)} %get-tuple-element.23), channel_id=1, source_target_pairs={{0,1},{1,0},{2,3},{3,2},{4,5},{5,4},{6,7},{7,6},{8,9},{9,8},{10,11... | collective-permute-start | bytes 884744 | tf_op jit(solution)/shard_map/ppermute | solution.py:24
  53.0 5.2 %collective-permute-start.2 = (bf16[640,1152]{1,0:T(8,128)(2,1)S(1)}, bf16[640,1152]{1,0:T(8,128)(2,1)S(1)}, u32[]{:S(2)}, u32[]{:S(2)}) collective-permute-start(bf16[640,1152]{1,0:T(8,128)(2,1)S(1)} %bitcast.8), channel_id=1, source_target_pairs={{0,1},{1,0},{2,3},{3,2},{4,5},{5,4},{6,7},{7,6},{8,9},{9,8},{10,11... | collective-permute-start | bytes 4423688 | tf_op jit(solution)/shard_map/ppermute | solution.py:24
  59.7 1.7 %copy-start.5 = (bf16[1024,1152]{1,0:T(8,128)(2,1)S(1)}, bf16[1024,1152]{1,0:T(8,128)(2,1)}, u32[]{:S(2)}) copy-start(bf16[1024,1152]{1,0:T(8,128)(2,1)} %all-gather.2.cloned.1.call-done.text_ref) | copy-start | bytes 7077892
  65.6 3.9 %collective-permute-start.3 = (bf16[256,1152]{1,0:T(8,128)(2,1)S(1)}, bf16[256,1152]{1,0:T(8,128)(2,1)S(1)}, u32[]{:S(2)}, u32[]{:S(2)}) collective-permute-start(bf16[256,1152]{1,0:T(8,128)(2,1)S(1)} %get-tuple-element.31.back_ref), channel_id=1, source_target_pairs={{0,1},{1,0},{2,3},{3,2},{4,5},{5,4},{6,7},{7,6},{8,9},{9,8},{10,11... | collective-permute-start | bytes 1769480 | tf_op jit(solution)/shard_map/ppermute | solution.py:24
  93.9 34.0 %copy-start = (bf16[128,1152]{1,0:T(8,128)(2,1)S(1)}, bf16[128,1152]{1,0:T(8,128)(2,1)}, u32[]{:S(2)}) copy-start(bf16[128,1152]{1,0:T(8,128)(2,1)} %get-tuple-element.30.unit_ref) | copy-start | bytes 884740
  93.9 34.0 %copy-start.3 = (f32[128,1]{1,0:T(8,128)S(1)}, f32[128,1]{1,0:T(8,128)}, u32[]{:S(2)}) copy-start(f32[128,1]{1,0:T(8,128)} %get-tuple-element.33.norm_ref) | copy-start | bytes 1540
  125.2 6.6 %collective-permute-start.4 = (f32[18,1152]{1,0:T(8,128)S(1)}, f32[18,1152]{1,0:T(8,128)S(1)}, u32[]{:S(2)}, u32[]{:S(2)}) collective-permute-start(f32[18,1152]{1,0:T(8,128)S(1)} %shard_map.94), channel_id=1, source_target_pairs={{0,256},{256,0},{1,257},{257,1},{2,258},{258,2},{3,259},{259,3},{4... | collective-permute-start | bytes 248840 | tf_op jit(solution)/shard_map/ppermute | solution.py:24
  127.9 1.0 copy-start.2
Sparse Core Ops, SparseCore 0:
  10.7 48.9 all-gather.1
  65.7 43.9 reduce-scatter.1

commit v10 on v9

--- a/solution.py
+++ b/solution.py
@@ -41,20 +41,17 @@
     return tn((spots == chosen).astype(BF16), cands)
 
 
-def text_kernel(chosen_hbm, cand_hbm, weight_hbm, unit_ref, norm_ref, padded_ref, chosen_ref, cand_ref, weight_ref, wide_ref, sem):
+def text_kernel(chosen_hbm, cand_hbm, unit_ref, norm_ref, chosen_ref, cand_ref, sem):
     loads = [pltpu.make_async_copy(source, target, sem.at[k]) for k, (source, target) in enumerate(
-        ((chosen_hbm, chosen_ref), (cand_hbm, cand_ref), (weight_hbm, weight_ref)))]
+        ((chosen_hbm, chosen_ref), (cand_hbm, cand_ref)))]
     for load in loads:
         load.start()
-    wide_ref[...] = jnp.zeros_like(wide_ref)
     for load in loads:
         load.wait()
     texts = pick_rows(chosen_ref[...], cand_ref[...])
     norm = jnp.sqrt(jnp.sum(texts * texts, axis=1, keepdims=True) + EPS)
     unit_ref[...] = (texts / norm).astype(BF16)
     norm_ref[...] = norm
-    wide_ref[:weight_ref.shape[0], :] = weight_ref[...].astype(F32)
-    padded_ref[...] = wide_ref[...].astype(BF16)
 
 
 def image_kernel(chosen_ref, cand_ref, out_ref):
@@ -125,14 +122,17 @@
         store.wait()
 
 
-def join_kernel(cols_mine_ref, cols_there_ref, back_ref, there_ref, out_ref):
-    out_ref[...] = (nn(cols_mine_ref[...], back_ref[...]) + nn(cols_there_ref[...], there_ref[...])).astype(BF16)
+def join_kernel(own_ref, cols_ref, back_ref, out_ref):
+    out_ref[...] = (own_ref[...] + nn(cols_ref[...], back_ref[...])).astype(BF16)
 
 
 def fold_kernel(came_ref, out_ref, sum_ref, flat_ref):
-    total = came_ref[0].astype(F32)
-    for k in range(1, came_ref.shape[0]):
-        total += came_ref[k].astype(F32)
+    share = sum_ref.shape[0]
+    total = None
+    for k in range(came_ref.shape[0]):
+        both = came_ref[k].astype(F32)
+        both = both[:share] + both[share:]
+        total = both if total is None else total + both
     sum_ref[...] = total
     flat_ref[...] = jnp.zeros_like(flat_ref)
     pieces = flat_ref.shape[0]
@@ -192,14 +192,14 @@
     scalars = jnp.stack([logit_temp[0], logit_offset[0], loss_scale[0] / total])
 
     chosen = selection[None, :]
-    text_unit, txt_norm, part = call(
-        text_kernel, [((pairs, width), BF16), ((pairs, 1), F32), ((PADDED, width), BF16)], [HBM] * 3, (VMEM,) * 3,
-        [pltpu.VMEM((1, pairs), jnp.int32), pltpu.VMEM((cands, depth), BF16), pltpu.VMEM((own_rows, width), BF16),
-         pltpu.VMEM((PADDED, width), F32), pltpu.SemaphoreType.DMA((3,))],
+    text_unit, txt_norm = call(
+        text_kernel, [((pairs, width), BF16), ((pairs, 1), F32)], [HBM] * 2, (VMEM,) * 2,
+        [pltpu.VMEM((1, pairs), jnp.int32), pltpu.VMEM((cands, depth), BF16), pltpu.SemaphoreType.DMA((2,))],
         cost=2 * pairs * cands * width, limit=WHOLE,
-    )(chosen, text_cand, head_weight)
+    )(chosen, text_cand)
     text_all = lax.all_gather(text_unit, "y", axis=0, tiled=True)
 
+    part = jnp.pad(head_weight, ((0, PADDED - own_rows), (0, 0)))
     slab = lax.all_gather(part, "zh", axis=0, tiled=True)
     slab, chosen = lax.optimization_barrier((slab, chosen))
     (picked,) = call(
@@ -233,19 +233,23 @@
         cost=6 * rows * n_y * pairs * width, limit=ROOMY,
     )(scalars, spot, image_unit, img_norm, text_all)
     text_back = lax.psum_scatter(text_part.reshape(n_y, pairs, width), "y", scatter_dimension=0)
+    back_there = hop(proj_back, "c", 1)
+    (own,) = call(
+        half_kernel, [((depth // 2, width), F32)], [VMEM] * 2, (VMEM,), cost=rows * depth * width,
+    )(cols_mine, proj_back)
     (head,) = call(
-        join_kernel, [((depth // 2, width), BF16)], [VMEM] * 4, (VMEM,), cost=2 * rows * depth * width,
-    )(cols_mine, cols_there, proj_back, hop(proj_back, "c", 1))
+        join_kernel, [((depth // 2, width), BF16)], [VMEM] * 3, (VMEM,), cost=rows * depth * width,
+    )(own, cols_there, back_there)
 
     share = depth // 4 // n_x
     came = lax.all_to_all(head.reshape(2 * n_x, share, width), ("x", "zl"), 0, 0)
     piece = share // n_zh
     strips = piece * (width // LANES)
-    strips += -strips % 8
+    strips += -strips % 16
     (folded,) = call(
         fold_kernel, [((n_zh, strips, LANES), BF16)], [VMEM], (VMEM,),
         [pltpu.VMEM((share, width), F32), pltpu.VMEM((n_zh, strips, LANES), F32)],
-    )(came)
+    )(came.reshape(n_x, 2 * share, width))
     came = lax.all_to_all(folded, "zh", 0, 0)
     head = jnp.sum(came.astype(F32), axis=0).astype(BF16)
     came = lax.all_to_all(jnp.broadcast_to(head[None], (n_y,) + head.shape), "y", 0, 0)

time: 140 us -> 140 us (level)
    pallas_call x2 -> x3, Pallas kernels: 3.22 us -> 3.34 us  [the longest x1 2.24 us: shards(): call(text_kernel, [((pairs, width), BF16), ((pairs, 1), F32)], [HBM] * 2,...]
  transfers between devices with their start and end apart: 8 -> 8, of which waited for: 7 -> 6; matrix products, arithmetic and copies ran while one was open for 1% -> 2% of each run, Pallas kernels for 5% -> 5%
where the time goes in v10:
time: 140 us; the launch traced here: 139 us
  blocking collectives  75.2 us (54%)
  starting transfers between devices  17 us (12%)
  between operations  16.2 us (12%)
  Pallas kernels  13.5 us (10%)
  waiting for transfers between devices  11.9 us (8%)
  local copies, waits for them, and re-layouts  4.79 us (3%)
    all_to_all x1, blocking collectives, shards(): lax.all_to_all(head.reshape(2 * n_x, share, width), ('x', 'zl'), 0, 0)  23.4 us
    all_gather x1, blocking collectives, shards(): slab = lax.all_gather(part, 'zh', axis=0, tiled=True)  20.6 us
    all_to_all x1, blocking collectives, shards(): came = lax.all_to_all(folded, 'zh', 0, 0)  15.7 us
    all_to_all x1, blocking collectives, shards(): lax.all_to_all(jnp.broadcast_to(head[None], (n_y,) + head.shape), 'y', 0, 0)  15.5 us
    ppermute x5, starting transfers between devices, hop(): lax.ppermute(value, axis, [(s, (s + steps) % count) for s in range(count)])  12 us
    ppermute x5, waiting for transfers between devices, hop(): lax.ppermute(value, axis, [(s, (s + steps) % count) for s in range(count)])  9.02 us
    all_to_all x1, starting transfers between devices, shards(): lax.all_to_all(jnp.broadcast_to(slab[None], (n_x,) + slab.shape), 'x', 0, 0)  4.96 us
    pallas_call x1, Pallas kernels, shards(): call(main_kernel, [((rows, width), BF16), ((n_y * pairs, width), BF16)],...  4.24 us
  transfers between devices with their start and end apart: 8, of which 6 were waited for; matrix products, arithmetic and copies ran while one was open for 2% of the time, Pallas kernels for 5%

profile of v10, /device:TPU:2, one launch (start us, length us, event | category | flops | bytes accessed | tf_op | source)
XLA Modules:
  0.0 139.4 jit_solution(16356189099668026742)
XLA Ops:
  7.2 0.0 all-gather.2.cloned.1.call-start
  7.2 2.2 %shard_map.90 = (bf16[128,1152]{1,0:T(8,128)(2,1)}, f32[128,1]{1,0:T(8,128)}) custom-call(s32[1,128]{1,0:T(1,128)} %bitcast.14, bf16[256,1152]{1,0:T(8,128)(2,1)} %cand_hbm.1), custom_call_target="tpu_custom_call" | custom-call | flops 75497472 | bytes 2000000 | tf_op jit(solution)/shard_map/pallas_call | solution.py:195
  9.5 0.0 all-gather.2.cloned.1.call-update
  9.5 0.9 pad.4
  10.4 20.6 %all_gather.6 = bf16[160,1152]{1,0:T(8,128)(2,1)S(1)} all-gather(bf16[40,1152]{1,0:T(8,128)(2,1)S(1)} %pad.4), channel_id=1, replica_groups=mesh['zl'=2,'y'=8,'x'=4,'zh'=4,'c'=2] {'zh'}, dimensions={0}, use_global_device_ids=true | all-gather | bytes 460800 | tf_op jit(solution)/shard_map/all_gather | solution.py:203
  31.0 1.2 broadcast_in_dim.7
  32.2 0.0 copy-start.1
  32.2 0.0 copy-start.4
  32.2 5.0 %all-to-all-start = ((bf16[4,160,1152]{2,1,0:T(8,128)(2,1)}), bf16[4,160,1152]{2,1,0:T(8,128)(2,1)S(1)}, u32[]{:S(2)}, u32[]{:S(2)}) async-start(bf16[4,160,1152]{2,1,0:T(8,128)(2,1)} %broadcast_in_dim.7), calls=%async_computation | async-start | bytes 2949120 | tf_op jit(solution)/shard_map/all_to_all | solution.py:209
  37.1 0.0 reduce-scatter.2.cloned.1.call-start
  37.1 0.0 copy-done.1
  37.1 0.0 copy-done.4
  37.2 0.3 shard_map.86.refs_1_
  37.4 3.4 %collective-permute-start = (bf16[128,1152]{1,0:T(8,128)(2,1)S(1)}, bf16[128,1152]{1,0:T(8,128)(2,1)S(1)}, u32[]{:S(2)}, u32[]{:S(2)}) collective-permute-start(bf16[128,1152]{1,0:T(8,128)(2,1)S(1)} %shard_map.86.refs_1_), channel_id=1, source_target_pairs={{0,256},{256,0},{1,257},{257,1},{2,258},{258,2},{3,259},{259,3},{4... | collective-permute-start | bytes 884744 | tf_op jit(solution)/shard_map/ppermute | solution.py:24
  40.9 0.1 pad_add_fusion.refs_0_.spot_ref
  40.9 5.1 %collective-permute-done.refs_2_ = bf16[128,1152]{1,0:T(8,128)(2,1)S(1)} collective-permute-done((bf16[128,1152]{1,0:T(8,128)(2,1)S(1)}, bf16[128,1152]{1,0:T(8,128)(2,1)S(1)}, u32[]{:S(2)}, u32[]{:S(2)}) %collective-permute-start) | collective-permute-done | bytes 294944 | tf_op jit(solution)/shard_map/ppermute | solution.py:24
  46.1 1.3 shard_map.87
  47.4 1.9 %collective-permute-start.1 = (bf16[576,256]{1,0:T(8,128)(2,1)S(1)}, bf16[576,256]{1,0:T(8,128)(2,1)S(1)}, u32[]{:S(2)}, u32[]{:S(2)}) collective-permute-start(bf16[576,256]{1,0:T(8,128)(2,1)S(1)} %get-tuple-element.22), channel_id=1, source_target_pairs={{0,1},{1,0},{2,3},{3,2},{4,5},{5,4},{6,7},{7,6},{8,9},{9,8},{10,11... | collective-permute-start | bytes 884744 | tf_op jit(solution)/shard_map/ppermute | solution.py:24
  49.3 1.5 %collective-permute-done.1.cols_ref = bf16[576,256]{1,0:T(8,128)(2,1)S(1)} collective-permute-done((bf16[576,256]{1,0:T(8,128)(2,1)S(1)}, bf16[576,256]{1,0:T(8,128)(2,1)S(1)}, u32[]{:S(2)}, u32[]{:S(2)}) %collective-permute-start.1) | collective-permute-done | bytes 294944 | tf_op jit(solution)/shard_map/ppermute | solution.py:24
  50.8 2.8 %all-to-all-done = bf16[4,160,1152]{2,1,0:T(8,128)(2,1)S(1)} async-done(((bf16[4,160,1152]{2,1,0:T(8,128)(2,1)}), bf16[4,160,1152]{2,1,0:T(8,128)(2,1)S(1)}, u32[]{:S(2)}, u32[]{:S(2)}) %all-to-all-start) | async-done | bytes 1474592 | tf_op jit(solution)/shard_map/all_to_all | solution.py:209
  53.7 1.9 %collective-permute-start.2 = (bf16[640,1152]{1,0:T(8,128)(2,1)S(1)}, bf16[640,1152]{1,0:T(8,128)(2,1)S(1)}, u32[]{:S(2)}, u32[]{:S(2)}) collective-permute-start(bf16[640,1152]{1,0:T(8,128)(2,1)S(1)} %bitcast.9), channel_id=1, source_target_pairs={{0,1},{1,0},{2,3},{3,2},{4,5},{5,4},{6,7},{7,6},{8,9},{9,8},{10,11... | collective-permute-start | bytes 4423688 | tf_op jit(solution)/shard_map/ppermute | solution.py:24
  57.5 0.1 pad_maximum_fusion.1.scal_ref
  57.6 0.7 shard_map.88.half_ref
  58.3 0.5 collective-permute-done.2.weight_ref
  58.8 0.8 shard_map.89
  59.7 0.0 all-gather.2.cloned.1.call-done.text_ref
  59.7 0.0 copy-start.5
  59.7 1.7 %copy-done.5 = bf16[1024,1152]{1,0:T(8,128)(2,1)S(1)} copy-done((bf16[1024,1152]{1,0:T(8,128)(2,1)S(1)}, bf16[1024,1152]{1,0:T(8,128)(2,1)}, u32[]{:S(2)}) %copy-start.5) | copy-done | bytes 2359320
  61.4 4.2 %shard_map.91 = (bf16[256,1152]{1,0:T(8,128)(2,1)S(1)}, bf16[1024,1152]{1,0:T(8,128)(2,1)}) custom-call(f32[3]{0:T(128)S(1)} %pad_maximum_fusion.1.scal_ref, s32[3]{0:T(128)S(1)} %pad_add_fusion.refs_0_.spot_ref, bf16[256,1152]{1,0:T(8,128)(2,1)S(1)} %get-tuple-element.25.unit_ref, f32[256,1]{1,0:T(8,128)S(1)} %get-tuple-element.26.norm_ref, ...), custom_call_target="tpu_custom_call" | custom-call | flops 1811939328 | bytes 2000000 | tf_op jit(solution)/shard_map/pallas_call | solution.py:227
  65.6 0.0 reduce-scatter.2.cloned.1.call-update
  65.6 2.0 %collective-permute-start.3 = (bf16[256,1152]{1,0:T(8,128)(2,1)S(1)}, bf16[256,1152]{1,0:T(8,128)(2,1)S(1)}, u32[]{:S(2)}, u32[]{:S(2)}) collective-permute-start(bf16[256,1152]{1,0:T(8,128)(2,1)S(1)} %get-tuple-element.28.weight_ref), channel_id=1, source_target_pairs={{0,1},{1,0},{2,3},{3,2},{4,5},{5,4},{6,7},{7,6},{8,9},{9,8},{10,11... | collective-permute-start | bytes 1769480 | tf_op jit(solution)/shard_map/ppermute | solution.py:24
  67.7 0.5 shard_map.92.own_ref
  68.2 1.3 collective-permute-done.3.back_ref
  69.5 0.6 shard_map.93
  70.1 23.4 %all_to_all.20 = bf16[8,72,1152]{2,1,0:T(8,128)(2,1)S(1)} all-to-all(bf16[8,72,1152]{2,1,0:T(8,128)(2,1)S(1)} %bitcast.12), channel_id=1, replica_groups=mesh['zl'=2,'y'=8,'x'=4,'zh'=4,'c'=2] {'x','zl'}, dimensions={0} | all-to-all | bytes 2654208 | tf_op jit(solution)/shard_map/all_to_all | solution.py:245
  93.5 0.0 copy-start
  93.5 0.0 copy-start.3
  93.5 0.3 shard_map.94
  93.8 15.7 %all_to_all.21 = bf16[4,176,128]{2,1,0:T(8,128)(2,1)S(1)} all-to-all(bf16[4,176,128]{2,1,0:T(8,128)(2,1)S(1)} %shard_map.94), channel_id=1, replica_groups=mesh['zl'=2,'y'=8,'x'=4,'zh'=4,'c'=2] {'zh'}, dimensions={0} | all-to-all | bytes 360448 | tf_op jit(solution)/shard_map/all_to_all | solution.py:253
  109.6 15.5 %all_to_all.22.came_ref = bf16[8,176,128]{2,1,0:T(8,128)(2,1)S(1)} all-to-all(bf16[8,176,128]{2,1,0:T(8,128)(2,1)S(1)} %broadcast_in_dim.8), channel_id=1, replica_groups=mesh['zl'=2,'y'=8,'x'=4,'zh'=4,'c'=2] {'y'}, dimensions={0} | all-to-all | bytes 720896 | tf_op jit(solution)/shard_map/all_to_all | solution.py:255
  125.2 0.1 shard_map.95
  125.2 2.7 %collective-permute-start.4 = (f32[18,1152]{1,0:T(8,128)S(1)}, f32[18,1152]{1,0:T(8,128)S(1)}, u32[]{:S(2)}, u32[]{:S(2)}) collective-permute-start(f32[18,1152]{1,0:T(8,128)S(1)} %shard_map.95), channel_id=1, source_target_pairs={{0,256},{256,0},{1,257},{257,1},{2,258},{258,2},{3,259},{259,3},{4... | collective-permute-start | bytes 248840 | tf_op jit(solution)/shard_map/ppermute | solution.py:24
  127.9 0.0 reduce-scatter.2.cloned.1.call-done
  127.9 0.0 copy-done
  127.9 0.0 copy-done.3
  128.0 0.0 copy-start.2
  128.0 1.0 copy-done.2
  128.9 2.4 %shard_map.96 = f32[256,1152]{1,0:T(8,128)} custom-call(f32[3]{0:T(128)S(1)} %pad_maximum_fusion.1.scal_ref, s32[1,128]{1,0:T(1,128)S(1)} %bitcast.16, bf16[128,1152]{1,0:T(8,128)(2,1)S(1)} %bitcast.13, bf16[128,1152]{1,0:T(8,128)(2,1)S(1)} %copy-done, f32[128,1]{1,0:T(8,128)S(1)} %copy-done.3), custom_call_target="tpu_custom_call" | custom-call | flops 226492416 | bytes 2000000 | tf_op jit(solution)/shard_map/pallas_call | solution.py:259
  131.3 0.5 collective-permute-done.4
  131.9 0.7 pad_maximum_fusion
  (3 shorter events, 0.1 us)
Async XLA Ops:
  7.2 52.5 %all-gather.2.cloned.1.call-start = ((), (), s32[]{:S(2)}) async-start(), calls=%async_computation.5 | async-start | bytes 2654208 | tf_op jit(solution)/shard_map/all_gather | solution.py:200
  32.2 5.0 %copy-start.1 = (bf16[256,1152]{1,0:T(8,128)(2,1)S(1)}, bf16[256,1152]{1,0:T(8,128)(2,1)}, u32[]{:S(2)}) copy-start(bf16[256,1152]{1,0:T(8,128)(2,1)} %cand_ref.1) | copy-start | bytes 1769476
  32.2 5.0 %copy-start.4 = (s32[128]{0:T(128)S(1)}, s32[128]{0:T(128)}, u32[]{:S(2)}) copy-start(s32[128]{0:T(128)} %param.9) | copy-start | bytes 1540
  32.2 21.5 %all-to-all-start = ((bf16[4,160,1152]{2,1,0:T(8,128)(2,1)}), bf16[4,160,1152]{2,1,0:T(8,128)(2,1)S(1)}, u32[]{:S(2)}, u32[]{:S(2)}) async-start(bf16[4,160,1152]{2,1,0:T(8,128)(2,1)} %broadcast_in_dim.7), calls=%async_computation | async-start | bytes 2949120 | tf_op jit(solution)/shard_map/all_to_all | solution.py:209
  37.1 90.8 %reduce-scatter.2.cloned.1.call-start = ((), (), s32[]{:S(2)}) async-start(), calls=%async_computation.6 | async-start | bytes 2654208 | tf_op jit(solution)/shard_map/reduce_scatter | solution.py:235
  37.4 8.6 %collective-permute-start = (bf16[128,1152]{1,0:T(8,128)(2,1)S(1)}, bf16[128,1152]{1,0:T(8,128)(2,1)S(1)}, u32[]{:S(2)}, u32[]{:S(2)}) collective-permute-start(bf16[128,1152]{1,0:T(8,128)(2,1)S(1)} %shard_map.86.refs_1_), channel_id=1, source_target_pairs={{0,256},{256,0},{1,257},{257,1},{2,258},{258,2},{3,259},{259,3},{4... | collective-permute-start | bytes 884744 | tf_op jit(solution)/shard_map/ppermute | solution.py:24
  47.4 3.5 %collective-permute-start.1 = (bf16[576,256]{1,0:T(8,128)(2,1)S(1)}, bf16[576,256]{1,0:T(8,128)(2,1)S(1)}, u32[]{:S(2)}, u32[]{:S(2)}) collective-permute-start(bf16[576,256]{1,0:T(8,128)(2,1)S(1)} %get-tuple-element.22), channel_id=1, source_target_pairs={{0,1},{1,0},{2,3},{3,2},{4,5},{5,4},{6,7},{7,6},{8,9},{9,8},{10,11... | collective-permute-start | bytes 884744 | tf_op jit(solution)/shard_map/ppermute | solution.py:24
  53.7 5.2 %collective-permute-start.2 = (bf16[640,1152]{1,0:T(8,128)(2,1)S(1)}, bf16[640,1152]{1,0:T(8,128)(2,1)S(1)}, u32[]{:S(2)}, u32[]{:S(2)}) collective-permute-start(bf16[640,1152]{1,0:T(8,128)(2,1)S(1)} %bitcast.9), channel_id=1, source_target_pairs={{0,1},{1,0},{2,3},{3,2},{4,5},{5,4},{6,7},{7,6},{8,9},{9,8},{10,11... | collective-permute-start | bytes 4423688 | tf_op jit(solution)/shard_map/ppermute | solution.py:24
  59.7 1.7 %copy-start.5 = (bf16[1024,1152]{1,0:T(8,128)(2,1)S(1)}, bf16[1024,1152]{1,0:T(8,128)(2,1)}, u32[]{:S(2)}) copy-start(bf16[1024,1152]{1,0:T(8,128)(2,1)} %all-gather.2.cloned.1.call-done.text_ref) | copy-start | bytes 7077892
  65.6 3.9 %collective-permute-start.3 = (bf16[256,1152]{1,0:T(8,128)(2,1)S(1)}, bf16[256,1152]{1,0:T(8,128)(2,1)S(1)}, u32[]{:S(2)}, u32[]{:S(2)}) collective-permute-start(bf16[256,1152]{1,0:T(8,128)(2,1)S(1)} %get-tuple-element.28.weight_ref), channel_id=1, source_target_pairs={{0,1},{1,0},{2,3},{3,2},{4,5},{5,4},{6,7},{7,6},{8,9},{9,8},{10,11... | collective-permute-start | bytes 1769480 | tf_op jit(solution)/shard_map/ppermute | solution.py:24
  93.5 34.4 %copy-start = (bf16[128,1152]{1,0:T(8,128)(2,1)S(1)}, bf16[128,1152]{1,0:T(8,128)(2,1)}, u32[]{:S(2)}) copy-start(bf16[128,1152]{1,0:T(8,128)(2,1)} %get-tuple-element.27.unit_ref) | copy-start | bytes 884740
  93.5 34.4 %copy-start.3 = (f32[128,1]{1,0:T(8,128)S(1)}, f32[128,1]{1,0:T(8,128)}, u32[]{:S(2)}) copy-start(f32[128,1]{1,0:T(8,128)} %get-tuple-element.31.norm_ref) | copy-start | bytes 1540
  125.2 6.6 %collective-permute-start.4 = (f32[18,1152]{1,0:T(8,128)S(1)}, f32[18,1152]{1,0:T(8,128)S(1)}, u32[]{:S(2)}, u32[]{:S(2)}) collective-permute-start(f32[18,1152]{1,0:T(8,128)S(1)} %shard_map.95), channel_id=1, source_target_pairs={{0,256},{256,0},{1,257},{257,1},{2,258},{258,2},{3,259},{259,3},{4... | collective-permute-start | bytes 248840 | tf_op jit(solution)/shard_map/ppermute | solution.py:24
  128.0 1.0 copy-start.2
Sparse Core Ops, SparseCore 0:
  10.7 48.9 all-gather.1
  65.8 44.1 reduce-scatter.1

commit v11 on v10

--- a/solution.py
+++ b/solution.py
@@ -8,7 +8,7 @@
 EPS = 1e-06
 ALL = ("zl", "y", "x", "zh", "c")
 PADDED = 40
-CHUNK = 256
+CHUNK = 512
 VMEM = pl.BlockSpec(memory_space=pltpu.VMEM)
 SMEM = pl.BlockSpec(memory_space=pltpu.SMEM)
 HBM = pl.BlockSpec(memory_space=pltpu.HBM)

time: 140 us -> 140 us (level)
  no operation moved by 1% of the time
where the time goes in v11:
time: 140 us; the launch traced here: 139 us
  blocking collectives  75.2 us (54%)
  starting transfers between devices  17 us (12%)
  between operations  16.2 us (12%)
  Pallas kernels  13.1 us (9%)
  waiting for transfers between devices  11.9 us (8%)
  local copies, waits for them, and re-layouts  4.79 us (3%)
    all_to_all x1, blocking collectives, shards(): lax.all_to_all(head.reshape(2 * n_x, share, width), ('x', 'zl'), 0, 0)  23.4 us
    all_gather x1, blocking collectives, shards(): slab = lax.all_gather(part, 'zh', axis=0, tiled=True)  20.6 us
    all_to_all x1, blocking collectives, shards(): came = lax.all_to_all(folded, 'zh', 0, 0)  15.7 us
    all_to_all x1, blocking collectives, shards(): lax.all_to_all(jnp.broadcast_to(head[None], (n_y,) + head.shape), 'y', 0, 0)  15.6 us
    ppermute x5, starting transfers between devices, hop(): lax.ppermute(value, axis, [(s, (s + steps) % count) for s in range(count)])  12 us
    ppermute x5, waiting for transfers between devices, hop(): lax.ppermute(value, axis, [(s, (s + steps) % count) for s in range(count)])  9.01 us
    all_to_all x1, starting transfers between devices, shards(): lax.all_to_all(jnp.broadcast_to(slab[None], (n_x,) + slab.shape), 'x', 0, 0)  4.96 us
    pallas_call x1, Pallas kernels, shards(): call(main_kernel, [((rows, width), BF16), ((n_y * pairs, width), BF16)],...  3.82 us
  transfers between devices with their start and end apart: 8, of which 6 were waited for; matrix products, arithmetic and copies ran while one was open for 2% of the time, Pallas kernels for 5%

profile of v11, /device:TPU:2, one launch (start us, length us, event | category | flops | bytes accessed | tf_op | source)
XLA Modules:
  0.0 139.0 jit_solution(17707801525809033690)
XLA Ops:
  7.2 0.0 all-gather.2.cloned.1.call-start
  7.2 2.2 %shard_map.90 = (bf16[128,1152]{1,0:T(8,128)(2,1)}, f32[128,1]{1,0:T(8,128)}) custom-call(s32[1,128]{1,0:T(1,128)} %bitcast.14, bf16[256,1152]{1,0:T(8,128)(2,1)} %cand_hbm.1), custom_call_target="tpu_custom_call" | custom-call | flops 75497472 | bytes 2000000 | tf_op jit(solution)/shard_map/pallas_call | solution.py:195
  9.5 0.0 all-gather.2.cloned.1.call-update
  9.5 0.9 pad.4
  10.4 20.6 %all_gather.6 = bf16[160,1152]{1,0:T(8,128)(2,1)S(1)} all-gather(bf16[40,1152]{1,0:T(8,128)(2,1)S(1)} %pad.4), channel_id=1, replica_groups=mesh['zl'=2,'y'=8,'x'=4,'zh'=4,'c'=2] {'zh'}, dimensions={0}, use_global_device_ids=true | all-gather | bytes 460800 | tf_op jit(solution)/shard_map/all_gather | solution.py:203
  31.0 1.2 broadcast_in_dim.7
  32.2 0.0 copy-start.1
  32.2 0.0 copy-start.4
  32.2 5.0 %all-to-all-start = ((bf16[4,160,1152]{2,1,0:T(8,128)(2,1)}), bf16[4,160,1152]{2,1,0:T(8,128)(2,1)S(1)}, u32[]{:S(2)}, u32[]{:S(2)}) async-start(bf16[4,160,1152]{2,1,0:T(8,128)(2,1)} %broadcast_in_dim.7), calls=%async_computation | async-start | bytes 2949120 | tf_op jit(solution)/shard_map/all_to_all | solution.py:209
  37.1 0.0 reduce-scatter.2.cloned.1.call-start
  37.1 0.0 copy-done.1
  37.1 0.0 copy-done.4
  37.2 0.3 shard_map.86.refs_1_
  37.4 3.4 %collective-permute-start = (bf16[128,1152]{1,0:T(8,128)(2,1)S(1)}, bf16[128,1152]{1,0:T(8,128)(2,1)S(1)}, u32[]{:S(2)}, u32[]{:S(2)}) collective-permute-start(bf16[128,1152]{1,0:T(8,128)(2,1)S(1)} %shard_map.86.refs_1_), channel_id=1, source_target_pairs={{0,256},{256,0},{1,257},{257,1},{2,258},{258,2},{3,259},{259,3},{4... | collective-permute-start | bytes 884744 | tf_op jit(solution)/shard_map/ppermute | solution.py:24
  40.9 0.1 pad_add_fusion.refs_0_.spot_ref
  40.9 5.1 %collective-permute-done.refs_2_ = bf16[128,1152]{1,0:T(8,128)(2,1)S(1)} collective-permute-done((bf16[128,1152]{1,0:T(8,128)(2,1)S(1)}, bf16[128,1152]{1,0:T(8,128)(2,1)S(1)}, u32[]{:S(2)}, u32[]{:S(2)}) %collective-permute-start) | collective-permute-done | bytes 294944 | tf_op jit(solution)/shard_map/ppermute | solution.py:24
  46.1 1.3 shard_map.87
  47.4 1.9 %collective-permute-start.1 = (bf16[576,256]{1,0:T(8,128)(2,1)S(1)}, bf16[576,256]{1,0:T(8,128)(2,1)S(1)}, u32[]{:S(2)}, u32[]{:S(2)}) collective-permute-start(bf16[576,256]{1,0:T(8,128)(2,1)S(1)} %get-tuple-element.22), channel_id=1, source_target_pairs={{0,1},{1,0},{2,3},{3,2},{4,5},{5,4},{6,7},{7,6},{8,9},{9,8},{10,11... | collective-permute-start | bytes 884744 | tf_op jit(solution)/shard_map/ppermute | solution.py:24
  49.3 1.5 %collective-permute-done.1.cols_ref = bf16[576,256]{1,0:T(8,128)(2,1)S(1)} collective-permute-done((bf16[576,256]{1,0:T(8,128)(2,1)S(1)}, bf16[576,256]{1,0:T(8,128)(2,1)S(1)}, u32[]{:S(2)}, u32[]{:S(2)}) %collective-permute-start.1) | collective-permute-done | bytes 294944 | tf_op jit(solution)/shard_map/ppermute | solution.py:24
  50.8 2.8 %all-to-all-done = bf16[4,160,1152]{2,1,0:T(8,128)(2,1)S(1)} async-done(((bf16[4,160,1152]{2,1,0:T(8,128)(2,1)}), bf16[4,160,1152]{2,1,0:T(8,128)(2,1)S(1)}, u32[]{:S(2)}, u32[]{:S(2)}) %all-to-all-start) | async-done | bytes 1474592 | tf_op jit(solution)/shard_map/all_to_all | solution.py:209
  53.7 1.9 %collective-permute-start.2 = (bf16[640,1152]{1,0:T(8,128)(2,1)S(1)}, bf16[640,1152]{1,0:T(8,128)(2,1)S(1)}, u32[]{:S(2)}, u32[]{:S(2)}) collective-permute-start(bf16[640,1152]{1,0:T(8,128)(2,1)S(1)} %bitcast.9), channel_id=1, source_target_pairs={{0,1},{1,0},{2,3},{3,2},{4,5},{5,4},{6,7},{7,6},{8,9},{9,8},{10,11... | collective-permute-start | bytes 4423688 | tf_op jit(solution)/shard_map/ppermute | solution.py:24
  57.5 0.1 pad_maximum_fusion.1.scal_ref
  57.6 0.7 shard_map.88.half_ref
  58.3 0.5 collective-permute-done.2.weight_ref
  58.8 0.8 shard_map.89
  59.7 0.0 all-gather.2.cloned.1.call-done.text_ref
  59.7 0.0 copy-start.5
  59.7 1.7 %copy-done.5 = bf16[1024,1152]{1,0:T(8,128)(2,1)S(1)} copy-done((bf16[1024,1152]{1,0:T(8,128)(2,1)S(1)}, bf16[1024,1152]{1,0:T(8,128)(2,1)}, u32[]{:S(2)}) %copy-start.5) | copy-done | bytes 2359320
  61.4 3.8 %shard_map.91 = (bf16[256,1152]{1,0:T(8,128)(2,1)S(1)}, bf16[1024,1152]{1,0:T(8,128)(2,1)}) custom-call(f32[3]{0:T(128)S(1)} %pad_maximum_fusion.1.scal_ref, s32[3]{0:T(128)S(1)} %pad_add_fusion.refs_0_.spot_ref, bf16[256,1152]{1,0:T(8,128)(2,1)S(1)} %get-tuple-element.25.unit_ref, f32[256,1]{1,0:T(8,128)S(1)} %get-tuple-element.26.norm_ref, ...), custom_call_target="tpu_custom_call" | custom-call | flops 1811939328 | bytes 2000000 | tf_op jit(solution)/shard_map/pallas_call | solution.py:227
  65.2 0.0 reduce-scatter.2.cloned.1.call-update
  65.2 2.0 %collective-permute-start.3 = (bf16[256,1152]{1,0:T(8,128)(2,1)S(1)}, bf16[256,1152]{1,0:T(8,128)(2,1)S(1)}, u32[]{:S(2)}, u32[]{:S(2)}) collective-permute-start(bf16[256,1152]{1,0:T(8,128)(2,1)S(1)} %get-tuple-element.28.weight_ref), channel_id=1, source_target_pairs={{0,1},{1,0},{2,3},{3,2},{4,5},{5,4},{6,7},{7,6},{8,9},{9,8},{10,11... | collective-permute-start | bytes 1769480 | tf_op jit(solution)/shard_map/ppermute | solution.py:24
  67.3 0.5 shard_map.92.own_ref
  67.8 1.3 collective-permute-done.3.back_ref
  69.1 0.6 shard_map.93
  69.7 23.4 %all_to_all.20 = bf16[8,72,1152]{2,1,0:T(8,128)(2,1)S(1)} all-to-all(bf16[8,72,1152]{2,1,0:T(8,128)(2,1)S(1)} %bitcast.12), channel_id=1, replica_groups=mesh['zl'=2,'y'=8,'x'=4,'zh'=4,'c'=2] {'x','zl'}, dimensions={0} | all-to-all | bytes 2654208 | tf_op jit(solution)/shard_map/all_to_all | solution.py:245
  93.1 0.0 copy-start
  93.1 0.0 copy-start.3
  93.1 0.3 shard_map.94
  93.4 15.7 %all_to_all.21 = bf16[4,176,128]{2,1,0:T(8,128)(2,1)S(1)} all-to-all(bf16[4,176,128]{2,1,0:T(8,128)(2,1)S(1)} %shard_map.94), channel_id=1, replica_groups=mesh['zl'=2,'y'=8,'x'=4,'zh'=4,'c'=2] {'zh'}, dimensions={0} | all-to-all | bytes 360448 | tf_op jit(solution)/shard_map/all_to_all | solution.py:253
  109.2 15.6 %all_to_all.22.came_ref = bf16[8,176,128]{2,1,0:T(8,128)(2,1)S(1)} all-to-all(bf16[8,176,128]{2,1,0:T(8,128)(2,1)S(1)} %broadcast_in_dim.8), channel_id=1, replica_groups=mesh['zl'=2,'y'=8,'x'=4,'zh'=4,'c'=2] {'y'}, dimensions={0} | all-to-all | bytes 720896 | tf_op jit(solution)/shard_map/all_to_all | solution.py:255
  124.7 0.1 shard_map.95
  124.8 2.7 %collective-permute-start.4 = (f32[18,1152]{1,0:T(8,128)S(1)}, f32[18,1152]{1,0:T(8,128)S(1)}, u32[]{:S(2)}, u32[]{:S(2)}) collective-permute-start(f32[18,1152]{1,0:T(8,128)S(1)} %shard_map.95), channel_id=1, source_target_pairs={{0,256},{256,0},{1,257},{257,1},{2,258},{258,2},{3,259},{259,3},{4... | collective-permute-start | bytes 248840 | tf_op jit(solution)/shard_map/ppermute | solution.py:24
  127.5 0.0 reduce-scatter.2.cloned.1.call-done
  127.5 0.0 copy-done
  127.5 0.0 copy-done.3
  127.5 0.0 copy-start.2
  127.5 1.0 copy-done.2
  128.5 2.4 %shard_map.96 = f32[256,1152]{1,0:T(8,128)} custom-call(f32[3]{0:T(128)S(1)} %pad_maximum_fusion.1.scal_ref, s32[1,128]{1,0:T(1,128)S(1)} %bitcast.16, bf16[128,1152]{1,0:T(8,128)(2,1)S(1)} %bitcast.13, bf16[128,1152]{1,0:T(8,128)(2,1)S(1)} %copy-done, f32[128,1]{1,0:T(8,128)S(1)} %copy-done.3), custom_call_target="tpu_custom_call" | custom-call | flops 226492416 | bytes 2000000 | tf_op jit(solution)/shard_map/pallas_call | solution.py:259
  130.9 0.5 collective-permute-done.4
  131.5 0.7 pad_maximum_fusion
  (3 shorter events, 0.1 us)
Async XLA Ops:
  7.2 52.5 %all-gather.2.cloned.1.call-start = ((), (), s32[]{:S(2)}) async-start(), calls=%async_computation.5 | async-start | bytes 2654208 | tf_op jit(solution)/shard_map/all_gather | solution.py:200
  32.2 5.0 %copy-start.1 = (bf16[256,1152]{1,0:T(8,128)(2,1)S(1)}, bf16[256,1152]{1,0:T(8,128)(2,1)}, u32[]{:S(2)}) copy-start(bf16[256,1152]{1,0:T(8,128)(2,1)} %cand_ref.1) | copy-start | bytes 1769476
  32.2 5.0 %copy-start.4 = (s32[128]{0:T(128)S(1)}, s32[128]{0:T(128)}, u32[]{:S(2)}) copy-start(s32[128]{0:T(128)} %param.9) | copy-start | bytes 1540
  32.2 21.5 %all-to-all-start = ((bf16[4,160,1152]{2,1,0:T(8,128)(2,1)}), bf16[4,160,1152]{2,1,0:T(8,128)(2,1)S(1)}, u32[]{:S(2)}, u32[]{:S(2)}) async-start(bf16[4,160,1152]{2,1,0:T(8,128)(2,1)} %broadcast_in_dim.7), calls=%async_computation | async-start | bytes 2949120 | tf_op jit(solution)/shard_map/all_to_all | solution.py:209
  37.1 90.4 %reduce-scatter.2.cloned.1.call-start = ((), (), s32[]{:S(2)}) async-start(), calls=%async_computation.6 | async-start | bytes 2654208 | tf_op jit(solution)/shard_map/reduce_scatter | solution.py:235
  37.4 8.6 %collective-permute-start = (bf16[128,1152]{1,0:T(8,128)(2,1)S(1)}, bf16[128,1152]{1,0:T(8,128)(2,1)S(1)}, u32[]{:S(2)}, u32[]{:S(2)}) collective-permute-start(bf16[128,1152]{1,0:T(8,128)(2,1)S(1)} %shard_map.86.refs_1_), channel_id=1, source_target_pairs={{0,256},{256,0},{1,257},{257,1},{2,258},{258,2},{3,259},{259,3},{4... | collective-permute-start | bytes 884744 | tf_op jit(solution)/shard_map/ppermute | solution.py:24
  47.4 3.5 %collective-permute-start.1 = (bf16[576,256]{1,0:T(8,128)(2,1)S(1)}, bf16[576,256]{1,0:T(8,128)(2,1)S(1)}, u32[]{:S(2)}, u32[]{:S(2)}) collective-permute-start(bf16[576,256]{1,0:T(8,128)(2,1)S(1)} %get-tuple-element.22), channel_id=1, source_target_pairs={{0,1},{1,0},{2,3},{3,2},{4,5},{5,4},{6,7},{7,6},{8,9},{9,8},{10,11... | collective-permute-start | bytes 884744 | tf_op jit(solution)/shard_map/ppermute | solution.py:24
  53.7 5.2 %collective-permute-start.2 = (bf16[640,1152]{1,0:T(8,128)(2,1)S(1)}, bf16[640,1152]{1,0:T(8,128)(2,1)S(1)}, u32[]{:S(2)}, u32[]{:S(2)}) collective-permute-start(bf16[640,1152]{1,0:T(8,128)(2,1)S(1)} %bitcast.9), channel_id=1, source_target_pairs={{0,1},{1,0},{2,3},{3,2},{4,5},{5,4},{6,7},{7,6},{8,9},{9,8},{10,11... | collective-permute-start | bytes 4423688 | tf_op jit(solution)/shard_map/ppermute | solution.py:24
  59.7 1.7 %copy-start.5 = (bf16[1024,1152]{1,0:T(8,128)(2,1)S(1)}, bf16[1024,1152]{1,0:T(8,128)(2,1)}, u32[]{:S(2)}) copy-start(bf16[1024,1152]{1,0:T(8,128)(2,1)} %all-gather.2.cloned.1.call-done.text_ref) | copy-start | bytes 7077892
  65.2 3.9 %collective-permute-start.3 = (bf16[256,1152]{1,0:T(8,128)(2,1)S(1)}, bf16[256,1152]{1,0:T(8,128)(2,1)S(1)}, u32[]{:S(2)}, u32[]{:S(2)}) collective-permute-start(bf16[256,1152]{1,0:T(8,128)(2,1)S(1)} %get-tuple-element.28.weight_ref), channel_id=1, source_target_pairs={{0,1},{1,0},{2,3},{3,2},{4,5},{5,4},{6,7},{7,6},{8,9},{9,8},{10,11... | collective-permute-start | bytes 1769480 | tf_op jit(solution)/shard_map/ppermute | solution.py:24
  93.1 34.4 %copy-start = (bf16[128,1152]{1,0:T(8,128)(2,1)S(1)}, bf16[128,1152]{1,0:T(8,128)(2,1)}, u32[]{:S(2)}) copy-start(bf16[128,1152]{1,0:T(8,128)(2,1)} %get-tuple-element.27.unit_ref) | copy-start | bytes 884740
  93.1 34.4 %copy-start.3 = (f32[128,1]{1,0:T(8,128)S(1)}, f32[128,1]{1,0:T(8,128)}, u32[]{:S(2)}) copy-start(f32[128,1]{1,0:T(8,128)} %get-tuple-element.31.norm_ref) | copy-start | bytes 1540
  124.8 6.6 %collective-permute-start.4 = (f32[18,1152]{1,0:T(8,128)S(1)}, f32[18,1152]{1,0:T(8,128)S(1)}, u32[]{:S(2)}, u32[]{:S(2)}) collective-permute-start(f32[18,1152]{1,0:T(8,128)S(1)} %shard_map.95), channel_id=1, source_target_pairs={{0,256},{256,0},{1,257},{257,1},{2,258},{258,2},{3,259},{259,3},{4... | collective-permute-start | bytes 248840 | tf_op jit(solution)/shard_map/ppermute | solution.py:24
  127.5 1.0 copy-start.2
Sparse Core Ops, SparseCore 0:
  10.7 48.9 all-gather.1
  65.3 44.2 reduce-scatter.1

commit v12 on v11

--- a/solution.py
+++ b/solution.py
@@ -143,14 +143,15 @@
     out_ref[...] = flat_ref[...].astype(BF16)
 
 
-def unfold_kernel(came_ref, out_ref, sum_ref):
-    total = came_ref[0].astype(F32)
-    for k in range(1, came_ref.shape[0]):
-        total += came_ref[k].astype(F32)
-    sum_ref[...] = total
-    size = out_ref.shape[0]
-    for t in range(out_ref.shape[1] // LANES):
-        out_ref[:, t * LANES:(t + 1) * LANES] = sum_ref[t * size:(t + 1) * size, :]
+def unfold_kernel(spot_ref, mine_ref, there_ref, out_ref, pair_ref):
+    first = spot_ref[0] == 0
+    mine, there = mine_ref[...], there_ref[...]
+    pair_ref[0] = jnp.where(first, mine, there)
+    pair_ref[1] = jnp.where(first, there, mine)
+    size = out_ref.shape[0] // 2
+    for half in range(2):
+        for t in range(out_ref.shape[1] // LANES):
+            out_ref[half * size:(half + 1) * size, t * LANES:(t + 1) * LANES] = pair_ref[half, t * size:(t + 1) * size, :]
 
 
 def place_kernel(scal_ref, chosen_ref, back_ref, unit_ref, norm_ref, out_ref):
@@ -253,14 +254,15 @@
     came = lax.all_to_all(folded, "zh", 0, 0)
     head = jnp.sum(came.astype(F32), axis=0).astype(BF16)
     came = lax.all_to_all(jnp.broadcast_to(head[None], (n_y,) + head.shape), "y", 0, 0)
-    (head,) = call(unfold_kernel, [((piece, width), F32)], [VMEM], (VMEM,), [pltpu.VMEM((strips, LANES), F32)])(came)
-
+    head = jnp.sum(came.astype(F32), axis=0)
     there = hop(head, "zl", 1)
     (text_grad,) = call(
         place_kernel, [((cands, width), F32)], [SMEM] + [VMEM] * 4, (VMEM,), cost=6 * cands * pairs * width,
     )(scalars, chosen, text_back, text_unit, txt_norm)
     there, text_grad = lax.optimization_barrier((there, text_grad))
-    head_grad = jnp.concatenate([jnp.where(my_zl == 0, head, there), jnp.where(my_zl == 0, there, head)], axis=0)
+    (head_grad,) = call(
+        unfold_kernel, [((own_rows, width), F32)], [SMEM, VMEM, VMEM], (VMEM,), [pltpu.VMEM((2, strips, LANES), F32)],
+    )(spot, head, there)
     return head_grad, text_grad
 
 

time: 140 us -> 140 us (level)
  no operation moved by 1% of the time
where the time goes in v12:
time: 140 us; the launch traced here: 139 us
  blocking collectives  75.3 us (54%)
  starting transfers between devices  17 us (12%)
  between operations  16.1 us (12%)
  Pallas kernels  14.2 us (10%)
  waiting for transfers between devices  11.7 us (8%)
  local copies, waits for them, and re-layouts  4.8 us (3%)
    all_to_all x1, blocking collectives, shards(): lax.all_to_all(head.reshape(2 * n_x, share, width), ('x', 'zl'), 0, 0)  23.4 us
    all_gather x1, blocking collectives, shards(): slab = lax.all_gather(part, 'zh', axis=0, tiled=True)  20.6 us
    all_to_all x1, blocking collectives, shards(): came = lax.all_to_all(folded, 'zh', 0, 0)  15.7 us
    all_to_all x1, blocking collectives, shards(): lax.all_to_all(jnp.broadcast_to(head[None], (n_y,) + head.shape), 'y', 0, 0)  15.6 us
    ppermute x5, starting transfers between devices, hop(): lax.ppermute(value, axis, [(s, (s + steps) % count) for s in range(count)])  12 us
    ppermute x5, waiting for transfers between devices, hop(): lax.ppermute(value, axis, [(s, (s + steps) % count) for s in range(count)])  8.8 us
    all_to_all x1, starting transfers between devices, shards(): lax.all_to_all(jnp.broadcast_to(slab[None], (n_x,) + slab.shape), 'x', 0, 0)  4.96 us
    pallas_call x1, Pallas kernels, shards(): call(main_kernel, [((rows, width), BF16), ((n_y * pairs, width), BF16)],...  3.83 us
  transfers between devices with their start and end apart: 8, of which 6 were waited for; matrix products, arithmetic and copies ran while one was open for 2% of the time, Pallas kernels for 5%

profile of v12, /device:TPU:2, one launch (start us, length us, event | category | flops | bytes accessed | tf_op | source)
XLA Modules:
  0.0 139.4 jit_solution(16490706192803425753)
XLA Ops:
  7.2 0.0 all-gather.2.cloned.1.call-start
  7.2 2.2 %shard_map.90 = (bf16[128,1152]{1,0:T(8,128)(2,1)}, f32[128,1]{1,0:T(8,128)}) custom-call(s32[1,128]{1,0:T(1,128)} %bitcast.14, bf16[256,1152]{1,0:T(8,128)(2,1)} %cand_hbm.1), custom_call_target="tpu_custom_call" | custom-call | flops 75497472 | bytes 2000000 | tf_op jit(solution)/shard_map/pallas_call | solution.py:196
  9.5 0.0 all-gather.2.cloned.1.call-update
  9.5 0.9 pad.4
  10.4 20.6 %all_gather.6 = bf16[160,1152]{1,0:T(8,128)(2,1)S(1)} all-gather(bf16[40,1152]{1,0:T(8,128)(2,1)S(1)} %pad.4), channel_id=1, replica_groups=mesh['zl'=2,'y'=8,'x'=4,'zh'=4,'c'=2] {'zh'}, dimensions={0}, use_global_device_ids=true | all-gather | bytes 460800 | tf_op jit(solution)/shard_map/all_gather | solution.py:204
  31.0 1.2 broadcast_in_dim.7
  32.2 0.0 copy-start.1
  32.2 0.0 copy-start.4
  32.2 5.0 %all-to-all-start = ((bf16[4,160,1152]{2,1,0:T(8,128)(2,1)}), bf16[4,160,1152]{2,1,0:T(8,128)(2,1)S(1)}, u32[]{:S(2)}, u32[]{:S(2)}) async-start(bf16[4,160,1152]{2,1,0:T(8,128)(2,1)} %broadcast_in_dim.7), calls=%async_computation | async-start | bytes 2949120 | tf_op jit(solution)/shard_map/all_to_all | solution.py:210
  37.2 0.0 reduce-scatter.2.cloned.1.call-start
  37.2 0.0 copy-done.1
  37.2 0.0 copy-done.4
  37.2 0.3 shard_map.86.refs_1_
  37.4 3.4 %collective-permute-start = (bf16[128,1152]{1,0:T(8,128)(2,1)S(1)}, bf16[128,1152]{1,0:T(8,128)(2,1)S(1)}, u32[]{:S(2)}, u32[]{:S(2)}) collective-permute-start(bf16[128,1152]{1,0:T(8,128)(2,1)S(1)} %shard_map.86.refs_1_), channel_id=1, source_target_pairs={{0,256},{256,0},{1,257},{257,1},{2,258},{258,2},{3,259},{259,3},{4... | collective-permute-start | bytes 884744 | tf_op jit(solution)/shard_map/ppermute | solution.py:24
  40.9 0.1 pad_add_fusion.refs_0_.spot_ref
  40.9 5.1 %collective-permute-done.refs_2_ = bf16[128,1152]{1,0:T(8,128)(2,1)S(1)} collective-permute-done((bf16[128,1152]{1,0:T(8,128)(2,1)S(1)}, bf16[128,1152]{1,0:T(8,128)(2,1)S(1)}, u32[]{:S(2)}, u32[]{:S(2)}) %collective-permute-start) | collective-permute-done | bytes 294944 | tf_op jit(solution)/shard_map/ppermute | solution.py:24
  46.1 1.3 shard_map.87
  47.4 1.9 %collective-permute-start.1 = (bf16[576,256]{1,0:T(8,128)(2,1)S(1)}, bf16[576,256]{1,0:T(8,128)(2,1)S(1)}, u32[]{:S(2)}, u32[]{:S(2)}) collective-permute-start(bf16[576,256]{1,0:T(8,128)(2,1)S(1)} %get-tuple-element.22), channel_id=1, source_target_pairs={{0,1},{1,0},{2,3},{3,2},{4,5},{5,4},{6,7},{7,6},{8,9},{9,8},{10,11... | collective-permute-start | bytes 884744 | tf_op jit(solution)/shard_map/ppermute | solution.py:24
  49.3 1.5 %collective-permute-done.1.cols_ref = bf16[576,256]{1,0:T(8,128)(2,1)S(1)} collective-permute-done((bf16[576,256]{1,0:T(8,128)(2,1)S(1)}, bf16[576,256]{1,0:T(8,128)(2,1)S(1)}, u32[]{:S(2)}, u32[]{:S(2)}) %collective-permute-start.1) | collective-permute-done | bytes 294944 | tf_op jit(solution)/shard_map/ppermute | solution.py:24
  50.8 2.8 %all-to-all-done = bf16[4,160,1152]{2,1,0:T(8,128)(2,1)S(1)} async-done(((bf16[4,160,1152]{2,1,0:T(8,128)(2,1)}), bf16[4,160,1152]{2,1,0:T(8,128)(2,1)S(1)}, u32[]{:S(2)}, u32[]{:S(2)}) %all-to-all-start) | async-done | bytes 1474592 | tf_op jit(solution)/shard_map/all_to_all | solution.py:210
  53.7 1.9 %collective-permute-start.2 = (bf16[640,1152]{1,0:T(8,128)(2,1)S(1)}, bf16[640,1152]{1,0:T(8,128)(2,1)S(1)}, u32[]{:S(2)}, u32[]{:S(2)}) collective-permute-start(bf16[640,1152]{1,0:T(8,128)(2,1)S(1)} %bitcast.9), channel_id=1, source_target_pairs={{0,1},{1,0},{2,3},{3,2},{4,5},{5,4},{6,7},{7,6},{8,9},{9,8},{10,11... | collective-permute-start | bytes 4423688 | tf_op jit(solution)/shard_map/ppermute | solution.py:24
  57.5 0.1 pad_maximum_fusion.scal_ref
  57.6 0.7 shard_map.88.half_ref
  58.3 0.6 collective-permute-done.2.weight_ref
  58.8 0.8 shard_map.89
  59.7 0.0 all-gather.2.cloned.1.call-done.text_ref
  59.7 0.0 copy-start.5
  59.7 1.7 %copy-done.5 = bf16[1024,1152]{1,0:T(8,128)(2,1)S(1)} copy-done((bf16[1024,1152]{1,0:T(8,128)(2,1)S(1)}, bf16[1024,1152]{1,0:T(8,128)(2,1)}, u32[]{:S(2)}) %copy-start.5) | copy-done | bytes 2359320
  61.4 3.8 %shard_map.91 = (bf16[256,1152]{1,0:T(8,128)(2,1)S(1)}, bf16[1024,1152]{1,0:T(8,128)(2,1)}) custom-call(f32[3]{0:T(128)S(1)} %pad_maximum_fusion.scal_ref, s32[3]{0:T(128)S(1)} %pad_add_fusion.refs_0_.spot_ref, bf16[256,1152]{1,0:T(8,128)(2,1)S(1)} %get-tuple-element.25.unit_ref, f32[256,1]{1,0:T(8,128)S(1)} %get-tuple-element.26.norm_ref, ...), custom_call_target="tpu_custom_call" | custom-call | flops 1811939328 | bytes 2000000 | tf_op jit(solution)/shard_map/pallas_call | solution.py:228
  65.2 0.0 reduce-scatter.2.cloned.1.call-update
  65.2 2.1 %collective-permute-start.3 = (bf16[256,1152]{1,0:T(8,128)(2,1)S(1)}, bf16[256,1152]{1,0:T(8,128)(2,1)S(1)}, u32[]{:S(2)}, u32[]{:S(2)}) collective-permute-start(bf16[256,1152]{1,0:T(8,128)(2,1)S(1)} %get-tuple-element.28.weight_ref), channel_id=1, source_target_pairs={{0,1},{1,0},{2,3},{3,2},{4,5},{5,4},{6,7},{7,6},{8,9},{9,8},{10,11... | collective-permute-start | bytes 1769480 | tf_op jit(solution)/shard_map/ppermute | solution.py:24
  67.3 0.5 shard_map.92.own_ref
  67.8 1.3 collective-permute-done.3.back_ref
  69.1 0.6 shard_map.93
  69.7 23.4 %all_to_all.20 = bf16[8,72,1152]{2,1,0:T(8,128)(2,1)S(1)} all-to-all(bf16[8,72,1152]{2,1,0:T(8,128)(2,1)S(1)} %bitcast.12), channel_id=1, replica_groups=mesh['zl'=2,'y'=8,'x'=4,'zh'=4,'c'=2] {'x','zl'}, dimensions={0} | all-to-all | bytes 2654208 | tf_op jit(solution)/shard_map/all_to_all | solution.py:246
  93.1 0.0 copy-start
  93.1 0.0 copy-start.3
  93.1 0.3 shard_map.94
  93.4 15.7 %all_to_all.21 = bf16[4,176,128]{2,1,0:T(8,128)(2,1)S(1)} all-to-all(bf16[4,176,128]{2,1,0:T(8,128)(2,1)S(1)} %shard_map.94), channel_id=1, replica_groups=mesh['zl'=2,'y'=8,'x'=4,'zh'=4,'c'=2] {'zh'}, dimensions={0} | all-to-all | bytes 360448 | tf_op jit(solution)/shard_map/all_to_all | solution.py:254
  109.2 15.6 %all_to_all.22 = bf16[8,176,128]{2,1,0:T(8,128)(2,1)S(1)} all-to-all(bf16[8,176,128]{2,1,0:T(8,128)(2,1)S(1)} %broadcast_in_dim.8), channel_id=1, replica_groups=mesh['zl'=2,'y'=8,'x'=4,'zh'=4,'c'=2] {'y'}, dimensions={0} | all-to-all | bytes 720896 | tf_op jit(solution)/shard_map/all_to_all | solution.py:256
  124.8 0.1 convert_reduce_fusion.mine_ref
  124.9 2.7 %collective-permute-start.4 = (f32[176,128]{1,0:T(8,128)S(1)}, f32[176,128]{1,0:T(8,128)S(1)}, u32[]{:S(2)}, u32[]{:S(2)}) collective-permute-start(f32[176,128]{1,0:T(8,128)S(1)} %convert_reduce_fusion.mine_ref), channel_id=1, source_target_pairs={{0,256},{256,0},{1,257},{257,1},{2,258},{258,2},{3,259},{259,3},{4... | collective-permute-start | bytes 270344 | tf_op jit(solution)/shard_map/ppermute | solution.py:24
  127.5 0.0 reduce-scatter.2.cloned.1.call-done
  127.6 0.0 copy-done
  127.6 0.0 copy-done.3
  127.6 0.0 copy-start.2
  127.6 1.0 copy-done.2
  128.5 2.4 %shard_map.95 = f32[256,1152]{1,0:T(8,128)} custom-call(f32[3]{0:T(128)S(1)} %pad_maximum_fusion.scal_ref, s32[1,128]{1,0:T(1,128)S(1)} %bitcast.16, bf16[128,1152]{1,0:T(8,128)(2,1)S(1)} %bitcast.13, bf16[128,1152]{1,0:T(8,128)(2,1)S(1)} %copy-done, f32[128,1]{1,0:T(8,128)S(1)} %copy-done.3), custom_call_target="tpu_custom_call" | custom-call | flops 226492416 | bytes 2000000 | tf_op jit(solution)/shard_map/pallas_call | solution.py:259
  131.0 0.3 collective-permute-done.4.there_ref
  131.3 1.2 shard_map.96
  (2 shorter events, 0.1 us)
Async XLA Ops:
  7.2 52.5 %all-gather.2.cloned.1.call-start = ((), (), s32[]{:S(2)}) async-start(), calls=%async_computation.5 | async-start | bytes 2654208 | tf_op jit(solution)/shard_map/all_gather | solution.py:201
  32.2 5.0 %copy-start.1 = (bf16[256,1152]{1,0:T(8,128)(2,1)S(1)}, bf16[256,1152]{1,0:T(8,128)(2,1)}, u32[]{:S(2)}) copy-start(bf16[256,1152]{1,0:T(8,128)(2,1)} %cand_ref.1) | copy-start | bytes 1769476
  32.2 5.0 %copy-start.4 = (s32[128]{0:T(128)S(1)}, s32[128]{0:T(128)}, u32[]{:S(2)}) copy-start(s32[128]{0:T(128)} %param.9) | copy-start | bytes 1540
  32.2 21.5 %all-to-all-start = ((bf16[4,160,1152]{2,1,0:T(8,128)(2,1)}), bf16[4,160,1152]{2,1,0:T(8,128)(2,1)S(1)}, u32[]{:S(2)}, u32[]{:S(2)}) async-start(bf16[4,160,1152]{2,1,0:T(8,128)(2,1)} %broadcast_in_dim.7), calls=%async_computation | async-start | bytes 2949120 | tf_op jit(solution)/shard_map/all_to_all | solution.py:210
  37.2 90.4 %reduce-scatter.2.cloned.1.call-start = ((), (), s32[]{:S(2)}) async-start(), calls=%async_computation.6 | async-start | bytes 2654208 | tf_op jit(solution)/shard_map/reduce_scatter | solution.py:236
  37.4 8.6 %collective-permute-start = (bf16[128,1152]{1,0:T(8,128)(2,1)S(1)}, bf16[128,1152]{1,0:T(8,128)(2,1)S(1)}, u32[]{:S(2)}, u32[]{:S(2)}) collective-permute-start(bf16[128,1152]{1,0:T(8,128)(2,1)S(1)} %shard_map.86.refs_1_), channel_id=1, source_target_pairs={{0,256},{256,0},{1,257},{257,1},{2,258},{258,2},{3,259},{259,3},{4... | collective-permute-start | bytes 884744 | tf_op jit(solution)/shard_map/ppermute | solution.py:24
  47.4 3.5 %collective-permute-start.1 = (bf16[576,256]{1,0:T(8,128)(2,1)S(1)}, bf16[576,256]{1,0:T(8,128)(2,1)S(1)}, u32[]{:S(2)}, u32[]{:S(2)}) collective-permute-start(bf16[576,256]{1,0:T(8,128)(2,1)S(1)} %get-tuple-element.22), channel_id=1, source_target_pairs={{0,1},{1,0},{2,3},{3,2},{4,5},{5,4},{6,7},{7,6},{8,9},{9,8},{10,11... | collective-permute-start | bytes 884744 | tf_op jit(solution)/shard_map/ppermute | solution.py:24
  53.7 5.2 %collective-permute-start.2 = (bf16[640,1152]{1,0:T(8,128)(2,1)S(1)}, bf16[640,1152]{1,0:T(8,128)(2,1)S(1)}, u32[]{:S(2)}, u32[]{:S(2)}) collective-permute-start(bf16[640,1152]{1,0:T(8,128)(2,1)S(1)} %bitcast.9), channel_id=1, source_target_pairs={{0,1},{1,0},{2,3},{3,2},{4,5},{5,4},{6,7},{7,6},{8,9},{9,8},{10,11... | collective-permute-start | bytes 4423688 | tf_op jit(solution)/shard_map/ppermute | solution.py:24
  59.7 1.7 %copy-start.5 = (bf16[1024,1152]{1,0:T(8,128)(2,1)S(1)}, bf16[1024,1152]{1,0:T(8,128)(2,1)}, u32[]{:S(2)}) copy-start(bf16[1024,1152]{1,0:T(8,128)(2,1)} %all-gather.2.cloned.1.call-done.text_ref) | copy-start | bytes 7077892
  65.2 3.9 %collective-permute-start.3 = (bf16[256,1152]{1,0:T(8,128)(2,1)S(1)}, bf16[256,1152]{1,0:T(8,128)(2,1)S(1)}, u32[]{:S(2)}, u32[]{:S(2)}) collective-permute-start(bf16[256,1152]{1,0:T(8,128)(2,1)S(1)} %get-tuple-element.28.weight_ref), channel_id=1, source_target_pairs={{0,1},{1,0},{2,3},{3,2},{4,5},{5,4},{6,7},{7,6},{8,9},{9,8},{10,11... | collective-permute-start | bytes 1769480 | tf_op jit(solution)/shard_map/ppermute | solution.py:24
  93.1 34.5 %copy-start = (bf16[128,1152]{1,0:T(8,128)(2,1)S(1)}, bf16[128,1152]{1,0:T(8,128)(2,1)}, u32[]{:S(2)}) copy-start(bf16[128,1152]{1,0:T(8,128)(2,1)} %get-tuple-element.27.unit_ref) | copy-start | bytes 884740
  93.1 34.5 %copy-start.3 = (f32[128,1]{1,0:T(8,128)S(1)}, f32[128,1]{1,0:T(8,128)}, u32[]{:S(2)}) copy-start(f32[128,1]{1,0:T(8,128)} %get-tuple-element.31.norm_ref) | copy-start | bytes 1540
  124.9 6.4 %collective-permute-start.4 = (f32[176,128]{1,0:T(8,128)S(1)}, f32[176,128]{1,0:T(8,128)S(1)}, u32[]{:S(2)}, u32[]{:S(2)}) collective-permute-start(f32[176,128]{1,0:T(8,128)S(1)} %convert_reduce_fusion.mine_ref), channel_id=1, source_target_pairs={{0,256},{256,0},{1,257},{257,1},{2,258},{258,2},{3,259},{259,3},{4... | collective-permute-start | bytes 270344 | tf_op jit(solution)/shard_map/ppermute | solution.py:24
  127.6 1.0 copy-start.2
Sparse Core Ops, SparseCore 0:
  10.7 48.9 all-gather.1
  65.3 44.2 reduce-scatter.1
